TPU v7x, 512 devices: a whole 4x8x8 slice. The times are simulated.
512 devices in a mesh: expert: 8 (over y), ffn: 32 (over x, z), dp: 2 (over core).
Axes of the slice: x: 4, y: 8, z: 8, core: 2. Of those that a mesh axis runs over, the one named last changes fastest.
Arguments:
- tokens: bfloat16 [2048, 2048], P(('expert', 'ffn'), 'dp'), may hold values from -6 to 6
- out_grad: bfloat16 [2048, 2048], P(('expert', 'ffn'), 'dp'), may hold values from -6 to 6
- expert_ids: int32 [2048, 2], P(('expert', 'ffn')), may hold values from 0 to 7, all different within a row; in each aligned block of 8 rows (0 to 7, 8 to 15, ...) at most 3 rows name the same one
- gate_probs: float32 [2048, 2], P(('expert', 'ffn')), may hold values from 0.1 to 1
- w_gate: bfloat16 [8, 2048, 8192], P('expert', 'dp', 'ffn'), may hold values from -0.125 to 0.125
- w_up: bfloat16 [8, 2048, 8192], P('expert', 'dp', 'ffn'), may hold values from -0.125 to 0.125
- w_down: bfloat16 [8, 8192, 2048], P('expert', 'ffn', 'dp'), may hold values from -0.0625 to 0.0625
Outputs:
- grad_tokens: bfloat16 [2048, 2048], P(('expert', 'ffn'), 'dp')
- grad_gate: bfloat16 [8, 2048, 8192], P('expert', 'dp', 'ffn')
- grad_up: bfloat16 [8, 2048, 8192], P('expert', 'dp', 'ffn')
- grad_down: bfloat16 [8, 8192, 2048], P('expert', 'ffn', 'dp')
- grad_probs: bfloat16 [2048, 2], P(('expert', 'ffn'))
Inputs may be any that keep to these rules, and one draw needn't show every extreme that they name: `expert_ids`: within each aligned block of 8 tokens (the tokens of one index of expert and ffn), every expert is named by at most 3 pairs, a bound that some block reaches; the two ids of a token differ.
All inputs are finite; a program needn't handle non-finite values.
Results may differ from a plain program's by a relative error of at most 0.019.
Values may be sent and summed in bfloat16 or wider, within the bound.
No kernel may reach another device: no remote copies, remote signals or barrier semaphores. Data moves between devices by JAX's collectives and lax.ppermute only.
A program may use at most 64 MiB of HBM per device.

v0:
```python
import jax
import jax.numpy as jnp
from jax import lax
from jax.sharding import PartitionSpec as P


def contract(left, right, left_dim, right_dim):
    return lax.dot_general(
        left, right, (((left_dim,), (right_dim,)), ((), ())), preferred_element_type=jnp.float32
    )


def local_terms(gate_pre, up_pre, backward, weight):
    sigmoid_gate = jax.nn.sigmoid(gate_pre)
    silu_gate = gate_pre * sigmoid_gate
    hidden = (silu_gate * up_pre).astype(jnp.bfloat16)
    score = jnp.sum(backward * hidden.astype(jnp.float32), axis=1)
    d_hidden = weight[:, None] * backward
    grad_gate_pre = (
        d_hidden * up_pre * sigmoid_gate * (1.0 + gate_pre * (1.0 - sigmoid_gate))
    ).astype(jnp.bfloat16)
    grad_up_pre = (d_hidden * silu_gate).astype(jnp.bfloat16)
    return (hidden, score, grad_gate_pre, grad_up_pre)


def per_device(tokens, out_grad, expert_ids, gate_probs, w_gate, w_up, w_down):
    experts = lax.axis_size("expert")
    shards = lax.axis_size("ffn")
    tok_rows = tokens.shape[0]
    width = tokens.shape[1]
    capacity = max(3 * tok_rows // 8, 2 * tok_rows // experts)
    slot_total = experts * capacity
    flat_ids = expert_ids.reshape(-1)
    onehot = (flat_ids[:, None] == jnp.arange(experts, dtype=jnp.int32)[None, :]).astype(jnp.int32)
    ranks = jnp.sum((jnp.cumsum(onehot, axis=0) - onehot) * onehot, axis=1)
    position = flat_ids * capacity + ranks
    placing = (position[None, :] == jnp.arange(slot_total, dtype=jnp.int32)[:, None]).astype(
        jnp.bfloat16
    )
    placing_tok = jnp.sum(placing.reshape(slot_total, tok_rows, 2), axis=2)
    send_x = jnp.dot(placing_tok, tokens, preferred_element_type=jnp.float32).astype(jnp.bfloat16)
    send_dy = jnp.dot(placing_tok, out_grad, preferred_element_type=jnp.float32).astype(
        jnp.bfloat16
    )
    probs = gate_probs.astype(jnp.bfloat16).reshape(-1)
    send_p = jnp.dot(placing, probs, preferred_element_type=jnp.float32).astype(jnp.bfloat16)
    send_x = send_x.reshape(experts, capacity, width)
    send_dy = send_dy.reshape(experts, capacity, width)
    send_p = send_p.reshape(experts, capacity)
    recv_x, recv_dy, recv_p = (
        lax.all_to_all(send_x, "expert", split_axis=0, concat_axis=0, tiled=True),
        lax.all_to_all(send_dy, "expert", split_axis=0, concat_axis=0, tiled=True),
        lax.all_to_all(send_p, "expert", split_axis=0, concat_axis=0, tiled=True),
    )
    rows_x, rows_dy, rows_p = (
        lax.all_gather(recv_x, "ffn", axis=0, tiled=True),
        lax.all_gather(recv_dy, "ffn", axis=0, tiled=True),
        lax.all_gather(recv_p, "ffn", axis=0, tiled=True),
    )
    rows_x = rows_x.reshape(-1, width)
    rows_dy = rows_dy.reshape(-1, width)
    weight = rows_p.reshape(-1).astype(jnp.float32)
    gate_w = w_gate[0]
    up_w = w_up[0]
    down_w = w_down[0]
    gate_part = jnp.dot(rows_x, gate_w, preferred_element_type=jnp.float32)
    up_part = jnp.dot(rows_x, up_w, preferred_element_type=jnp.float32)
    back_part = contract(rows_dy, down_w, 1, 1)
    gate_pre, up_pre, backward = lax.psum((gate_part, up_part, back_part), "dp")
    hidden, score, grad_gate_pre, grad_up_pre = local_terms(gate_pre, up_pre, backward, weight)
    scaled = (weight[:, None] * rows_dy.astype(jnp.float32)).astype(jnp.bfloat16)
    grad_gate = contract(rows_x, grad_gate_pre, 0, 0).astype(jnp.bfloat16)[None]
    grad_up = contract(rows_x, grad_up_pre, 0, 0).astype(jnp.bfloat16)[None]
    grad_down = contract(hidden, scaled, 0, 0).astype(jnp.bfloat16)[None]
    input_part = contract(grad_gate_pre, gate_w, 1, 1) + contract(grad_up_pre, up_w, 1, 1)
    summed, scores = (
        lax.psum_scatter(
            input_part.reshape(shards * experts, capacity, width),
            "ffn",
            scatter_dimension=0,
            tiled=True,
        ),
        lax.psum_scatter(
            score.reshape(shards * experts, capacity), "ffn", scatter_dimension=0, tiled=True
        ),
    )
    back_x, back_s = (
        lax.all_to_all(
            summed.astype(jnp.bfloat16), "expert", split_axis=0, concat_axis=0, tiled=True
        ),
        lax.all_to_all(
            scores.astype(jnp.bfloat16), "expert", split_axis=0, concat_axis=0, tiled=True
        ),
    )
    grad_tokens = jnp.dot(
        placing_tok.T, back_x.reshape(slot_total, width), preferred_element_type=jnp.float32
    ).astype(jnp.bfloat16)
    grad_probs = (
        jnp.dot(placing.T, back_s.reshape(-1), preferred_element_type=jnp.float32)
        .astype(jnp.bfloat16)
        .reshape(tok_rows, 2)
    )
    return (grad_tokens, grad_gate, grad_up, grad_down, grad_probs)


def solution(mesh):
    in_specs = (
        P(("expert", "ffn"), "dp"),
        P(("expert", "ffn"), "dp"),
        P(("expert", "ffn"), None),
        P(("expert", "ffn"), None),
        P("expert", "dp", "ffn"),
        P("expert", "dp", "ffn"),
        P("expert", "ffn", "dp"),
    )
    out_specs = (
        P(("expert", "ffn"), "dp"),
        P("expert", "dp", "ffn"),
        P("expert", "dp", "ffn"),
        P("expert", "ffn", "dp"),
        P(("expert", "ffn"), None),
    )
    return jax.shard_map(
        per_device, mesh=mesh, in_specs=in_specs, out_specs=out_specs, check_vma=False
    )
```

profile of v0, /device:TPU:8, one launch (start us, length us, event | category | flops | bytes accessed | tf_op | source)
XLA Modules:
  0.0 484.3 jit_solution(17050456012884972732)
XLA Ops:
  9.6 15.1 %all_to_all.37 = bf16[8,3,1024]{2,1,0:T(4,128)(2,1)S(1)} all-to-all(bf16[8,3,1024]{2,1,0:T(4,128)(2,1)S(1)} %reshape.76), channel_id=1, replica_groups=mesh['expert'=8,'ffn'=32,'dp'=2] {'expert'}, dimensions={0} | all-to-all | bytes 98304 | tf_op jit(solution)/shard_map/all_to_all | solution.py:52
  26.4 10.8 %all_to_all.38 = bf16[8,3,1024]{2,1,0:T(4,128)(2,1)S(1)} all-to-all(bf16[8,3,1024]{2,1,0:T(4,128)(2,1)S(1)} %reshape.78), channel_id=1, replica_groups=mesh['expert'=8,'ffn'=32,'dp'=2] {'expert'}, dimensions={0} | all-to-all | bytes 98304 | tf_op jit(solution)/shard_map/all_to_all | solution.py:51
  37.9 70.6 %all-gather.4.cloned.1.call-done = bf16[256,3,1024]{2,0,1:T(8,128)(2,1)} async-done(((bf16[8,3,1024]{2,0,1:T(8,128)(2,1)}), bf16[256,3,1024]{2,0,1:T(8,128)(2,1)}) %all-gather.4.cloned.1.call-update) | async-done | bytes 1572880 | tf_op jit(solution)/shard_map/all_gather | solution.py:57
  108.5 2.8 copy.63
  111.3 2.5 reshape.77
  113.8 78.7 %all-gather.6.cloned.1.call-done = bf16[256,3,1024]{2,0,1:T(8,128)(2,1)} async-done(((bf16[8,3,1024]{2,0,1:T(8,128)(2,1)}), bf16[256,3,1024]{2,0,1:T(8,128)(2,1)}) %all-gather.6.cloned.1.call-update) | async-done | bytes 1572880 | tf_op jit(solution)/shard_map/all_gather | solution.py:56
  192.5 4.1 copy.65
  196.6 3.9 reshape.79
  200.5 1.5 fusion.11
  202.0 1.5 fusion.14
  203.6 1.5 fusion.16
  206.8 7.3 %all-to-all-start = ((bf16[8,1,3]{2,1,0:T(2,128)(2,1)}), bf16[8,1,3]{2,1,0:T(2,128)(2,1)S(1)}, u32[]{:S(2)}, u32[]{:S(2)}) async-start(bf16[8,1,3]{2,1,0:T(2,128)(2,1)} %all_to_all.31), calls=%async_computation | async-start | bytes 8192 | tf_op jit(solution)/shard_map/all_to_all | solution.py:53
  216.0 4.2 all-to-all-done
  220.2 41.8 %all-gather = bf16[256,1,3]{2,1,0:T(2,128)(2,1)S(1)} all-gather(bf16[8,1,3]{2,1,0:T(2,128)(2,1)S(1)} %all-to-all-done), channel_id=2, replica_groups=mesh['expert'=8,'ffn'=32,'dp'=2] {'ffn'}, dimensions={0}, use_global_device_ids=true | all-gather | bytes 1584 | tf_op jit(solution)/shard_map/all_gather | solution.py:58
  262.6 2.2 multiply_reduce_fusion
  266.3 2.3 fusion.9
  268.5 1.5 fusion.5
  272.3 2.3 convolution_add_fusion
  274.6 5.8 %reshape.80 = f32[256,3,1024]{2,1,0:T(4,128)} reshape(f32[768,1024]{1,0:T(8,128)} %convolution_add_fusion) | data formatting | bytes 6291456 | tf_op jit(solution)/shard_map/reshape | solution.py:78
  280.4 173.2 %all-reduce.8 = (bf16[256,3,1024]{2,1,0:T(4,128)(2,1)S(1)}, bf16[256,3]{1,0:T(8,128)(2,1)S(1)}) all-reduce(f32[256,3,1024]{2,1,0:T(4,128)} %reshape.80, f32[256,3]{1,0:T(8,128)S(1)} %reshape.82), channel_id=3, replica_groups=mesh['expert'=8,'ffn'=32,'dp'=2] {'ffn'}, use_global_device_ids=true, to_apply=%region_6.7.clone | all-reduce | flops 787200 | bytes 4723200
  454.5 4.7 all-to-all-start.4
  459.8 5.5 %all-to-all-done.4 = bf16[8,1,3]{2,1,0:T(2,128)(2,1)S(1)} async-done(((bf16[8,1,3]{2,1,0:T(2,128)(2,1)}), bf16[8,1,3]{2,1,0:T(2,128)(2,1)S(1)}, u32[]{:S(2)}, u32[]{:S(2)}) %all-to-all-start.4) | async-done | bytes 80 | tf_op jit(solution)/shard_map/all_to_all | solution.py:91
  465.3 4.7 all-to-all-start.3
  471.0 5.9 %all-to-all-done.3 = bf16[8,3,1024]{2,1,0:T(4,128)(2,1)S(1)} async-done(((bf16[8,3,1024]{2,1,0:T(4,128)(2,1)}), bf16[8,3,1024]{2,1,0:T(4,128)(2,1)S(1)}, u32[]{:S(2)}, u32[]{:S(2)}) %all-to-all-start.3) | async-done | bytes 49184 | tf_op jit(solution)/shard_map/all_to_all | solution.py:88
  (59 shorter events, 15.4 us)
Async XLA Ops:
  7.2 193.3 %copy-start = (bf16[1,1024,256]{2,1,0:T(8,128)(2,1)S(1)}, bf16[1,1024,256]{2,1,0:T(8,128)(2,1)}, u32[]{:S(2)}) copy-start(bf16[1,1024,256]{2,1,0:T(8,128)(2,1)} %param.11) | copy-start | bytes 1572868
  7.2 101.3 %all-gather.4.cloned.1.call-start = ((), (), s32[]{:S(2)}) async-start(), calls=%async_computation.5 | async-start | bytes 1622016 | tf_op jit(solution)/shard_map/all_gather | solution.py:57
  25.4 167.1 %all-gather.6.cloned.1.call-start = ((), (), s32[]{:S(2)}) async-start(), calls=%async_computation.6 | async-start | bytes 1622016 | tf_op jit(solution)/shard_map/all_gather | solution.py:56
  37.8 224.8 %all-reduce.7.cloned.1.call-start = ((), (), s32[]{:S(2)}) async-start(), calls=%async_computation.7 | async-start | bytes 4718592 | tf_op jit(solution)/shard_map/psum | solution.py:69
  200.5 1.5 copy-start.4
  202.0 1.5 copy-start.2
  202.0 1.6 copy-start.5
  205.1 0.7 copy-start.6
  206.8 13.4 %all-to-all-start = ((bf16[8,1,3]{2,1,0:T(2,128)(2,1)}), bf16[8,1,3]{2,1,0:T(2,128)(2,1)S(1)}, u32[]{:S(2)}, u32[]{:S(2)}) async-start(bf16[8,1,3]{2,1,0:T(2,128)(2,1)} %all_to_all.31), calls=%async_computation | async-start | bytes 8192 | tf_op jit(solution)/shard_map/all_to_all | solution.py:53
  266.3 2.3 copy-start.3
  270.2 2.1 copy-start.1
  454.5 10.8 %all-to-all-start.4 = ((bf16[8,1,3]{2,1,0:T(2,128)(2,1)}), bf16[8,1,3]{2,1,0:T(2,128)(2,1)S(1)}, u32[]{:S(2)}, u32[]{:S(2)}) async-start(bf16[8,1,3]{2,1,0:T(2,128)(2,1)} %copy.67), calls=%async_computation.4 | async-start | bytes 8192 | tf_op jit(solution)/shard_map/all_to_all | solution.py:91
  465.3 11.7 %all-to-all-start.3 = ((bf16[8,3,1024]{2,1,0:T(4,128)(2,1)}), bf16[8,3,1024]{2,1,0:T(4,128)(2,1)S(1)}, u32[]{:S(2)}, u32[]{:S(2)}) async-start(bf16[8,3,1024]{2,1,0:T(4,128)(2,1)} %dynamic-slice_convert_fusion), calls=%async_computation.3 | async-start | bytes 131072 | tf_op jit(solution)/shard_map/all_to_all | solution.py:88
Sparse Core Ops, SparseCore 0:
  25.5 82.9 all-gather.3
  112.2 80.1 all-gather.5
  205.3 34.9 all-reduce.6
where the time goes:
time: 485 us; the launch traced here: 484 us
  blocking collectives  241 us (50%)
  waiting for transfers between devices  165 us (34%)
  local copies, waits for them, and re-layouts  27.7 us (6%)
  starting transfers between devices  16.8 us (3%)
  matrix products  16.3 us (3%)
  between operations  14.5 us (3%)
    unnamed x1, blocking collectives  173 us
    all_gather x1, waiting for transfers between devices, per_device(): lax.all_gather(recv_x, 'ffn', axis=0, tiled=True)  78.7 us
    all_gather x1, waiting for transfers between devices, per_device(): lax.all_gather(recv_dy, 'ffn', axis=0, tiled=True)  70.6 us
    all_gather x1, blocking collectives, per_device(): lax.all_gather(recv_p, 'ffn', axis=0, tiled=True)  41.8 us
    all_to_all x1, blocking collectives, per_device(): lax.all_to_all(send_dy, 'expert', split_axis=0, concat_axis=0, tiled=True)  15.1 us
    all_to_all x1, blocking collectives, per_device(): lax.all_to_all(send_x, 'expert', split_axis=0, concat_axis=0, tiled=True)  10.8 us
    dot_general x6, matrix products, contract(): lax.dot_general(left, right, (((left_dim,), (right_dim,)), ((), ())), pre...  10.5 us
  transfers between devices with their start and end apart: 6, of which 5 were waited for; matrix products, arithmetic and copies ran while one was open for 2% of the time, Pallas kernels for 0%

commit v1 on v0

v1 whole, which is shorter than its diff:
```python
import jax
import jax.numpy as jnp
from jax import lax
from jax.sharding import Mesh
from jax.sharding import PartitionSpec as P

CAP = 3
LANES = 128


def contract(left, right, left_dim, right_dim):
    return lax.dot_general(
        left, right, (((left_dim,), (right_dim,)), ((), ())), preferred_element_type=jnp.float32
    )


def exchange(block, axes):
    return lax.all_to_all(block, axes, split_axis=0, concat_axis=0, tiled=True)


def per_device(tokens, out_grad, expert_ids, gate_probs, w_gate, w_up, w_down):
    experts = lax.axis_size("expert")
    nx = lax.axis_size("x")
    nz = lax.axis_size("z")
    tok_rows, width = tokens.shape
    chunks = width // LANES
    slots = experts * CAP

    flat_ids = expert_ids.reshape(-1)
    onehot = (flat_ids[:, None] == jnp.arange(experts, dtype=jnp.int32)[None, :]).astype(jnp.int32)
    earlier = jnp.tril(jnp.ones((2 * tok_rows, 2 * tok_rows), jnp.int32), -1)
    same = (flat_ids[:, None] == flat_ids[None, :]).astype(jnp.int32)
    ranks = jnp.sum(same * earlier, axis=1)
    position = (flat_ids * CAP + ranks).reshape(tok_rows, 2)
    slot_names = jnp.arange(slots, dtype=jnp.int32)
    place0 = slot_names[:, None] == position[None, :, 0]
    place1 = slot_names[:, None] == position[None, :, 1]
    placing = (place0 | place1).astype(jnp.bfloat16)
    probs = gate_probs.astype(jnp.bfloat16).astype(jnp.float32)
    slot_prob = jnp.sum(
        jnp.where(place0, probs[None, :, 0], 0.0) + jnp.where(place1, probs[None, :, 1], 0.0),
        axis=1,
        keepdims=True,
    )
    send_x = contract(placing, tokens, 1, 0).astype(jnp.bfloat16)
    send_dy = (contract(placing, out_grad, 1, 0) * slot_prob).astype(jnp.bfloat16)
    send = jnp.concatenate([send_x, send_dy], axis=1)
    send = send.reshape(experts, 1, CAP * 2 * chunks, LANES)
    send = jnp.broadcast_to(send, (experts, nz, CAP * 2 * chunks, LANES))
    send = send.reshape(experts * nz, CAP * 2 * chunks, LANES)

    recv = exchange(send, ("expert", "z"))
    part_rows = experts * nz * CAP
    block = recv.reshape(part_rows, 2 * width)
    block = jnp.broadcast_to(block[None], (nx, part_rows, 2 * width))
    rows = exchange(block, "x").reshape(nx * part_rows, 2 * width)
    rows_x = rows[:, :width]
    rows_dy = rows[:, width:]

    gate_w = w_gate[0]
    up_w = w_up[0]
    down_w = w_down[0]
    partial = jnp.concatenate(
        [
            contract(rows_x, gate_w, 1, 0),
            contract(rows_x, up_w, 1, 0),
            contract(rows_dy, down_w, 1, 1),
        ],
        axis=1,
    ).astype(jnp.bfloat16)
    other = lax.ppermute(partial, "dp", [(0, 1), (1, 0)])
    total = partial.astype(jnp.float32) + other.astype(jnp.float32)
    hid = gate_w.shape[1]
    gate_pre, up_pre, d_hidden = total[:, :hid], total[:, hid : 2 * hid], total[:, 2 * hid :]

    sigmoid_gate = jax.nn.sigmoid(gate_pre)
    silu_gate = gate_pre * sigmoid_gate
    hidden = (silu_gate * up_pre).astype(jnp.bfloat16)
    score = jnp.sum(d_hidden * hidden.astype(jnp.float32), axis=1)
    grad_gate_pre = (
        d_hidden * up_pre * sigmoid_gate * (1.0 + gate_pre * (1.0 - sigmoid_gate))
    ).astype(jnp.bfloat16)
    grad_up_pre = (d_hidden * silu_gate).astype(jnp.bfloat16)

    input_part = (
        contract(grad_gate_pre, gate_w, 1, 1) + contract(grad_up_pre, up_w, 1, 1)
    ).astype(jnp.bfloat16)
    score_rows = score.astype(jnp.bfloat16).reshape(nx, 1, part_rows)
    score_rows = jnp.pad(score_rows, ((0, 0), (0, 7), (0, width - part_rows)))
    back = jnp.concatenate([input_part.reshape(nx, part_rows, width), score_rows], axis=1)
    back = exchange(back.reshape(nx * (part_rows + 8), width), "x")
    back = jnp.sum(back.reshape(nx, part_rows + 8, width).astype(jnp.float32), axis=0)
    back = back.astype(jnp.bfloat16)

    grad_gate = contract(rows_x, grad_gate_pre, 0, 0).astype(jnp.bfloat16)[None]
    grad_up = contract(rows_x, grad_up_pre, 0, 0).astype(jnp.bfloat16)[None]
    grad_down = contract(hidden, rows_dy, 0, 0).astype(jnp.bfloat16)[None]

    data = back[:part_rows].reshape(experts * nz, CAP * chunks, LANES)
    marks = jnp.pad(
        back[part_rows, :part_rows].reshape(experts * nz, 1, CAP),
        ((0, 0), (0, 7), (0, LANES - CAP)),
    )
    home = exchange(jnp.concatenate([data, marks], axis=1), ("expert", "z"))
    home = jnp.sum(
        home.reshape(experts, nz, CAP * chunks + 8, LANES).astype(jnp.float32), axis=1
    )
    pair_rows = home[:, : CAP * chunks].astype(jnp.bfloat16).reshape(slots, width)
    pair_score = home[:, CAP * chunks, :CAP].reshape(slots, 1)
    grad_tokens = contract(placing, pair_rows, 0, 0).astype(jnp.bfloat16)
    score0 = jnp.sum(jnp.where(place0, pair_score, 0.0), axis=0)
    score1 = jnp.sum(jnp.where(place1, pair_score, 0.0), axis=0)
    grad_probs = (jnp.stack([score0, score1], axis=1) / probs).astype(jnp.bfloat16)
    return (grad_tokens, grad_gate, grad_up, grad_down, grad_probs)


def solution(mesh):
    names = dict(zip(mesh.axis_names, mesh.devices.shape))
    nz = 8
    nx = names["ffn"] // nz
    grid = Mesh(
        mesh.devices.reshape(names["expert"], nx, nz, names["dp"]), ("expert", "x", "z", "dp")
    )
    toks = P(("expert", "x", "z"), "dp")
    pairs = P(("expert", "x", "z"), None)
    wide = P("expert", "dp", ("x", "z"))
    tall = P("expert", ("x", "z"), "dp")
    return jax.shard_map(
        per_device,
        mesh=grid,
        in_specs=(toks, toks, pairs, pairs, wide, wide, tall),
        out_specs=(toks, wide, wide, tall, pairs),
        check_vma=False,
    )
```

time: 485 us -> 152 us (0.31)
  the two profiles are of different devices: /device:TPU:8 before, /device:TPU:6 now
where the time goes in v1:
time: 152 us; the launch traced here: 149 us
  blocking collectives  102 us (67%)
  waiting for transfers between devices  14.1 us (9%)
  matrix products  13.2 us (9%)
  starting transfers between devices  11.2 us (7%)
  other arithmetic  4.8 us (3%)
  local copies, waits for them, and re-layouts  3.33 us (2%)
    all_to_all x3, blocking collectives, exchange(): return lax.all_to_all(block, axes, split_axis=0, concat_axis=0, tiled=True)  102 us
    dot_general x11, matrix products, contract(): lax.dot_general(left, right, (((left_dim,), (right_dim,)), ((), ())), pre...  13.2 us
    all_to_all x1, waiting for transfers between devices, exchange(): return lax.all_to_all(block, axes, split_axis=0, concat_axis=0, tiled=True)  11.3 us
    all_to_all x1, starting transfers between devices, exchange(): return lax.all_to_all(block, axes, split_axis=0, concat_axis=0, tiled=True)  9.31 us
  transfers between devices with their start and end apart: 2, of which 2 were waited for; matrix products, arithmetic and copies ran while one was open for 5% of the time, Pallas kernels for 0%

profile of v1, /device:TPU:6, one launch (start us, length us, event | category | flops | bytes accessed | tf_op | source)
XLA Modules:
  0.0 149.4 jit_solution(16161279547601517529)
XLA Ops:
  0.7 0.7 convert_convert_fusion
  1.4 0.8 copy.24
  2.7 1.0 convolution_convert_fusion.4
  3.8 1.0 fusion.17
  5.0 40.0 %all_to_all.21 = bf16[64,48,128]{2,1,0:T(8,128)(2,1)S(1)} all-to-all(bf16[64,48,128]{2,1,0:T(8,128)(2,1)S(1)} %bitcast.46), channel_id=1, replica_groups=mesh['expert'=8,'x'=4,'z'=8,'dp'=2] {'expert','z'}, dimensions={0} | all-to-all | bytes 1572864 | tf_op jit(solution)/shard_map/all_to_all | solution.py:18
  45.7 37.4 %all_to_all.22 = bf16[4,192,2048]{2,1,0:T(8,128)(2,1)S(1)} all-to-all(bf16[4,192,2048]{2,1,0:T(8,128)(2,1)S(1)} %broadcast_in_dim.81), channel_id=1, replica_groups=mesh['expert'=8,'x'=4,'z'=8,'dp'=2] {'x'}, dimensions={0} | all-to-all | bytes 6291456 | tf_op jit(solution)/shard_map/all_to_all | solution.py:18
  83.2 0.7 convolution_convert_fusion.2
  83.8 0.7 copy-done.6
  84.6 0.7 fusion.9
  85.2 0.7 convolution_convert_fusion.3
  86.0 1.9 %collective-permute-start = (bf16[768,768]{0,1:T(8,128)(2,1)S(1)}, bf16[768,768]{0,1:T(8,128)(2,1)S(1)}, u32[]{:S(2)}, u32[]{:S(2)}) collective-permute-start(bf16[768,768]{0,1:T(8,128)(2,1)S(1)} %pad_maximum_fusion), channel_id=1, source_target_pairs={{0,1},{1,0},{2,3},{3,2},{4,5},{5,4},{6,7},{7,6},{8,9},{9,8},{10,11... | collective-permute-start | bytes 3538952 | tf_op jit(solution)/shard_map/ppermute | solution.py:71
  87.9 2.8 %collective-permute-done = bf16[768,768]{0,1:T(8,128)(2,1)S(1)} collective-permute-done((bf16[768,768]{0,1:T(8,128)(2,1)S(1)}, bf16[768,768]{0,1:T(8,128)(2,1)S(1)}, u32[]{:S(2)}, u32[]{:S(2)}) %collective-permute-start) | collective-permute-done | bytes 1179680 | tf_op jit(solution)/shard_map/ppermute | solution.py:71
  91.0 1.3 multiply_reduce_fusion
  92.4 0.6 fusion.28
  93.0 0.6 add_convert_fusion
  93.8 24.4 %all_to_all.23 = bf16[4,200,1024]{2,1,0:T(8,128)(2,1)S(1)} all-to-all(bf16[4,200,1024]{2,1,0:T(8,128)(2,1)S(1)} %fusion.1), channel_id=1, replica_groups=mesh['expert'=8,'x'=4,'z'=8,'dp'=2] {'x'}, dimensions={0} | all-to-all | bytes 3276800 | tf_op jit(solution)/shard_map/all_to_all | solution.py:18
  119.0 0.9 fusion.24
  119.9 9.3 %all-to-all-start.3 = ((bf16[64,32,128]{2,1,0:T(8,128)(2,1)}), bf16[64,32,128]{2,1,0:T(8,128)(2,1)S(1)}, u32[]{:S(2)}, u32[]{:S(2)}) async-start(bf16[64,32,128]{2,1,0:T(8,128)(2,1)} %fusion.24), calls=%async_computation.3 | async-start | bytes 1048576 | tf_op jit(solution)/shard_map/all_to_all | solution.py:18
  129.2 2.8 %fusion.14 = bf16[1,256,1024]{2,1,0:T(8,128)(2,1)} fusion(bf16[768,256]{0,1:T(8,128)(2,1)S(1)} %copy-done.4, bf16[768,2048]{1,0:T(8,128)(2,1)} %bitcast.43), kind=kOutput, calls=%fused_computation.17 | convolution fusion | flops 402915328 | bytes 2490368 | tf_op jit(solution)/shard_map/dot_general | solution.py:12
  132.0 3.0 %fusion.13 = bf16[1,1024,256]{2,1,0:T(8,128)(2,1)} fusion(bf16[768,256]{0,1:T(8,128)(2,1)S(1)} %get-tuple-element.11, bf16[768,2048]{1,0:T(8,128)(2,1)} %bitcast.44), kind=kOutput, calls=%fused_computation.16 | convolution fusion | flops 402915328 | bytes 2490368 | tf_op jit(solution)/shard_map/dot_general | solution.py:12
  134.9 1.4 fusion.12
  136.4 11.3 %all-to-all-done.3 = bf16[64,32,128]{2,1,0:T(8,128)(2,1)S(1)} async-done(((bf16[64,32,128]{2,1,0:T(8,128)(2,1)}), bf16[64,32,128]{2,1,0:T(8,128)(2,1)S(1)}, u32[]{:S(2)}, u32[]{:S(2)}) %all-to-all-start.3) | async-done | bytes 524320 | tf_op jit(solution)/shard_map/all_to_all | solution.py:18
  147.9 0.8 convolution_convert_fusion.5
  148.9 0.5 fusion.41
  (41 shorter events, 3.2 us)
Async XLA Ops:
  0.6 84.6 %copy-start = (bf16[1,1024,256]{2,1,0:T(8,128)(2,1)S(1)}, bf16[1,1024,256]{2,1,0:T(8,128)(2,1)}, u32[]{:S(2)}) copy-start(bf16[1,1024,256]{2,1,0:T(8,128)(2,1)} %param.11) | copy-start | bytes 1572868
  45.7 37.5 %copy-start.3 = (bf16[1,1024,256]{2,1,0:T(8,128)(2,1)S(1)}, bf16[1,1024,256]{2,1,0:T(8,128)(2,1)}, u32[]{:S(2)}) copy-start(bf16[1,1024,256]{2,1,0:T(8,128)(2,1)} %param.12) | copy-start | bytes 1572868
  83.2 2.1 %copy-start.1 = (bf16[4,192,2048]{2,1,0:T(8,128)(2,1)}, bf16[4,192,2048]{2,1,0:T(8,128)(2,1)S(1)}, u32[]{:S(2)}) copy-start(bf16[4,192,2048]{2,1,0:T(8,128)(2,1)S(1)} %all_to_all.22) | copy-start | bytes 9437188
  83.2 1.4 copy-start.6
  86.0 4.7 %collective-permute-start = (bf16[768,768]{0,1:T(8,128)(2,1)S(1)}, bf16[768,768]{0,1:T(8,128)(2,1)S(1)}, u32[]{:S(2)}, u32[]{:S(2)}) collective-permute-start(bf16[768,768]{0,1:T(8,128)(2,1)S(1)} %pad_maximum_fusion), channel_id=1, source_target_pairs={{0,1},{1,0},{2,3},{3,2},{4,5},{5,4},{6,7},{7,6},{8,9},{9,8},{10,11... | collective-permute-start | bytes 3538952 | tf_op jit(solution)/shard_map/ppermute | solution.py:71
  118.6 10.6 %copy-start.4 = (bf16[768,256]{0,1:T(8,128)(2,1)S(1)}, bf16[768,256]{0,1:T(8,128)(2,1)}, u32[]{:S(2)}) copy-start(bf16[768,256]{0,1:T(8,128)(2,1)} %get-tuple-element.10) | copy-start | bytes 1179652
  119.9 27.8 %all-to-all-start.3 = ((bf16[64,32,128]{2,1,0:T(8,128)(2,1)}), bf16[64,32,128]{2,1,0:T(8,128)(2,1)S(1)}, u32[]{:S(2)}, u32[]{:S(2)}) async-start(bf16[64,32,128]{2,1,0:T(8,128)(2,1)} %fusion.24), calls=%async_computation.3 | async-start | bytes 1048576 | tf_op jit(solution)/shard_map/all_to_all | solution.py:18
  132.0 3.0 %copy-start.2 = (bf16[4,192,2048]{2,1,0:T(8,128)(2,1)S(1)}, bf16[4,192,2048]{2,1,0:T(8,128)(2,1)}, u32[]{:S(2)}) copy-start(bf16[4,192,2048]{2,1,0:T(8,128)(2,1)} %copy-done.1) | copy-start | bytes 9437188
  134.9 13.9 %copy-start.5 = (f32[8,2]{0,1:T(2,128)S(1)}, f32[8,2]{0,1:T(2,128)}, u32[]{:S(2)}) copy-start(f32[8,2]{0,1:T(2,128)} %param.10) | copy-start | bytes 196

commit v2 on v1

--- a/solution.py
+++ b/solution.py
@@ -52,26 +52,25 @@
     recv = exchange(send, ("expert", "z"))
     part_rows = experts * nz * CAP
     block = recv.reshape(part_rows, 2 * width)
-    block = jnp.broadcast_to(block[None], (nx, part_rows, 2 * width))
-    rows = exchange(block, "x").reshape(nx * part_rows, 2 * width)
-    rows_x = rows[:, :width]
-    rows_dy = rows[:, width:]
+    rows_dy = lax.all_gather(block[:, width:], "x", axis=0, tiled=True)
+    block = jnp.broadcast_to(block[None, :, :width], (nx, part_rows, width))
+    rows_x = exchange(block, "x").reshape(nx * part_rows, width)
 
     gate_w = w_gate[0]
     up_w = w_up[0]
     down_w = w_down[0]
-    partial = jnp.concatenate(
-        [
-            contract(rows_x, gate_w, 1, 0),
-            contract(rows_x, up_w, 1, 0),
-            contract(rows_dy, down_w, 1, 1),
-        ],
-        axis=1,
-    ).astype(jnp.bfloat16)
-    other = lax.ppermute(partial, "dp", [(0, 1), (1, 0)])
-    total = partial.astype(jnp.float32) + other.astype(jnp.float32)
     hid = gate_w.shape[1]
-    gate_pre, up_pre, d_hidden = total[:, :hid], total[:, hid : 2 * hid], total[:, 2 * hid :]
+
+    def both(partial):
+        partial = partial.astype(jnp.bfloat16)
+        other = lax.ppermute(partial, "dp", [(0, 1), (1, 0)])
+        return partial.astype(jnp.float32) + other.astype(jnp.float32)
+
+    pre = both(
+        jnp.concatenate([contract(rows_x, gate_w, 1, 0), contract(rows_x, up_w, 1, 0)], axis=1)
+    )
+    gate_pre, up_pre = pre[:, :hid], pre[:, hid:]
+    d_hidden = both(contract(rows_dy, down_w, 1, 1))
 
     sigmoid_gate = jax.nn.sigmoid(gate_pre)
     silu_gate = gate_pre * sigmoid_gate
@@ -99,11 +98,14 @@
     data = back[:part_rows].reshape(experts * nz, CAP * chunks, LANES)
     marks = jnp.pad(
         back[part_rows, :part_rows].reshape(experts * nz, 1, CAP),
-        ((0, 0), (0, 7), (0, LANES - CAP)),
+        ((0, 0), (0, 1), (0, LANES - CAP)),
     )
-    home = exchange(jnp.concatenate([data, marks], axis=1), ("expert", "z"))
+    home = jnp.concatenate([data, marks], axis=1)
+    home = exchange(
+        home.reshape(experts * nz, CAP * chunks // 2 + 1, 2, LANES), ("expert", "z")
+    )
     home = jnp.sum(
-        home.reshape(experts, nz, CAP * chunks + 8, LANES).astype(jnp.float32), axis=1
+        home.reshape(experts, nz, CAP * chunks + 2, LANES).astype(jnp.float32), axis=1
     )
     pair_rows = home[:, : CAP * chunks].astype(jnp.bfloat16).reshape(slots, width)
     pair_score = home[:, CAP * chunks, :CAP].reshape(slots, 1)

time: 152 us -> 160 us (1.053)
  between operations: 0.88 us -> 14.4 us
  blocking collectives: 102 us -> 97.8 us
  local copies, waits for them, and re-layouts: 3.33 us -> 5.21 us
    all_to_all x3, blocking collectives: 102 us -> 97.8 us  [exchange(): return lax.all_to_all(block, axes, split_axis=0, concat_axis=0, tiled=True)]
    ppermute x1 -> x2, starting transfers between devices: 1.92 us -> 4.33 us  [both(): other = lax.ppermute(partial, 'dp', [(0, 1), (1, 0)])]
    all_to_all x1, starting transfers between devices: 9.31 us -> 7.28 us  [exchange(): return lax.all_to_all(block, axes, split_axis=0, concat_axis=0, tiled=True)]
    ppermute x1 -> x2, waiting for transfers between devices: 2.81 us -> 1.15 us  [both(): other = lax.ppermute(partial, 'dp', [(0, 1), (1, 0)])]
    all_to_all x1, waiting for transfers between devices: 11.3 us -> 12.9 us  [exchange(): return lax.all_to_all(block, axes, split_axis=0, concat_axis=0, tiled=True)]
    dot_general x11, matrix products: 13.2 us -> 11.6 us  [contract(): lax.dot_general(left, right, (((left_dim,), (right_dim,)), ((), ())), pre...]
  transfers between devices with their start and end apart: 2 -> 4, of which waited for: 2 -> 2; matrix products, arithmetic and copies ran while one was open for 5% -> 5% of each run, Pallas kernels for 0% -> 0%
where the time goes in v2:
time: 160 us; the launch traced here: 158 us
  blocking collectives  97.8 us (61%)
  between operations  14.4 us (9%)
  waiting for transfers between devices  14.1 us (9%)
  starting transfers between devices  11.6 us (7%)
  matrix products  11.6 us (7%)
  local copies, waits for them, and re-layouts  5.21 us (3%)
  other arithmetic  3.37 us (2%)
    all_to_all x3, blocking collectives, exchange(): return lax.all_to_all(block, axes, split_axis=0, concat_axis=0, tiled=True)  97.8 us
    all_to_all x1, waiting for transfers between devices, exchange(): return lax.all_to_all(block, axes, split_axis=0, concat_axis=0, tiled=True)  12.9 us
    dot_general x11, matrix products, contract(): lax.dot_general(left, right, (((left_dim,), (right_dim,)), ((), ())), pre...  11.6 us
    all_to_all x1, starting transfers between devices, exchange(): return lax.all_to_all(block, axes, split_axis=0, concat_axis=0, tiled=True)  7.28 us
    ppermute x2, starting transfers between devices, both(): other = lax.ppermute(partial, 'dp', [(0, 1), (1, 0)])  4.33 us
  transfers between devices with their start and end apart: 4, of which 2 were waited for; matrix products, arithmetic and copies ran while one was open for 5% of the time, Pallas kernels for 0%

profile of v2, /device:TPU:6, one launch (start us, length us, event | category | flops | bytes accessed | tf_op | source)
XLA Modules:
  0.0 158.1 jit_solution(15955969230307733989)
XLA Ops:
  7.2 0.7 convert_convert_fusion
  8.0 0.8 copy.33
  9.3 1.0 convolution_convert_fusion.6
  10.4 1.0 fusion.5
  11.5 40.0 %all_to_all.21 = bf16[64,48,128]{2,1,0:T(8,128)(2,1)S(1)} all-to-all(bf16[64,48,128]{2,1,0:T(8,128)(2,1)S(1)} %bitcast.48), channel_id=1, replica_groups=mesh['expert'=8,'x'=4,'z'=8,'dp'=2] {'expert','z'}, dimensions={0} | all-to-all | bytes 1572864 | tf_op jit(solution)/shard_map/all_to_all | solution.py:18
  51.9 0.8 fusion.26
  52.9 32.8 %all_to_all.22 = bf16[4,192,1024]{2,1,0:T(8,128)(2,1)S(1)} all-to-all(bf16[4,192,1024]{2,1,0:T(8,128)(2,1)S(1)} %broadcast_in_dim.79), channel_id=1, replica_groups=mesh['expert'=8,'x'=4,'z'=8,'dp'=2] {'x'}, dimensions={0} | all-to-all | bytes 3145728 | tf_op jit(solution)/shard_map/all_to_all | solution.py:18
  85.8 0.6 convolution_convert_fusion.3
  86.5 0.6 convolution_convert_fusion.4
  87.2 1.9 %collective-permute-start.1 = (bf16[768,512]{0,1:T(8,128)(2,1)S(1)}, bf16[768,512]{0,1:T(8,128)(2,1)S(1)}, u32[]{:S(2)}, u32[]{:S(2)}) collective-permute-start(bf16[768,512]{0,1:T(8,128)(2,1)S(1)} %pad_maximum_fusion), channel_id=1, source_target_pairs={{0,1},{1,0},{2,3},{3,2},{4,5},{5,4},{6,7},{7,6},{8,9},{9,8},{10,11... | collective-permute-start | bytes 2359304 | tf_op jit(solution)/shard_map/ppermute | solution.py:66
  89.1 2.0 %convolution_convert_fusion.5 = bf16[768,256]{0,1:T(8,128)(2,1)S(1)} fusion(bf16[768,1024]{1,0:T(8,128)(2,1)} %all-gather.2.cloned.1.call-done, bf16[1,256,1024]{2,1,0:T(8,128)(2,1)S(1)} %copy-done.9), kind=kOutput, calls=%fused_computation.10 | convolution fusion | flops 402849792 | bytes 2490368 | tf_op jit(solution)/shard_map/dot_general | solution.py:12
  91.2 2.4 %collective-permute-start = (bf16[768,256]{0,1:T(8,128)(2,1)S(1)}, bf16[768,256]{0,1:T(8,128)(2,1)S(1)}, u32[]{:S(2)}, u32[]{:S(2)}) collective-permute-start(bf16[768,256]{0,1:T(8,128)(2,1)S(1)} %convolution_convert_fusion.5), channel_id=1, source_target_pairs={{0,1},{1,0},{2,3},{3,2},{4,5},{5,4},{6,7},{7,6},{8,9},{9,8},{10,11... | collective-permute-start | bytes 1179656 | tf_op jit(solution)/shard_map/ppermute | solution.py:66
  93.8 1.2 collective-permute-done
  94.9 0.5 multiply_reduce_fusion
  95.5 0.6 fusion.11
  96.7 0.6 add_convert_fusion
  97.5 24.9 %all_to_all.23 = bf16[4,200,1024]{2,1,0:T(8,128)(2,1)S(1)} all-to-all(bf16[4,200,1024]{2,1,0:T(8,128)(2,1)S(1)} %fusion.1), channel_id=1, replica_groups=mesh['expert'=8,'x'=4,'z'=8,'dp'=2] {'x'}, dimensions={0} | all-to-all | bytes 3276800 | tf_op jit(solution)/shard_map/all_to_all | solution.py:18
  123.4 1.2 copy.38
  124.6 7.3 %all-to-all-start.3 = ((bf16[64,13,2,128]{3,2,1,0:T(2,128)(2,1)}), bf16[64,13,2,128]{3,2,1,0:T(2,128)(2,1)S(1)}, u32[]{:S(2)}, u32[]{:S(2)}) async-start(bf16[64,13,2,128]{3,2,1,0:T(2,128)(2,1)} %copy.38), calls=%async_computation.3 | async-start | bytes 851968 | tf_op jit(solution)/shard_map/all_to_all | solution.py:18
  131.9 1.4 fusion.4
  133.4 1.4 fusion.3
  134.8 1.4 fusion.2
  136.2 12.9 %all-to-all-done.3 = bf16[64,13,2,128]{3,2,1,0:T(2,128)(2,1)S(1)} async-done(((bf16[64,13,2,128]{3,2,1,0:T(2,128)(2,1)}), bf16[64,13,2,128]{3,2,1,0:T(2,128)(2,1)S(1)}, u32[]{:S(2)}, u32[]{:S(2)}) %all-to-all-start.3) | async-done | bytes 426016 | tf_op jit(solution)/shard_map/all_to_all | solution.py:18
  149.7 0.8 convolution_convert_fusion.7
  (57 shorter events, 4.6 us)
Async XLA Ops:
  7.2 79.3 %copy-start = (bf16[1,1024,256]{2,1,0:T(8,128)(2,1)S(1)}, bf16[1,1024,256]{2,1,0:T(8,128)(2,1)}, u32[]{:S(2)}) copy-start(bf16[1,1024,256]{2,1,0:T(8,128)(2,1)} %param.11) | copy-start | bytes 1572868
  7.2 81.9 %all-gather.2.cloned.1.call-start = ((), (), s32[]{:S(2)}) async-start(), calls=%async_computation.4 | async-start | bytes 1966080 | tf_op jit(solution)/shard_map/all_gather | solution.py:55
  52.9 32.9 %copy-start.6 = (bf16[1,1024,256]{2,1,0:T(8,128)(2,1)S(1)}, bf16[1,1024,256]{2,1,0:T(8,128)(2,1)}, u32[]{:S(2)}) copy-start(bf16[1,1024,256]{2,1,0:T(8,128)(2,1)} %param.12) | copy-start | bytes 1572868
  85.8 1.3 copy-start.2
  86.4 2.7 %copy-start.9 = (bf16[1,256,1024]{2,1,0:T(8,128)(2,1)S(1)}, bf16[1,256,1024]{2,1,0:T(8,128)(2,1)}, u32[]{:S(2)}) copy-start(bf16[1,256,1024]{2,1,0:T(8,128)(2,1)} %param.13) | copy-start | bytes 1572868
  87.2 6.4 %collective-permute-start.1 = (bf16[768,512]{0,1:T(8,128)(2,1)S(1)}, bf16[768,512]{0,1:T(8,128)(2,1)S(1)}, u32[]{:S(2)}, u32[]{:S(2)}) collective-permute-start(bf16[768,512]{0,1:T(8,128)(2,1)S(1)} %pad_maximum_fusion), channel_id=1, source_target_pairs={{0,1},{1,0},{2,3},{3,2},{4,5},{5,4},{6,7},{7,6},{8,9},{9,8},{10,11... | collective-permute-start | bytes 2359304 | tf_op jit(solution)/shard_map/ppermute | solution.py:66
  91.2 3.7 %collective-permute-start = (bf16[768,256]{0,1:T(8,128)(2,1)S(1)}, bf16[768,256]{0,1:T(8,128)(2,1)S(1)}, u32[]{:S(2)}, u32[]{:S(2)}) collective-permute-start(bf16[768,256]{0,1:T(8,128)(2,1)S(1)} %convolution_convert_fusion.5), channel_id=1, source_target_pairs={{0,1},{1,0},{2,3},{3,2},{4,5},{5,4},{6,7},{7,6},{8,9},{9,8},{10,11... | collective-permute-start | bytes 1179656 | tf_op jit(solution)/shard_map/ppermute | solution.py:66
  95.5 0.7 copy-start.4
  95.5 1.1 copy-start.7
  123.1 8.8 %copy-start.1 = (bf16[768,1024]{1,0:T(8,128)(2,1)S(1)}, bf16[768,1024]{1,0:T(8,128)(2,1)}, u32[]{:S(2)}) copy-start(bf16[768,1024]{1,0:T(8,128)(2,1)} %all-gather.2.cloned.1.call-done) | copy-start | bytes 4718596
  124.6 24.5 %all-to-all-start.3 = ((bf16[64,13,2,128]{3,2,1,0:T(2,128)(2,1)}), bf16[64,13,2,128]{3,2,1,0:T(2,128)(2,1)S(1)}, u32[]{:S(2)}, u32[]{:S(2)}) async-start(bf16[64,13,2,128]{3,2,1,0:T(2,128)(2,1)} %copy.38), calls=%async_computation.3 | async-start | bytes 851968 | tf_op jit(solution)/shard_map/all_to_all | solution.py:18
  131.9 1.4 copy-start.3
  131.9 1.5 copy-start.5
  134.8 15.9 %copy-start.8 = (f32[8,2]{0,1:T(2,128)S(1)}, f32[8,2]{0,1:T(2,128)}, u32[]{:S(2)}) copy-start(f32[8,2]{0,1:T(2,128)} %param.10) | copy-start | bytes 196
Sparse Core Ops, SparseCore 0:
  52.8 33.0 all-gather.1

commit v3 on v2

--- a/solution.py
+++ b/solution.py
@@ -49,51 +49,86 @@
     send = jnp.broadcast_to(send, (experts, nz, CAP * 2 * chunks, LANES))
     send = send.reshape(experts * nz, CAP * 2 * chunks, LANES)
 
-    recv = exchange(send, ("expert", "z"))
     part_rows = experts * nz * CAP
-    block = recv.reshape(part_rows, 2 * width)
-    rows_dy = lax.all_gather(block[:, width:], "x", axis=0, tiled=True)
-    block = jnp.broadcast_to(block[None, :, :width], (nx, part_rows, width))
-    rows_x = exchange(block, "x").reshape(nx * part_rows, width)
-
     gate_w = w_gate[0]
     up_w = w_up[0]
     down_w = w_down[0]
     hid = gate_w.shape[1]
 
-    def both(partial):
-        partial = partial.astype(jnp.bfloat16)
-        other = lax.ppermute(partial, "dp", [(0, 1), (1, 0)])
-        return partial.astype(jnp.float32) + other.astype(jnp.float32)
+    def meet(block, mask):
+        return lax.ppermute(block, "x", [(i, i ^ mask) for i in range(nx)])
 
-    pre = both(
-        jnp.concatenate([contract(rows_x, gate_w, 1, 0), contract(rows_x, up_w, 1, 0)], axis=1)
+    def swap(block):
+        return lax.ppermute(block, "dp", [(0, 1), (1, 0)])
+
+    def stacked(gate, up, down):
+        return jnp.concatenate([gate, up] + jnp.split(down, width // hid, axis=1), axis=0)
+
+    def unstacked(stack):
+        gate, up, down = jnp.split(stack, 3, axis=0)
+        return gate, up, jnp.concatenate(jnp.split(down, width // hid, axis=0), axis=1)
+
+    gate_n, up_n, down_n = unstacked(meet(stacked(gate_w, up_w, down_w), 1))
+    gate_w = jnp.concatenate([gate_w, gate_n], axis=1)
+    up_w = jnp.concatenate([up_w, up_n], axis=1)
+    down_w = jnp.concatenate([down_w, down_n], axis=0)
+
+    def project(rows):
+        return jnp.concatenate(
+            [
+                contract(rows[:, :width], gate_w, 1, 0),
+                contract(rows[:, :width], up_w, 1, 0),
+                contract(rows[:, width:], down_w, 1, 1),
+            ],
+            axis=1,
+        ).astype(jnp.bfloat16)
+
+    def pullback(partial, other):
+        total = partial.astype(jnp.float32) + other.astype(jnp.float32)
+        gate_pre, up_pre, d_hidden = jnp.split(total, 3, axis=1)
+        sigmoid_gate = jax.nn.sigmoid(gate_pre)
+        silu_gate = gate_pre * sigmoid_gate
+        hidden = (silu_gate * up_pre).astype(jnp.bfloat16)
+        score = jnp.sum(d_hidden * hidden.astype(jnp.float32), axis=1)
+        grad_gate_pre = (
+            d_hidden * up_pre * sigmoid_gate * (1.0 + gate_pre * (1.0 - sigmoid_gate))
+        ).astype(jnp.bfloat16)
+        grad_up_pre = (d_hidden * silu_gate).astype(jnp.bfloat16)
+        input_part = (
+            contract(grad_gate_pre, gate_w, 1, 1) + contract(grad_up_pre, up_w, 1, 1)
+        ).astype(jnp.bfloat16)
+        return hidden, grad_gate_pre, grad_up_pre, input_part, score.astype(jnp.bfloat16)
+
+    def packed(input_part, score):
+        score_row = jnp.pad(score.reshape(1, part_rows), ((0, 7), (0, width - part_rows)))
+        return jnp.concatenate([input_part, score_row], axis=0)
+
+    own = exchange(send, ("expert", "z")).reshape(part_rows, 2 * width)
+    guest = meet(own, 3)
+    own, guest = lax.optimization_barrier((own, guest))
+    rows = jnp.concatenate([guest, own], axis=0)
+    partial = project(rows)
+    hidden, grad_gate_pre, grad_up_pre, input_part, score = pullback(partial, swap(partial))
+    back = meet(packed(input_part[:part_rows], score[:part_rows]), 3)
+    back = (
+        packed(input_part[part_rows:], score[part_rows:]).astype(jnp.float32)
+        + back.astype(jnp.float32)
+    ).astype(jnp.bfloat16)
+    rows_x, rows_dy = rows[:, :width], rows[:, width:]
+
+    def weight_grads(part):
+        return (
+            contract(rows_x, grad_gate_pre[:, part], 0, 0),
+            contract(rows_x, grad_up_pre[:, part], 0, 0),
+            contract(hidden[:, part], rows_dy, 0, 0),
+        )
+
+    theirs = [g.astype(jnp.bfloat16) for g in weight_grads(slice(hid, None))]
+    theirs = unstacked(meet(stacked(*theirs), 1))
+    grad_gate, grad_up, grad_down = (
+        (mine + other.astype(jnp.float32)).astype(jnp.bfloat16)[None]
+        for mine, other in zip(weight_grads(slice(0, hid)), theirs)
     )
-    gate_pre, up_pre = pre[:, :hid], pre[:, hid:]
-    d_hidden = both(contract(rows_dy, down_w, 1, 1))
-
-    sigmoid_gate = jax.nn.sigmoid(gate_pre)
-    silu_gate = gate_pre * sigmoid_gate
-    hidden = (silu_gate * up_pre).astype(jnp.bfloat16)
-    score = jnp.sum(d_hidden * hidden.astype(jnp.float32), axis=1)
-    grad_gate_pre = (
-        d_hidden * up_pre * sigmoid_gate * (1.0 + gate_pre * (1.0 - sigmoid_gate))
-    ).astype(jnp.bfloat16)
-    grad_up_pre = (d_hidden * silu_gate).astype(jnp.bfloat16)
-
-    input_part = (
-        contract(grad_gate_pre, gate_w, 1, 1) + contract(grad_up_pre, up_w, 1, 1)
-    ).astype(jnp.bfloat16)
-    score_rows = score.astype(jnp.bfloat16).reshape(nx, 1, part_rows)
-    score_rows = jnp.pad(score_rows, ((0, 0), (0, 7), (0, width - part_rows)))
-    back = jnp.concatenate([input_part.reshape(nx, part_rows, width), score_rows], axis=1)
-    back = exchange(back.reshape(nx * (part_rows + 8), width), "x")
-    back = jnp.sum(back.reshape(nx, part_rows + 8, width).astype(jnp.float32), axis=0)
-    back = back.astype(jnp.bfloat16)
-
-    grad_gate = contract(rows_x, grad_gate_pre, 0, 0).astype(jnp.bfloat16)[None]
-    grad_up = contract(rows_x, grad_up_pre, 0, 0).astype(jnp.bfloat16)[None]
-    grad_down = contract(hidden, rows_dy, 0, 0).astype(jnp.bfloat16)[None]
 
     data = back[:part_rows].reshape(experts * nz, CAP * chunks, LANES)
     marks = jnp.pad(

time: 160 us -> 132 us (0.82); the launches traced: 158 us -> 132 us
  blocking collectives: 97.8 us -> 29.3 us
  waiting for transfers between devices: 14.1 us -> 40.8 us
  starting transfers between devices: 11.6 us -> 28.9 us
  between operations: 14.4 us -> 1.08 us
  local copies, waits for them, and re-layouts: 5.21 us -> 14.6 us
  matrix products: 11.6 us -> 13.9 us
    all_to_all x3 -> x1, blocking collectives: 97.8 us -> 29.3 us  [exchange(): return lax.all_to_all(block, axes, split_axis=0, concat_axis=0, tiled=True)]
    ppermute x2 -> x5, waiting for transfers between devices: 1.15 us -> 24.3 us  [the longest x4 21.5 us: meet(): return lax.ppermute(block, 'x', [(i, i ^ mask) for i in range(nx)])]
    all_to_all x1, starting transfers between devices: 7.28 us -> 16.7 us  [exchange(): return lax.all_to_all(block, axes, split_axis=0, concat_axis=0, tiled=True)]
    ppermute x2 -> x5, starting transfers between devices: 4.33 us -> 12.2 us  [the longest x4 10.3 us: meet(): return lax.ppermute(block, 'x', [(i, i ^ mask) for i in range(nx)])]
    unnamed x21 -> x32, local copies, waits for them, and re-layouts: 1.34 us -> 6.66 us
    all_to_all x1, waiting for transfers between devices: 12.9 us -> 16.6 us  [exchange(): return lax.all_to_all(block, axes, split_axis=0, concat_axis=0, tiled=True)]
    split x0 -> x3, local copies, waits for them, and re-layouts: none -> 3.53 us  [the longest x2 2.26 us: unstacked(): jnp.split(down, width // hid, axis=0)]
    dot_general x11 -> x14, matrix products: 11.6 us -> 13.9 us  [contract(): lax.dot_general(left, right, (((left_dim,), (right_dim,)), ((), ())), pre...]
  transfers between devices with their start and end apart: 4 -> 6, of which waited for: 2 -> 4; matrix products, arithmetic and copies ran while one was open for 5% -> 11% of each run, Pallas kernels for 0% -> 0%
where the time goes in v3:
time: 132 us
  waiting for transfers between devices  40.8 us (31%)
  blocking collectives  29.3 us (22%)
  starting transfers between devices  28.9 us (22%)
  local copies, waits for them, and re-layouts  14.6 us (11%)
  matrix products  13.9 us (11%)
  other arithmetic  3.15 us (2%)
    all_to_all x1, blocking collectives, exchange(): return lax.all_to_all(block, axes, split_axis=0, concat_axis=0, tiled=True)  29.3 us
    ppermute x4, waiting for transfers between devices, meet(): return lax.ppermute(block, 'x', [(i, i ^ mask) for i in range(nx)])  21.5 us
    all_to_all x1, starting transfers between devices, exchange(): return lax.all_to_all(block, axes, split_axis=0, concat_axis=0, tiled=True)  16.7 us
    all_to_all x1, waiting for transfers between devices, exchange(): return lax.all_to_all(block, axes, split_axis=0, concat_axis=0, tiled=True)  16.6 us
    dot_general x14, matrix products, contract(): lax.dot_general(left, right, (((left_dim,), (right_dim,)), ((), ())), pre...  13.9 us
    ppermute x4, starting transfers between devices, meet(): return lax.ppermute(block, 'x', [(i, i ^ mask) for i in range(nx)])  10.3 us
    unnamed x32, local copies, waits for them, and re-layouts  6.66 us
    ppermute x1, waiting for transfers between devices, swap(): return lax.ppermute(block, 'dp', [(0, 1), (1, 0)])  2.81 us
  transfers between devices with their start and end apart: 6, of which 4 were waited for; matrix products, arithmetic and copies ran while one was open for 11% of the time, Pallas kernels for 0%

profile of v3, /device:TPU:6, one launch (start us, length us, event | category | flops | bytes accessed | tf_op | source)
XLA Modules:
  0.0 131.7 jit_solution(10838385205509084892)
XLA Ops:
  3.2 1.0 fusion.2
  4.2 1.0 broadcast_in_dim.72
  5.2 16.7 %all-to-all-start = ((bf16[64,48,128]{2,1,0:T(8,128)(2,1)}), bf16[64,48,128]{2,1,0:T(8,128)(2,1)S(1)}, u32[]{:S(2)}, u32[]{:S(2)}) async-start(bf16[64,48,128]{2,1,0:T(8,128)(2,1)} %bitcast.2), calls=%async_computation | async-start | bytes 1572864 | tf_op jit(solution)/shard_map/all_to_all | solution.py:18
  22.0 0.8 constant_dynamic-update-slice_fusion.3
  22.8 0.8 constant_dynamic-update-slice_fusion.2
  26.3 2.7 %collective-permute-start.1 = (bf16[3072,256]{1,0:T(8,128)(2,1)}, bf16[3072,256]{1,0:T(8,128)(2,1)}, u32[]{:S(2)}, u32[]{:S(2)}) collective-permute-start(bf16[3072,256]{1,0:T(8,128)(2,1)} %slice_dynamic-update-slice_fusion.4), channel_id=1, source_target_pairs={{0,16},{16,0},{32,48},{48,32},{1,17},{17,1},{33,49},{49,33},{2,18}... | collective-permute-start | bytes 4718600 | tf_op jit(solution)/shard_map/ppermute | solution.py:59
  29.0 16.6 %all-to-all-done = bf16[64,48,128]{2,1,0:T(8,128)(2,1)S(1)} async-done(((bf16[64,48,128]{2,1,0:T(8,128)(2,1)}), bf16[64,48,128]{2,1,0:T(8,128)(2,1)S(1)}, u32[]{:S(2)}, u32[]{:S(2)}) %all-to-all-start) | async-done | bytes 786464 | tf_op jit(solution)/shard_map/all_to_all | solution.py:18
  45.9 2.4 %collective-permute-start = (bf16[192,2048]{1,0:T(8,128)(2,1)S(1)}, bf16[192,2048]{1,0:T(8,128)(2,1)S(1)}, u32[]{:S(2)}, u32[]{:S(2)}) collective-permute-start(bf16[192,2048]{1,0:T(8,128)(2,1)S(1)} %reshape.48), channel_id=1, source_target_pairs={{0,48},{16,32},{32,16},{48,0},{1,49},{17,33},{33,17},{49,1},{2,50}... | collective-permute-start | bytes 2359304 | tf_op jit(solution)/shard_map/ppermute | solution.py:59
  48.3 16.0 %collective-permute-done.1 = bf16[3072,256]{1,0:T(8,128)(2,1)} collective-permute-done((bf16[3072,256]{1,0:T(8,128)(2,1)}, bf16[3072,256]{1,0:T(8,128)(2,1)}, u32[]{:S(2)}, u32[]{:S(2)}) %collective-permute-start.1) | collective-permute-done | bytes 1572896 | tf_op jit(solution)/shard_map/ppermute | solution.py:59
  64.4 1.1 fusion.67
  65.5 1.3 fusion.66
  68.8 1.9 %collective-permute-start.2 = (bf16[384,1536]{1,0:T(8,128)(2,1)S(1)}, bf16[384,1536]{1,0:T(8,128)(2,1)S(1)}, u32[]{:S(2)}, u32[]{:S(2)}) collective-permute-start(bf16[384,1536]{1,0:T(8,128)(2,1)S(1)} %pad_maximum_fusion), channel_id=1, source_target_pairs={{0,1},{1,0},{2,3},{3,2},{4,5},{5,4},{6,7},{7,6},{8,9},{9,8},{10,11... | collective-permute-start | bytes 3538952 | tf_op jit(solution)/shard_map/ppermute | solution.py:62
  70.7 2.8 %collective-permute-done.2 = bf16[384,1536]{1,0:T(8,128)(2,1)S(1)} collective-permute-done((bf16[384,1536]{1,0:T(8,128)(2,1)S(1)}, bf16[384,1536]{1,0:T(8,128)(2,1)S(1)}, u32[]{:S(2)}, u32[]{:S(2)}) %collective-permute-start.2) | collective-permute-done | bytes 1179680 | tf_op jit(solution)/shard_map/ppermute | solution.py:62
  75.6 1.3 fusion
  77.6 2.4 %collective-permute-start.3 = (bf16[200,1024]{1,0:T(8,128)(2,1)S(1)}, bf16[200,1024]{1,0:T(8,128)(2,1)S(1)}, u32[]{:S(2)}, u32[]{:S(2)}) collective-permute-start(bf16[200,1024]{1,0:T(8,128)(2,1)S(1)} %fusion.30), channel_id=1, source_target_pairs={{0,48},{16,32},{32,16},{48,0},{1,49},{17,33},{33,17},{49,1},{2,50}... | collective-permute-start | bytes 1228808 | tf_op jit(solution)/shard_map/ppermute | solution.py:59
  80.0 1.3 fusion.1
  84.0 2.8 %collective-permute-start.4 = (bf16[3072,256]{1,0:T(8,128)(2,1)}, bf16[3072,256]{1,0:T(8,128)(2,1)}, u32[]{:S(2)}, u32[]{:S(2)}) collective-permute-start(bf16[3072,256]{1,0:T(8,128)(2,1)} %slice_dynamic-update-slice_fusion), channel_id=1, source_target_pairs={{0,16},{16,0},{32,48},{48,32},{1,17},{17,1},{33,49},{49,33},{2,18}... | collective-permute-start | bytes 4718600 | tf_op jit(solution)/shard_map/ppermute | solution.py:59
  86.7 5.4 %collective-permute-done.3 = bf16[200,1024]{1,0:T(8,128)(2,1)S(1)} collective-permute-done((bf16[200,1024]{1,0:T(8,128)(2,1)S(1)}, bf16[200,1024]{1,0:T(8,128)(2,1)S(1)}, u32[]{:S(2)}, u32[]{:S(2)}) %collective-permute-start.3) | collective-permute-done | bytes 409632 | tf_op jit(solution)/shard_map/ppermute | solution.py:59
  93.3 29.3 %all_to_all.10 = bf16[64,13,2,128]{3,2,1,0:T(2,128)(2,1)S(1)} all-to-all(bf16[64,13,2,128]{3,2,1,0:T(2,128)(2,1)S(1)} %copy.28), channel_id=1, replica_groups=mesh['expert'=8,'x'=4,'z'=8,'dp'=2] {'expert','z'}, dimensions={0} | all-to-all | bytes 851968 | tf_op jit(solution)/shard_map/all_to_all | solution.py:18
  123.9 0.8 convolution_convert_fusion.7
  124.7 1.1 fusion.65
  125.9 1.3 fusion.23
  127.1 2.3 %fusion.27 = bf16[1,1024,256]{2,1,0:T(8,128)(2,1)} fusion(bf16[3072,256]{1,0:T(8,128)(2,1)} %collective-permute-done.4, bf16[384,2048]{1,0:T(8,128)(2,1)S(1)} %copy-done.5, bf16[384,512]{1,0:T(8,128)(2,1)S(1)} %get-tuple-element.16), kind=kOutput, calls=%fused_computation.49 | convolution fusion | flops 202113024 | bytes 2031616 | tf_op jit(solution)/shard_map/dot_general | solution.py:12
  129.4 2.3 %fusion.26 = bf16[1,1024,256]{2,1,0:T(8,128)(2,1)} fusion(bf16[3072,256]{1,0:T(8,128)(2,1)} %collective-permute-done.4, bf16[384,2048]{1,0:T(8,128)(2,1)S(1)} %copy-done.5, bf16[384,512]{1,0:T(8,128)(2,1)S(1)} %get-tuple-element.15), kind=kOutput, calls=%fused_computation.48 | convolution fusion | flops 202113024 | bytes 2031616 | tf_op jit(solution)/shard_map/dot_general | solution.py:12
  (79 shorter events, 15.2 us)
Async XLA Ops:
  0.6 2.0 %copy-start = (bf16[8,1024]{1,0:T(8,128)(2,1)S(1)}, bf16[8,1024]{1,0:T(8,128)(2,1)}, u32[]{:S(2)}) copy-start(bf16[8,1024]{1,0:T(8,128)(2,1)} %param.7) | copy-start | bytes 49156
  2.6 0.5 copy-start.6
  2.7 0.5 copy-start.8
  2.7 19.3 %copy-start.2 = (bf16[1,1024,256]{2,1,0:T(8,128)(2,1)S(1)}, bf16[1,1024,256]{2,1,0:T(8,128)(2,1)}, u32[]{:S(2)}) copy-start(bf16[1,1024,256]{2,1,0:T(8,128)(2,1)} %param.11) | copy-start | bytes 1572868
  4.2 18.6 %copy-start.1 = (bf16[1,1024,256]{2,1,0:T(8,128)(2,1)S(1)}, bf16[1,1024,256]{2,1,0:T(8,128)(2,1)}, u32[]{:S(2)}) copy-start(bf16[1,1024,256]{2,1,0:T(8,128)(2,1)} %param.12) | copy-start | bytes 1572868
  5.2 18.4 %copy-start.3 = (bf16[1,256,1024]{2,1,0:T(8,128)(2,1)S(1)}, bf16[1,256,1024]{2,1,0:T(8,128)(2,1)}, u32[]{:S(2)}) copy-start(bf16[1,256,1024]{2,1,0:T(8,128)(2,1)} %param.13) | copy-start | bytes 1572868
  5.2 40.4 %all-to-all-start = ((bf16[64,48,128]{2,1,0:T(8,128)(2,1)}), bf16[64,48,128]{2,1,0:T(8,128)(2,1)S(1)}, u32[]{:S(2)}, u32[]{:S(2)}) async-start(bf16[64,48,128]{2,1,0:T(8,128)(2,1)} %bitcast.2), calls=%async_computation | async-start | bytes 1572864 | tf_op jit(solution)/shard_map/all_to_all | solution.py:18
  26.3 38.1 %collective-permute-start.1 = (bf16[3072,256]{1,0:T(8,128)(2,1)}, bf16[3072,256]{1,0:T(8,128)(2,1)}, u32[]{:S(2)}, u32[]{:S(2)}) collective-permute-start(bf16[3072,256]{1,0:T(8,128)(2,1)} %slice_dynamic-update-slice_fusion.4), channel_id=1, source_target_pairs={{0,16},{16,0},{32,48},{48,32},{1,17},{17,1},{33,49},{49,33},{2,18}... | collective-permute-start | bytes 4718600 | tf_op jit(solution)/shard_map/ppermute | solution.py:59
  45.9 20.8 %collective-permute-start = (bf16[192,2048]{1,0:T(8,128)(2,1)S(1)}, bf16[192,2048]{1,0:T(8,128)(2,1)S(1)}, u32[]{:S(2)}, u32[]{:S(2)}) collective-permute-start(bf16[192,2048]{1,0:T(8,128)(2,1)S(1)} %reshape.48), channel_id=1, source_target_pairs={{0,48},{16,32},{32,16},{48,0},{1,49},{17,33},{33,17},{49,1},{2,50}... | collective-permute-start | bytes 2359304 | tf_op jit(solution)/shard_map/ppermute | solution.py:59
  66.9 13.1 %copy-start.4 = (bf16[384,2048]{1,0:T(8,128)(2,1)}, bf16[384,2048]{1,0:T(8,128)(2,1)S(1)}, u32[]{:S(2)}) copy-start(bf16[384,2048]{1,0:T(8,128)(2,1)S(1)} %constant_dynamic-update-slice_fusion) | copy-start | bytes 4718596
  68.8 4.7 %collective-permute-start.2 = (bf16[384,1536]{1,0:T(8,128)(2,1)S(1)}, bf16[384,1536]{1,0:T(8,128)(2,1)S(1)}, u32[]{:S(2)}, u32[]{:S(2)}) collective-permute-start(bf16[384,1536]{1,0:T(8,128)(2,1)S(1)} %pad_maximum_fusion), channel_id=1, source_target_pairs={{0,1},{1,0},{2,3},{3,2},{4,5},{5,4},{6,7},{7,6},{8,9},{9,8},{10,11... | collective-permute-start | bytes 3538952 | tf_op jit(solution)/shard_map/ppermute | solution.py:62
  77.6 14.6 %collective-permute-start.3 = (bf16[200,1024]{1,0:T(8,128)(2,1)S(1)}, bf16[200,1024]{1,0:T(8,128)(2,1)S(1)}, u32[]{:S(2)}, u32[]{:S(2)}) collective-permute-start(bf16[200,1024]{1,0:T(8,128)(2,1)S(1)} %fusion.30), channel_id=1, source_target_pairs={{0,48},{16,32},{32,16},{48,0},{1,49},{17,33},{33,17},{49,1},{2,50}... | collective-permute-start | bytes 1228808 | tf_op jit(solution)/shard_map/ppermute | solution.py:59
  84.0 40.8 %collective-permute-start.4 = (bf16[3072,256]{1,0:T(8,128)(2,1)}, bf16[3072,256]{1,0:T(8,128)(2,1)}, u32[]{:S(2)}, u32[]{:S(2)}) collective-permute-start(bf16[3072,256]{1,0:T(8,128)(2,1)} %slice_dynamic-update-slice_fusion), channel_id=1, source_target_pairs={{0,16},{16,0},{32,48},{48,32},{1,17},{17,1},{33,49},{49,33},{2,18}... | collective-permute-start | bytes 4718600 | tf_op jit(solution)/shard_map/ppermute | solution.py:59
  92.8 30.3 %copy-start.7 = (s32[8]{0:T(128)S(1)}, s32[8]{0:T(128)}, u32[]{:S(2)}) copy-start(s32[8]{0:T(128)} %copy-done.6) | copy-start | bytes 100
  92.8 30.3 %copy-start.9 = (s32[8]{0:T(128)S(1)}, s32[8]{0:T(128)}, u32[]{:S(2)}) copy-start(s32[8]{0:T(128)} %copy-done.8) | copy-start | bytes 100
  92.9 30.5 %copy-start.10 = (f32[8,2]{0,1:T(2,128)S(1)}, f32[8,2]{0,1:T(2,128)}, u32[]{:S(2)}) copy-start(f32[8,2]{0,1:T(2,128)} %param.10) | copy-start | bytes 196
  122.6 3.2 %copy-start.5 = (bf16[384,2048]{1,0:T(8,128)(2,1)S(1)}, bf16[384,2048]{1,0:T(8,128)(2,1)}, u32[]{:S(2)}) copy-start(bf16[384,2048]{1,0:T(8,128)(2,1)} %copy-done.4) | copy-start | bytes 4718596

commit v4 on v3

--- a/solution.py
+++ b/solution.py
@@ -1,6 +1,8 @@
 import jax
 import jax.numpy as jnp
 from jax import lax
+from jax.experimental import pallas as pl
+from jax.experimental.pallas import tpu as pltpu
 from jax.sharding import Mesh
 from jax.sharding import PartitionSpec as P
 
@@ -16,6 +18,54 @@
 
 def exchange(block, axes):
     return lax.all_to_all(block, axes, split_axis=0, concat_axis=0, tiled=True)
+
+
+def dispatch_kernel(ids_ref, probs_ref, tokens_ref, out_grad_ref, send_ref, position_ref, stage_ref):
+    experts, nz = send_ref.shape[0], send_ref.shape[1]
+    toks, width = tokens_ref.shape
+    chunks = width // LANES
+    ids = [ids_ref[k : k + 1, :] for k in range(2)]
+    probs = [probs_ref[k : k + 1, :].astype(jnp.bfloat16).astype(jnp.float32) for k in range(2)]
+    a = lax.broadcasted_iota(jnp.int32, (toks, toks), 0)
+    b = lax.broadcasted_iota(jnp.int32, (toks, toks), 1)
+    columns = [
+        jnp.sum(jnp.where(a == b, jnp.broadcast_to(i, (toks, toks)), 0), axis=1, keepdims=True)
+        for i in ids
+    ]
+    places = []
+    for k in range(2):
+        rank = jnp.zeros((1, toks), jnp.int32)
+        for other in range(2):
+            earlier = (a < b) if other >= k else (a <= b)
+            match = (columns[other] == ids[k]) & earlier
+            rank = rank + jnp.sum(match.astype(jnp.int32), axis=0, keepdims=True)
+        position_ref[k : k + 1, :] = ids[k] * CAP + rank
+        places.append((ids[k], rank))
+    names = lax.broadcasted_iota(jnp.int32, (experts, toks), 0)
+    x = tokens_ref[...].astype(jnp.float32)
+    dy = out_grad_ref[...].astype(jnp.float32)
+    for slot in range(CAP):
+        masks = [(names == i) & (rank == slot) for i, rank in places]
+        hit = (masks[0] | masks[1]).astype(jnp.float32)
+        weight = jnp.sum(
+            jnp.where(masks[0], probs[0], 0.0) + jnp.where(masks[1], probs[1], 0.0),
+            axis=1,
+            keepdims=True,
+        )
+        rows_x = jnp.zeros((experts, width), jnp.float32)
+        rows_dy = jnp.zeros((experts, width), jnp.float32)
+        for t in range(toks):
+            rows_x = rows_x + hit[:, t : t + 1] * x[t : t + 1, :]
+            rows_dy = rows_dy + hit[:, t : t + 1] * dy[t : t + 1, :]
+        rows_dy = rows_dy * weight
+        for c in range(chunks):
+            lanes = slice(c * LANES, (c + 1) * LANES)
+            stage_ref[:, slot * 2 * chunks + c, :] = rows_x[:, lanes]
+            stage_ref[:, slot * 2 * chunks + chunks + c, :] = rows_dy[:, lanes]
+    for e in range(experts):
+        block = stage_ref[e].astype(jnp.bfloat16)
+        for z in range(nz):
+            send_ref[e, z] = block
 
 
 def per_device(tokens, out_grad, expert_ids, gate_probs, w_gate, w_up, w_down):
@@ -26,29 +76,26 @@
     chunks = width // LANES
     slots = experts * CAP
 
-    flat_ids = expert_ids.reshape(-1)
-    onehot = (flat_ids[:, None] == jnp.arange(experts, dtype=jnp.int32)[None, :]).astype(jnp.int32)
-    earlier = jnp.tril(jnp.ones((2 * tok_rows, 2 * tok_rows), jnp.int32), -1)
-    same = (flat_ids[:, None] == flat_ids[None, :]).astype(jnp.int32)
-    ranks = jnp.sum(same * earlier, axis=1)
-    position = (flat_ids * CAP + ranks).reshape(tok_rows, 2)
+    probs = gate_probs.astype(jnp.bfloat16).astype(jnp.float32)
+    rows_out = CAP * 2 * chunks
+    send, position = pl.pallas_call(
+        dispatch_kernel,
+        out_shape=(
+            jax.ShapeDtypeStruct((experts, nz, rows_out, LANES), jnp.bfloat16),
+            jax.ShapeDtypeStruct((2, tok_rows), jnp.int32),
+        ),
+        in_specs=[pl.BlockSpec(memory_space=pltpu.VMEM)] * 4,
+        out_specs=(
+            pl.BlockSpec(memory_space=pltpu.VMEM),
+            pl.BlockSpec(memory_space=pltpu.VMEM),
+        ),
+        scratch_shapes=[pltpu.VMEM((experts, rows_out, LANES), jnp.float32)],
+    )(expert_ids.T, gate_probs.T, tokens, out_grad)
+    send = send.reshape(experts * nz, rows_out, LANES)
     slot_names = jnp.arange(slots, dtype=jnp.int32)
-    place0 = slot_names[:, None] == position[None, :, 0]
-    place1 = slot_names[:, None] == position[None, :, 1]
+    place0 = slot_names[:, None] == position[0][None, :]
+    place1 = slot_names[:, None] == position[1][None, :]
     placing = (place0 | place1).astype(jnp.bfloat16)
-    probs = gate_probs.astype(jnp.bfloat16).astype(jnp.float32)
-    slot_prob = jnp.sum(
-        jnp.where(place0, probs[None, :, 0], 0.0) + jnp.where(place1, probs[None, :, 1], 0.0),
-        axis=1,
-        keepdims=True,
-    )
-    send_x = contract(placing, tokens, 1, 0).astype(jnp.bfloat16)
-    send_dy = (contract(placing, out_grad, 1, 0) * slot_prob).astype(jnp.bfloat16)
-    send = jnp.concatenate([send_x, send_dy], axis=1)
-    send = send.reshape(experts, 1, CAP * 2 * chunks, LANES)
-    send = jnp.broadcast_to(send, (experts, nz, CAP * 2 * chunks, LANES))
-    send = send.reshape(experts * nz, CAP * 2 * chunks, LANES)
-
     part_rows = experts * nz * CAP
     gate_w = w_gate[0]
     up_w = w_up[0]
@@ -124,10 +171,11 @@
         )
 
     theirs = [g.astype(jnp.bfloat16) for g in weight_grads(slice(hid, None))]
-    theirs = unstacked(meet(stacked(*theirs), 1))
+    theirs = meet(stacked(*theirs), 1)
+    mine = lax.optimization_barrier(weight_grads(slice(0, hid)))
     grad_gate, grad_up, grad_down = (
-        (mine + other.astype(jnp.float32)).astype(jnp.bfloat16)[None]
-        for mine, other in zip(weight_grads(slice(0, hid)), theirs)
+        (own_part + other.astype(jnp.float32)).astype(jnp.bfloat16)[None]
+        for own_part, other in zip(mine, unstacked(theirs))
     )
 
     data = back[:part_rows].reshape(experts * nz, CAP * chunks, LANES)

time: 132 us -> 130 us (0.985)
  blocking collectives: 29.3 us -> 0 us
  starting transfers between devices: 28.9 us -> 41.6 us
  waiting for transfers between devices: 40.8 us -> 53 us
  matrix products: 13.9 us -> 11.1 us
  other arithmetic: 3.15 us -> 5.53 us
  Pallas kernels: 0 us -> 2.19 us
    all_to_all x1 -> x0, blocking collectives: 29.3 us -> none  [exchange(): return lax.all_to_all(block, axes, split_axis=0, concat_axis=0, tiled=True)]
    all_to_all x1 -> x2, starting transfers between devices: 16.7 us -> 29.4 us  [exchange(): return lax.all_to_all(block, axes, split_axis=0, concat_axis=0, tiled=True)]
    all_to_all x1 -> x2, waiting for transfers between devices: 16.6 us -> 29.1 us  [exchange(): return lax.all_to_all(block, axes, split_axis=0, concat_axis=0, tiled=True)]
    broadcast_in_dim x0 -> x2, other arithmetic: none -> 3.36 us  [per_device(): (own_part + other.astype(jnp.float32)).astype(jnp.bfloat16)[None]]
    dot_general x14 -> x12, matrix products: 13.9 us -> 11.1 us  [contract(): lax.dot_general(left, right, (((left_dim,), (right_dim,)), ((), ())), pre...]
    pallas_call x0 -> x1, Pallas kernels: none -> 2.19 us  [per_device(): pl.pallas_call(dispatch_kernel, out_shape=(jax.ShapeDtypeStruct((experts,...]
    unnamed x32 -> x31, local copies, waits for them, and re-layouts: 6.66 us -> 6.71 us
  transfers between devices with their start and end apart: 6 -> 7, of which waited for: 4 -> 5; matrix products, arithmetic and copies ran while one was open for 11% -> 16% of each run, Pallas kernels for 0% -> 0%
where the time goes in v4:
time: 130 us; the launch traced here: 129 us
  waiting for transfers between devices  53 us (41%)
  starting transfers between devices  41.6 us (32%)
  local copies, waits for them, and re-layouts  15.1 us (12%)
  matrix products  11.1 us (9%)
  other arithmetic  5.53 us (4%)
  Pallas kernels  2.19 us (2%)
    all_to_all x2, starting transfers between devices, exchange(): return lax.all_to_all(block, axes, split_axis=0, concat_axis=0, tiled=True)  29.4 us
    all_to_all x2, waiting for transfers between devices, exchange(): return lax.all_to_all(block, axes, split_axis=0, concat_axis=0, tiled=True)  29.1 us
    ppermute x4, waiting for transfers between devices, meet(): return lax.ppermute(block, 'x', [(i, i ^ mask) for i in range(nx)])  21 us
    dot_general x12, matrix products, contract(): lax.dot_general(left, right, (((left_dim,), (right_dim,)), ((), ())), pre...  11.1 us
    ppermute x4, starting transfers between devices, meet(): return lax.ppermute(block, 'x', [(i, i ^ mask) for i in range(nx)])  10.3 us
    unnamed x31, local copies, waits for them, and re-layouts  6.71 us
    broadcast_in_dim x2, other arithmetic, per_device(): (own_part + other.astype(jnp.float32)).astype(jnp.bfloat16)[None]  3.36 us
    ppermute x1, waiting for transfers between devices, swap(): return lax.ppermute(block, 'dp', [(0, 1), (1, 0)])  2.81 us
  transfers between devices with their start and end apart: 7, of which 5 were waited for; matrix products, arithmetic and copies ran while one was open for 16% of the time, Pallas kernels for 0%

profile of v4, /device:TPU:6, one launch (start us, length us, event | category | flops | bytes accessed | tf_op | source)
XLA Modules:
  0.0 129.5 jit_solution(307947364605318084)
XLA Ops:
  0.7 2.2 %shard_map.110 = (bf16[8,8,48,128]{3,2,1,0:T(8,128)(2,1)}, s32[2,8]{1,0:T(2,128)}) custom-call(s32[2,8]{1,0:T(2,128)} %bitcast.43, f32[2,8]{1,0:T(2,128)} %bitcast.40, bf16[8,1024]{1,0:T(8,128)(2,1)} %tokens_ref.1, bf16[8,1024]{1,0:T(8,128)(2,1)} %out_grad_ref.1), custom_call_target="tpu_custom_call" | custom-call | tf_op jit(solution)/shard_map/pallas_call | solution.py:81
  2.9 16.7 %all-to-all-start = ((bf16[64,48,128]{2,1,0:T(8,128)(2,1)}), bf16[64,48,128]{2,1,0:T(8,128)(2,1)S(1)}, u32[]{:S(2)}, u32[]{:S(2)}) async-start(bf16[64,48,128]{2,1,0:T(8,128)(2,1)} %bitcast.34), calls=%async_computation | async-start | bytes 1572864 | tf_op jit(solution)/shard_map/all_to_all | solution.py:20
  23.9 2.7 %collective-permute-start.1 = (bf16[3072,256]{1,0:T(8,128)(2,1)}, bf16[3072,256]{1,0:T(8,128)(2,1)}, u32[]{:S(2)}, u32[]{:S(2)}) collective-permute-start(bf16[3072,256]{1,0:T(8,128)(2,1)} %slice_dynamic-update-slice_fusion.4), channel_id=1, source_target_pairs={{0,16},{16,0},{32,48},{48,32},{1,17},{17,1},{33,49},{49,33},{2,18}... | collective-permute-start | bytes 4718600 | tf_op jit(solution)/shard_map/ppermute | solution.py:106
  26.7 16.6 %all-to-all-done = bf16[64,48,128]{2,1,0:T(8,128)(2,1)S(1)} async-done(((bf16[64,48,128]{2,1,0:T(8,128)(2,1)}), bf16[64,48,128]{2,1,0:T(8,128)(2,1)S(1)}, u32[]{:S(2)}, u32[]{:S(2)}) %all-to-all-start) | async-done | bytes 786464 | tf_op jit(solution)/shard_map/all_to_all | solution.py:20
  43.6 2.4 %collective-permute-start = (bf16[192,2048]{1,0:T(8,128)(2,1)S(1)}, bf16[192,2048]{1,0:T(8,128)(2,1)S(1)}, u32[]{:S(2)}, u32[]{:S(2)}) collective-permute-start(bf16[192,2048]{1,0:T(8,128)(2,1)S(1)} %reshape.36), channel_id=1, source_target_pairs={{0,48},{16,32},{32,16},{48,0},{1,49},{17,33},{33,17},{49,1},{2,50}... | collective-permute-start | bytes 2359304 | tf_op jit(solution)/shard_map/ppermute | solution.py:106
  46.0 16.0 %collective-permute-done.1 = bf16[3072,256]{1,0:T(8,128)(2,1)} collective-permute-done((bf16[3072,256]{1,0:T(8,128)(2,1)}, bf16[3072,256]{1,0:T(8,128)(2,1)}, u32[]{:S(2)}, u32[]{:S(2)}) %collective-permute-start.1) | collective-permute-done | bytes 1572896 | tf_op jit(solution)/shard_map/ppermute | solution.py:106
  62.0 1.1 fusion.52
  63.1 1.3 fusion.51
  66.9 1.9 %collective-permute-start.2 = (bf16[384,1536]{1,0:T(8,128)(2,1)S(1)}, bf16[384,1536]{1,0:T(8,128)(2,1)S(1)}, u32[]{:S(2)}, u32[]{:S(2)}) collective-permute-start(bf16[384,1536]{1,0:T(8,128)(2,1)S(1)} %pad_maximum_fusion), channel_id=1, source_target_pairs={{0,1},{1,0},{2,3},{3,2},{4,5},{5,4},{6,7},{7,6},{8,9},{9,8},{10,11... | collective-permute-start | bytes 3538952 | tf_op jit(solution)/shard_map/ppermute | solution.py:109
  68.8 2.8 %collective-permute-done.2 = bf16[384,1536]{1,0:T(8,128)(2,1)S(1)} collective-permute-done((bf16[384,1536]{1,0:T(8,128)(2,1)S(1)}, bf16[384,1536]{1,0:T(8,128)(2,1)S(1)}, u32[]{:S(2)}, u32[]{:S(2)}) %collective-permute-start.2) | collective-permute-done | bytes 1179680 | tf_op jit(solution)/shard_map/ppermute | solution.py:109
  73.6 1.3 fusion
  75.7 2.4 %collective-permute-start.3 = (bf16[200,1024]{1,0:T(8,128)(2,1)S(1)}, bf16[200,1024]{1,0:T(8,128)(2,1)S(1)}, u32[]{:S(2)}, u32[]{:S(2)}) collective-permute-start(bf16[200,1024]{1,0:T(8,128)(2,1)S(1)} %fusion.25), channel_id=1, source_target_pairs={{0,48},{16,32},{32,16},{48,0},{1,49},{17,33},{33,17},{49,1},{2,50}... | collective-permute-start | bytes 1228808 | tf_op jit(solution)/shard_map/ppermute | solution.py:106
  78.1 1.3 fusion.1
  82.5 2.8 %collective-permute-start.4 = (bf16[3072,256]{1,0:T(8,128)(2,1)}, bf16[3072,256]{1,0:T(8,128)(2,1)}, u32[]{:S(2)}, u32[]{:S(2)}) collective-permute-start(bf16[3072,256]{1,0:T(8,128)(2,1)} %slice_dynamic-update-slice_fusion), channel_id=1, source_target_pairs={{0,16},{16,0},{32,48},{48,32},{1,17},{17,1},{33,49},{49,33},{2,18}... | collective-permute-start | bytes 4718600 | tf_op jit(solution)/shard_map/ppermute | solution.py:106
  85.3 5.0 %collective-permute-done.3 = bf16[200,1024]{1,0:T(8,128)(2,1)S(1)} collective-permute-done((bf16[200,1024]{1,0:T(8,128)(2,1)S(1)}, bf16[200,1024]{1,0:T(8,128)(2,1)S(1)}, u32[]{:S(2)}, u32[]{:S(2)}) %collective-permute-start.3) | collective-permute-done | bytes 409632 | tf_op jit(solution)/shard_map/ppermute | solution.py:106
  91.0 1.2 copy.20
  92.2 12.6 %all-to-all-start.1 = ((bf16[64,13,2,128]{3,2,1,0:T(2,128)(2,1)}), bf16[64,13,2,128]{3,2,1,0:T(2,128)(2,1)}, u32[]{:S(2)}, u32[]{:S(2)}) async-start(bf16[64,13,2,128]{3,2,1,0:T(2,128)(2,1)} %copy.20), calls=%async_computation.1 | async-start | bytes 851968 | tf_op jit(solution)/shard_map/all_to_all | solution.py:20
  104.9 1.4 %fusion.17 = f32[256,1024]{1,0:T(8,128)S(1)} fusion(bf16[384,2048]{1,0:T(8,128)(2,1)S(1)} %constant_dynamic-update-slice_fusion, bf16[384,512]{1,0:T(8,128)(2,1)} %copy-done.6), kind=kOutput, calls=%fused_computation.41 | convolution fusion | flops 201326592 | bytes 2031616 | tf_op jit(solution)/shard_map/dot_general | solution.py:14
  106.2 1.5 %fusion.28 = f32[1024,256]{1,0:T(8,128)} fusion(bf16[384,2048]{1,0:T(8,128)(2,1)S(1)} %constant_dynamic-update-slice_fusion, bf16[384,512]{1,0:T(8,128)(2,1)S(1)} %get-tuple-element.24), kind=kOutput, calls=%fused_computation.52 | convolution fusion | flops 201326592 | bytes 2031616 | tf_op jit(solution)/shard_map/dot_general | solution.py:14
  107.7 1.5 %fusion.30 = f32[1024,256]{1,0:T(8,128)} fusion(bf16[384,2048]{1,0:T(8,128)(2,1)S(1)} %constant_dynamic-update-slice_fusion, bf16[384,512]{1,0:T(8,128)(2,1)S(1)} %get-tuple-element.23), kind=kOutput, calls=%fused_computation.54 | convolution fusion | flops 201326592 | bytes 2031616 | tf_op jit(solution)/shard_map/dot_general | solution.py:14
  109.2 12.6 %all-to-all-done.1 = bf16[64,13,2,128]{3,2,1,0:T(2,128)(2,1)} async-done(((bf16[64,13,2,128]{3,2,1,0:T(2,128)(2,1)}), bf16[64,13,2,128]{3,2,1,0:T(2,128)(2,1)}, u32[]{:S(2)}, u32[]{:S(2)}) %all-to-all-start.1) | async-done | bytes 426016 | tf_op jit(solution)/shard_map/all_to_all | solution.py:20
  121.8 1.1 copy.21
  124.8 1.3 fusion.50
  127.1 2.4 %fusion.21 = (bf16[1,1024,256]{2,1,0:T(8,128)(2,1)}, bf16[1,1024,256]{2,1,0:T(8,128)(2,1)}) fusion(f32[1024,256]{1,0:T(8,128)S(1)} %copy-done, bf16[3072,256]{1,0:T(8,128)(2,1)} %collective-permute-done.4, f32[1024,256]{1,0:T(8,128)S(1)} %copy-done.1), kind=kLoop, calls=%fused_computation.45 | loop fusion | flops 1572864 | bytes 4194304 | tf_op jit(solution)/shard_map/broadcast_in_dim | solution.py:177
  (69 shorter events, 16.5 us)
Async XLA Ops:
  0.6 18.9 %copy-start.4 = (bf16[1,1024,256]{2,1,0:T(8,128)(2,1)S(1)}, bf16[1,1024,256]{2,1,0:T(8,128)(2,1)}, u32[]{:S(2)}) copy-start(bf16[1,1024,256]{2,1,0:T(8,128)(2,1)} %param.11) | copy-start | bytes 1572868
  0.6 19.8 %copy-start.2 = (bf16[1,1024,256]{2,1,0:T(8,128)(2,1)S(1)}, bf16[1,1024,256]{2,1,0:T(8,128)(2,1)}, u32[]{:S(2)}) copy-start(bf16[1,1024,256]{2,1,0:T(8,128)(2,1)} %param.12) | copy-start | bytes 1572868
  2.8 18.4 %copy-start.7 = (bf16[1,256,1024]{2,1,0:T(8,128)(2,1)S(1)}, bf16[1,256,1024]{2,1,0:T(8,128)(2,1)}, u32[]{:S(2)}) copy-start(bf16[1,256,1024]{2,1,0:T(8,128)(2,1)} %param.13) | copy-start | bytes 1572868
  2.9 40.4 %all-to-all-start = ((bf16[64,48,128]{2,1,0:T(8,128)(2,1)}), bf16[64,48,128]{2,1,0:T(8,128)(2,1)S(1)}, u32[]{:S(2)}, u32[]{:S(2)}) async-start(bf16[64,48,128]{2,1,0:T(8,128)(2,1)} %bitcast.34), calls=%async_computation | async-start | bytes 1572864 | tf_op jit(solution)/shard_map/all_to_all | solution.py:20
  23.9 38.1 %collective-permute-start.1 = (bf16[3072,256]{1,0:T(8,128)(2,1)}, bf16[3072,256]{1,0:T(8,128)(2,1)}, u32[]{:S(2)}, u32[]{:S(2)}) collective-permute-start(bf16[3072,256]{1,0:T(8,128)(2,1)} %slice_dynamic-update-slice_fusion.4), channel_id=1, source_target_pairs={{0,16},{16,0},{32,48},{48,32},{1,17},{17,1},{33,49},{49,33},{2,18}... | collective-permute-start | bytes 4718600 | tf_op jit(solution)/shard_map/ppermute | solution.py:106
  43.6 20.8 %collective-permute-start = (bf16[192,2048]{1,0:T(8,128)(2,1)S(1)}, bf16[192,2048]{1,0:T(8,128)(2,1)S(1)}, u32[]{:S(2)}, u32[]{:S(2)}) collective-permute-start(bf16[192,2048]{1,0:T(8,128)(2,1)S(1)} %reshape.36), channel_id=1, source_target_pairs={{0,48},{16,32},{32,16},{48,0},{1,49},{17,33},{33,17},{49,1},{2,50}... | collective-permute-start | bytes 2359304 | tf_op jit(solution)/shard_map/ppermute | solution.py:106
  65.1 1.0 copy-start.8
  66.9 4.7 %collective-permute-start.2 = (bf16[384,1536]{1,0:T(8,128)(2,1)S(1)}, bf16[384,1536]{1,0:T(8,128)(2,1)S(1)}, u32[]{:S(2)}, u32[]{:S(2)}) collective-permute-start(bf16[384,1536]{1,0:T(8,128)(2,1)S(1)} %pad_maximum_fusion), channel_id=1, source_target_pairs={{0,1},{1,0},{2,3},{3,2},{4,5},{5,4},{6,7},{7,6},{8,9},{9,8},{10,11... | collective-permute-start | bytes 3538952 | tf_op jit(solution)/shard_map/ppermute | solution.py:109
  72.0 1.0 copy-start.3
  72.5 6.9 %copy-start.6 = (bf16[384,512]{1,0:T(8,128)(2,1)}, bf16[384,512]{1,0:T(8,128)(2,1)S(1)}, u32[]{:S(2)}) copy-start(bf16[384,512]{1,0:T(8,128)(2,1)S(1)} %get-tuple-element.22) | copy-start | bytes 1179652
  73.6 1.3 %copy-start.5 = (bf16[1,1024,256]{2,1,0:T(8,128)(2,1)S(1)}, bf16[1,1024,256]{2,1,0:T(8,128)(2,1)}, u32[]{:S(2)}) copy-start(bf16[1,1024,256]{2,1,0:T(8,128)(2,1)} %param.11) | copy-start | bytes 1572868
  75.7 14.6 %collective-permute-start.3 = (bf16[200,1024]{1,0:T(8,128)(2,1)S(1)}, bf16[200,1024]{1,0:T(8,128)(2,1)S(1)}, u32[]{:S(2)}, u32[]{:S(2)}) collective-permute-start(bf16[200,1024]{1,0:T(8,128)(2,1)S(1)} %fusion.25), channel_id=1, source_target_pairs={{0,48},{16,32},{32,16},{48,0},{1,49},{17,33},{33,17},{49,1},{2,50}... | collective-permute-start | bytes 1228808 | tf_op jit(solution)/shard_map/ppermute | solution.py:106
  82.5 42.3 %collective-permute-start.4 = (bf16[3072,256]{1,0:T(8,128)(2,1)}, bf16[3072,256]{1,0:T(8,128)(2,1)}, u32[]{:S(2)}, u32[]{:S(2)}) collective-permute-start(bf16[3072,256]{1,0:T(8,128)(2,1)} %slice_dynamic-update-slice_fusion), channel_id=1, source_target_pairs={{0,16},{16,0},{32,48},{48,32},{1,17},{17,1},{33,49},{49,33},{2,18}... | collective-permute-start | bytes 4718600 | tf_op jit(solution)/shard_map/ppermute | solution.py:106
  90.7 14.2 %copy-start.10 = (s32[2,8]{1,0:T(2,128)S(1)}, s32[2,8]{1,0:T(2,128)}, u32[]{:S(2)}) copy-start(s32[2,8]{1,0:T(2,128)} %get-tuple-element.12) | copy-start | bytes 196
  92.2 29.6 %all-to-all-start.1 = ((bf16[64,13,2,128]{3,2,1,0:T(2,128)(2,1)}), bf16[64,13,2,128]{3,2,1,0:T(2,128)(2,1)}, u32[]{:S(2)}, u32[]{:S(2)}) async-start(bf16[64,13,2,128]{3,2,1,0:T(2,128)(2,1)} %copy.20), calls=%async_computation.1 | async-start | bytes 851968 | tf_op jit(solution)/shard_map/all_to_all | solution.py:20
  107.7 15.8 %copy-start.9 = (f32[8,2]{0,1:T(2,128)S(1)}, f32[8,2]{0,1:T(2,128)}, u32[]{:S(2)}) copy-start(f32[8,2]{0,1:T(2,128)} %param.10) | copy-start | bytes 196
  124.8 2.2 %copy-start = (f32[1024,256]{1,0:T(8,128)S(1)}, f32[1024,256]{1,0:T(8,128)}, u32[]{:S(2)}) copy-start(f32[1024,256]{1,0:T(8,128)} %fusion.28) | copy-start | bytes 3145732
  124.8 2.2 %copy-start.1 = (f32[1024,256]{1,0:T(8,128)S(1)}, f32[1024,256]{1,0:T(8,128)}, u32[]{:S(2)}) copy-start(f32[1024,256]{1,0:T(8,128)} %fusion.30) | copy-start | bytes 3145732

commit v5 on v4

--- a/solution.py
+++ b/solution.py
@@ -1,3 +1,5 @@
+import functools
+
 import jax
 import jax.numpy as jnp
 from jax import lax
@@ -68,6 +70,117 @@
             send_ref[e, z] = block
 
 
+def project_kernel(guest_ref, own_ref, gate_ref, up_ref, down_ref, stack_ref, partial_ref):
+    width, hid = gate_ref.shape
+    half = own_ref.shape[0]
+    for h, rows_ref in enumerate((guest_ref, own_ref)):
+        rows = slice(h * half, (h + 1) * half)
+        x = rows_ref[:, :width]
+        parts = [
+            contract(x, gate_ref[...], 1, 0),
+            contract(x, stack_ref[:width, :], 1, 0),
+            contract(x, up_ref[...], 1, 0),
+            contract(x, stack_ref[width : 2 * width, :], 1, 0),
+            contract(rows_ref[:, width:], down_ref[...], 1, 1),
+        ]
+        total = None
+        for k in range(width // hid):
+            piece = contract(
+                rows_ref[:, width + k * hid : width + (k + 1) * hid],
+                stack_ref[2 * width + k * hid : 2 * width + (k + 1) * hid, :],
+                1,
+                1,
+            )
+            total = piece if total is None else total + piece
+        parts.append(total)
+        for k, part in enumerate(parts):
+            partial_ref[rows, k * hid : (k + 1) * hid] = part.astype(jnp.bfloat16)
+
+
+def pullback_kernel(
+    partial_ref, other_ref, gate_ref, up_ref, stack_ref,
+    pack_guest_ref, pack_own_ref, hidden_ref, gate_pre_ref, up_pre_ref, score_ref,
+):
+    width, hid = gate_ref.shape
+    both = 2 * hid
+    half = partial_ref.shape[0] // 2
+    step = 16
+
+    def one(i, carry):
+        rows = pl.ds(pl.multiple_of(i * step, step), step)
+        total = partial_ref[rows, :].astype(jnp.float32) + other_ref[rows, :].astype(jnp.float32)
+        gate_pre, up_pre, d_hidden = total[:, :both], total[:, both : 2 * both], total[:, 2 * both :]
+        sigmoid_gate = jax.nn.sigmoid(gate_pre)
+        silu_gate = gate_pre * sigmoid_gate
+        hidden = (silu_gate * up_pre).astype(jnp.bfloat16)
+        score = jnp.sum(d_hidden * hidden.astype(jnp.float32), axis=1, keepdims=True)
+        hidden_ref[rows, :] = hidden
+        gate_pre_ref[rows, :] = (
+            d_hidden * up_pre * sigmoid_gate * (1.0 + gate_pre * (1.0 - sigmoid_gate))
+        ).astype(jnp.bfloat16)
+        up_pre_ref[rows, :] = (d_hidden * silu_gate).astype(jnp.bfloat16)
+        score_ref[rows, :] = jnp.broadcast_to(score, (step, LANES))
+        return carry
+
+    lax.fori_loop(0, partial_ref.shape[0] // step, one, 0)
+    a = lax.broadcasted_iota(jnp.int32, (half, LANES), 0)
+    b = lax.broadcasted_iota(jnp.int32, (half, LANES), 1)
+    for h, pack_ref in enumerate((pack_guest_ref, pack_own_ref)):
+        rows = slice(h * half, (h + 1) * half)
+        pack_ref[:half, :] = (
+            contract(gate_pre_ref[rows, :hid], gate_ref[...], 1, 1)
+            + contract(gate_pre_ref[rows, hid:], stack_ref[:width, :], 1, 1)
+            + contract(up_pre_ref[rows, :hid], up_ref[...], 1, 1)
+            + contract(up_pre_ref[rows, hid:], stack_ref[width : 2 * width, :], 1, 1)
+        ).astype(jnp.bfloat16)
+        pack_ref[half:, :] = jnp.zeros((pack_ref.shape[0] - half, width), jnp.bfloat16)
+        score = score_ref[rows, :]
+        for k in range(-(-half // LANES)):
+            row = jnp.sum(jnp.where(a == b + k * LANES, score, 0.0), axis=0, keepdims=True)
+            pack_ref[half:, k * LANES : (k + 1) * LANES] = jnp.broadcast_to(
+                row, (pack_ref.shape[0] - half, LANES)
+            ).astype(jnp.bfloat16)
+
+
+def products_kernel(guest_ref, own_ref, hidden_ref, gate_pre_ref, up_pre_ref, out_ref, *, first):
+    hid = out_ref.shape[1]
+    width = guest_ref.shape[1] // 2
+    half = guest_ref.shape[0]
+    part = slice(first, first + hid)
+    step = 256
+
+    def product(left, right):
+        return sum(
+            contract(left(ref, rows), right(ref, rows), 0, 0)
+            for ref, rows in ((guest_ref, slice(0, half)), (own_ref, slice(half, 2 * half)))
+        ).astype(out_ref.dtype)
+
+    for k in range(width // step):
+        cols = slice(k * step, (k + 1) * step)
+        out_ref[cols, :] = product(lambda ref, _: ref[:, cols], lambda _, rows: gate_pre_ref[rows, part])
+        out_ref[width + k * step : width + (k + 1) * step, :] = product(
+            lambda ref, _: ref[:, cols], lambda _, rows: up_pre_ref[rows, part]
+        )
+    for k in range(width // hid):
+        cols = slice(width + k * hid, width + (k + 1) * hid)
+        out_ref[2 * width + k * hid : 2 * width + (k + 1) * hid, :] = product(
+            lambda _, rows: hidden_ref[rows, part], lambda ref, _: ref[:, cols]
+        )
+
+
+def settle_kernel(mine_ref, theirs_ref, gate_ref, up_ref, down_ref):
+    width, hid = gate_ref.shape[1:]
+
+    def total(start, size):
+        rows = slice(start, start + size)
+        return (mine_ref[rows, :] + theirs_ref[rows, :].astype(jnp.float32)).astype(jnp.bfloat16)
+
+    gate_ref[0] = total(0, width)
+    up_ref[0] = total(width, width)
+    for k in range(width // hid):
+        down_ref[0, :, k * hid : (k + 1) * hid] = total(2 * width + k * hid, hid)
+
+
 def per_device(tokens, out_grad, expert_ids, gate_probs, w_gate, w_up, w_down):
     experts = lax.axis_size("expert")
     nx = lax.axis_size("x")
@@ -111,71 +224,62 @@
     def stacked(gate, up, down):
         return jnp.concatenate([gate, up] + jnp.split(down, width // hid, axis=1), axis=0)
 
-    def unstacked(stack):
-        gate, up, down = jnp.split(stack, 3, axis=0)
-        return gate, up, jnp.concatenate(jnp.split(down, width // hid, axis=0), axis=1)
-
-    gate_n, up_n, down_n = unstacked(meet(stacked(gate_w, up_w, down_w), 1))
-    gate_w = jnp.concatenate([gate_w, gate_n], axis=1)
-    up_w = jnp.concatenate([up_w, up_n], axis=1)
-    down_w = jnp.concatenate([down_w, down_n], axis=0)
-
-    def project(rows):
-        return jnp.concatenate(
-            [
-                contract(rows[:, :width], gate_w, 1, 0),
-                contract(rows[:, :width], up_w, 1, 0),
-                contract(rows[:, width:], down_w, 1, 1),
-            ],
-            axis=1,
-        ).astype(jnp.bfloat16)
-
-    def pullback(partial, other):
-        total = partial.astype(jnp.float32) + other.astype(jnp.float32)
-        gate_pre, up_pre, d_hidden = jnp.split(total, 3, axis=1)
-        sigmoid_gate = jax.nn.sigmoid(gate_pre)
-        silu_gate = gate_pre * sigmoid_gate
-        hidden = (silu_gate * up_pre).astype(jnp.bfloat16)
-        score = jnp.sum(d_hidden * hidden.astype(jnp.float32), axis=1)
-        grad_gate_pre = (
-            d_hidden * up_pre * sigmoid_gate * (1.0 + gate_pre * (1.0 - sigmoid_gate))
-        ).astype(jnp.bfloat16)
-        grad_up_pre = (d_hidden * silu_gate).astype(jnp.bfloat16)
-        input_part = (
-            contract(grad_gate_pre, gate_w, 1, 1) + contract(grad_up_pre, up_w, 1, 1)
-        ).astype(jnp.bfloat16)
-        return hidden, grad_gate_pre, grad_up_pre, input_part, score.astype(jnp.bfloat16)
-
-    def packed(input_part, score):
-        score_row = jnp.pad(score.reshape(1, part_rows), ((0, 7), (0, width - part_rows)))
-        return jnp.concatenate([input_part, score_row], axis=0)
-
+    weights = meet(stacked(gate_w, up_w, down_w), 1)
     own = exchange(send, ("expert", "z")).reshape(part_rows, 2 * width)
     guest = meet(own, 3)
     own, guest = lax.optimization_barrier((own, guest))
-    rows = jnp.concatenate([guest, own], axis=0)
-    partial = project(rows)
-    hidden, grad_gate_pre, grad_up_pre, input_part, score = pullback(partial, swap(partial))
-    back = meet(packed(input_part[:part_rows], score[:part_rows]), 3)
-    back = (
-        packed(input_part[part_rows:], score[part_rows:]).astype(jnp.float32)
-        + back.astype(jnp.float32)
-    ).astype(jnp.bfloat16)
-    rows_x, rows_dy = rows[:, :width], rows[:, width:]
-
-    def weight_grads(part):
-        return (
-            contract(rows_x, grad_gate_pre[:, part], 0, 0),
-            contract(rows_x, grad_up_pre[:, part], 0, 0),
-            contract(hidden[:, part], rows_dy, 0, 0),
-        )
-
-    theirs = [g.astype(jnp.bfloat16) for g in weight_grads(slice(hid, None))]
-    theirs = meet(stacked(*theirs), 1)
-    mine = lax.optimization_barrier(weight_grads(slice(0, hid)))
-    grad_gate, grad_up, grad_down = (
-        (own_part + other.astype(jnp.float32)).astype(jnp.bfloat16)[None]
-        for own_part, other in zip(mine, unstacked(theirs))
+
+    vmem = pl.BlockSpec(memory_space=pltpu.VMEM)
+    params = pltpu.CompilerParams(vmem_limit_bytes=40 * 1024 * 1024)
+
+    def call(kernel, outs, args, scratch=(), flops=0):
+        return pl.pallas_call(
+            kernel,
+            out_shape=tuple(jax.ShapeDtypeStruct(s, d) for s, d in outs),
+            in_specs=[vmem] * len(args),
+            out_specs=tuple(vmem for _ in outs),
+            scratch_shapes=list(scratch),
+            compiler_params=params,
+            cost_estimate=pl.CostEstimate(flops=flops, bytes_accessed=6 << 20, transcendentals=0),
+        )(*args)
+
+    bf16 = jnp.bfloat16
+    all_rows, both = 2 * part_rows, 2 * hid
+    dot_flops = 2 * all_rows * width * both
+    (partial,) = call(
+        project_kernel,
+        [((all_rows, 3 * both), bf16)],
+        (guest, own, gate_w, up_w, down_w, weights),
+        flops=3 * dot_flops,
+    )
+    pack_rows = part_rows + 16
+    pack_guest, pack_own, hidden, grad_gate_pre, grad_up_pre = call(
+        pullback_kernel,
+        [((pack_rows, width), bf16)] * 2 + [((all_rows, both), bf16)] * 3,
+        (partial, swap(partial), gate_w, up_w, weights),
+        [pltpu.VMEM((all_rows, LANES), jnp.float32)],
+        flops=2 * dot_flops,
+    )
+    back = meet(pack_guest, 3)
+    terms = (guest, own, hidden, grad_gate_pre, grad_up_pre)
+    (theirs,) = call(
+        functools.partial(products_kernel, first=hid),
+        [((3 * width, hid), bf16)],
+        terms,
+        flops=3 * dot_flops // 2,
+    )
+    theirs = meet(theirs, 1)
+    back = (pack_own.astype(jnp.float32) + back.astype(jnp.float32)).astype(bf16)
+    (mine,) = call(
+        functools.partial(products_kernel, first=0),
+        [((3 * width, hid), jnp.float32)],
+        terms,
+        flops=3 * dot_flops // 2,
+    )
+    grad_gate, grad_up, grad_down = call(
+        settle_kernel,
+        [((1, width, hid), bf16), ((1, width, hid), bf16), ((1, hid, width), bf16)],
+        (mine, theirs),
     )
 
     data = back[:part_rows].reshape(experts * nz, CAP * chunks, LANES)

time: 130 us -> 126 us (0.969)
  Pallas kernels: 2.19 us -> 13.7 us
  matrix products: 11.1 us -> 0.8 us
  other arithmetic: 5.53 us -> 1.2 us
  waiting for transfers between devices: 53 us -> 56.5 us
  starting transfers between devices: 41.6 us -> 38.3 us
    pallas_call x0 -> x5, Pallas kernels: none -> 11.5 us  [call(): pl.pallas_call(kernel, out_shape=tuple((jax.ShapeDtypeStruct(s, d) for s,...]
    dot_general x12 -> x1, matrix products: 11.1 us -> 0.8 us  [contract(): lax.dot_general(left, right, (((left_dim,), (right_dim,)), ((), ())), pre...]
    ppermute x4, waiting for transfers between devices: 21 us -> 25.6 us  [meet(): return lax.ppermute(block, 'x', [(i, i ^ mask) for i in range(nx)])]
    split x3 -> x0, local copies, waits for them, and re-layouts: 3.67 us -> none  [the longest x2 2.41 us: unstacked(): jnp.split(down, width // hid, axis=0)]
    broadcast_in_dim x2 -> x0, other arithmetic: 3.36 us -> none  [per_device(): (own_part + other.astype(jnp.float32)).astype(jnp.bfloat16)[None]]
    unnamed x31 -> x37, local copies, waits for them, and re-layouts: 6.71 us -> 9.32 us
    all_to_all x2, starting transfers between devices: 29.4 us -> 27 us  [exchange(): return lax.all_to_all(block, axes, split_axis=0, concat_axis=0, tiled=True)]
  transfers between devices with their start and end apart: 7 -> 7, of which waited for: 5 -> 5; matrix products, arithmetic and copies ran while one was open for 16% -> 8% of each run, Pallas kernels for 0% -> 3%
where the time goes in v5:
time: 126 us
  waiting for transfers between devices  56.5 us (45%)
  starting transfers between devices  38.3 us (30%)
  local copies, waits for them, and re-layouts  14.3 us (11%)
  Pallas kernels  13.7 us (11%)
    all_to_all x2, waiting for transfers between devices, exchange(): return lax.all_to_all(block, axes, split_axis=0, concat_axis=0, tiled=True)  28 us
    all_to_all x2, starting transfers between devices, exchange(): return lax.all_to_all(block, axes, split_axis=0, concat_axis=0, tiled=True)  27 us
    ppermute x4, waiting for transfers between devices, meet(): return lax.ppermute(block, 'x', [(i, i ^ mask) for i in range(nx)])  25.6 us
    pallas_call x5, Pallas kernels, call(): pl.pallas_call(kernel, out_shape=tuple((jax.ShapeDtypeStruct(s, d) for s,...  11.5 us
    ppermute x4, starting transfers between devices, meet(): return lax.ppermute(block, 'x', [(i, i ^ mask) for i in range(nx)])  9.41 us
    unnamed x37, local copies, waits for them, and re-layouts  9.32 us
    ppermute x1, waiting for transfers between devices, swap(): return lax.ppermute(block, 'dp', [(0, 1), (1, 0)])  2.81 us
  transfers between devices with their start and end apart: 7, of which 5 were waited for; matrix products, arithmetic and copies ran while one was open for 8% of the time, Pallas kernels for 3%

profile of v5, /device:TPU:6, one launch (start us, length us, event | category | flops | bytes accessed | tf_op | source)
XLA Modules:
  0.0 125.7 jit_solution(5082275396257768720)
XLA Ops:
  0.7 2.2 %shard_map.110 = (bf16[8,8,48,128]{3,2,1,0:T(8,128)(2,1)}, s32[2,8]{1,0:T(2,128)}) custom-call(s32[2,8]{1,0:T(2,128)} %bitcast.35, f32[2,8]{1,0:T(2,128)} %bitcast.32, bf16[8,1024]{1,0:T(8,128)(2,1)} %tokens_ref.1, bf16[8,1024]{1,0:T(8,128)(2,1)} %out_grad_ref.1), custom_call_target="tpu_custom_call" | custom-call | tf_op jit(solution)/shard_map/pallas_call | solution.py:194
  2.8 16.9 %all-to-all-start = ((bf16[64,48,128]{2,1,0:T(8,128)(2,1)}), bf16[64,48,128]{2,1,0:T(8,128)(2,1)}, u32[]{:S(2)}, u32[]{:S(2)}) async-start(bf16[64,48,128]{2,1,0:T(8,128)(2,1)} %bitcast.31), calls=%async_computation | async-start | bytes 1572864 | tf_op jit(solution)/shard_map/all_to_all | solution.py:22
  24.2 2.7 %collective-permute-start.1 = (bf16[3072,256]{1,0:T(8,128)(2,1)}, bf16[3072,256]{1,0:T(8,128)(2,1)S(1)}, u32[]{:S(2)}, u32[]{:S(2)}) collective-permute-start(bf16[3072,256]{1,0:T(8,128)(2,1)} %slice_dynamic-update-slice_fusion), channel_id=1, source_target_pairs={{0,16},{16,0},{32,48},{48,32},{1,17},{17,1},{33,49},{49,33},{2,18}... | collective-permute-start | bytes 4718600 | tf_op jit(solution)/shard_map/ppermute | solution.py:219
  26.9 16.4 %all-to-all-done = bf16[64,48,128]{2,1,0:T(8,128)(2,1)} async-done(((bf16[64,48,128]{2,1,0:T(8,128)(2,1)}), bf16[64,48,128]{2,1,0:T(8,128)(2,1)}, u32[]{:S(2)}, u32[]{:S(2)}) %all-to-all-start) | async-done | bytes 786464 | tf_op jit(solution)/shard_map/all_to_all | solution.py:22
  43.3 1.4 %reshape.30.own_ref = bf16[192,2048]{1,0:T(8,128)(2,1)S(1)} reshape(bf16[64,48,128]{2,1,0:T(8,128)(2,1)} %all-to-all-done) | data formatting | bytes 1572864 | tf_op jit(solution)/shard_map/reshape | solution.py:228
  44.7 2.4 %collective-permute-start = (bf16[192,2048]{1,0:T(8,128)(2,1)S(1)}, bf16[192,2048]{1,0:T(8,128)(2,1)S(1)}, u32[]{:S(2)}, u32[]{:S(2)}) collective-permute-start(bf16[192,2048]{1,0:T(8,128)(2,1)S(1)} %reshape.30.own_ref), channel_id=1, source_target_pairs={{0,48},{16,32},{32,16},{48,0},{1,49},{17,33},{33,17},{49,1},{2,50}... | collective-permute-start | bytes 2359304 | tf_op jit(solution)/shard_map/ppermute | solution.py:219
  47.1 17.2 %collective-permute-done.guest_ref = bf16[192,2048]{1,0:T(8,128)(2,1)S(1)} collective-permute-done((bf16[192,2048]{1,0:T(8,128)(2,1)S(1)}, bf16[192,2048]{1,0:T(8,128)(2,1)S(1)}, u32[]{:S(2)}, u32[]{:S(2)}) %collective-permute-start) | collective-permute-done | bytes 786464 | tf_op jit(solution)/shard_map/ppermute | solution.py:219
  64.4 1.3 %copy-done.7 = bf16[1,256,1024]{2,1,0:T(8,128)(2,1)S(1)} copy-done((bf16[1,256,1024]{2,1,0:T(8,128)(2,1)S(1)}, bf16[1,256,1024]{2,1,0:T(8,128)(2,1)}, u32[]{:S(2)}) %copy-start.7) | copy-done | bytes 524312
  65.7 1.7 %shard_map.111.partial_ref = bf16[384,1536]{1,0:T(8,128)(2,1)S(1)} custom-call(bf16[192,2048]{1,0:T(8,128)(2,1)S(1)} %collective-permute-done.guest_ref, bf16[192,2048]{1,0:T(8,128)(2,1)S(1)} %reshape.30.own_ref, bf16[1024,256]{1,0:T(8,128)(2,1)S(1)} %bitcast.20, bf16[1024,256]{1,0:T(8,128)(2,1)S(1)} %bitcast.22, bf16[256,1024]{1,0:T(8,128)(2,1)S(1)} %bitcast.28, ...), custom_call_target="tpu_custom_call" | custom-call | flops 1207959552 | bytes 6291456 | tf_op jit(solution)/shard_map/pallas_call | solution.py:236
  67.4 1.9 %collective-permute-start.2 = (bf16[384,1536]{1,0:T(8,128)(2,1)S(1)}, bf16[384,1536]{1,0:T(8,128)(2,1)S(1)}, u32[]{:S(2)}, u32[]{:S(2)}) collective-permute-start(bf16[384,1536]{1,0:T(8,128)(2,1)S(1)} %shard_map.111.partial_ref), channel_id=1, source_target_pairs={{0,1},{1,0},{2,3},{3,2},{4,5},{5,4},{6,7},{7,6},{8,9},{9,8},{10,11... | collective-permute-start | bytes 3538952 | tf_op jit(solution)/shard_map/ppermute | solution.py:222
  69.3 2.8 %collective-permute-done.2.other_ref = bf16[384,1536]{1,0:T(8,128)(2,1)S(1)} collective-permute-done((bf16[384,1536]{1,0:T(8,128)(2,1)S(1)}, bf16[384,1536]{1,0:T(8,128)(2,1)S(1)}, u32[]{:S(2)}, u32[]{:S(2)}) %collective-permute-start.2) | collective-permute-done | bytes 1179680 | tf_op jit(solution)/shard_map/ppermute | solution.py:222
  72.1 3.8 %shard_map.112 = (bf16[208,1024]{1,0:T(8,128)(2,1)S(1)}, bf16[208,1024]{1,0:T(8,128)(2,1)S(1)}, bf16[384,512]{1,0:T(8,128)(2,1)S(1)}, bf16[384,512]{1,0:T(8,128)(2,1)S(1)}, bf16[384,512]{1,0:T(8,128)(2,1)S(1)}) custom-call(bf16[384,1536]{1,0:T(8,128)(2,1)S(1)} %shard_map.111.partial_ref, bf16[384,1536]{1,0:T(8,128)(2,1)S(1)} %collective-permute-done.2.other_ref, ...), custom_call_target="tpu_custom_call" | custom-call | flops 805306368 | bytes 6291456 | tf_op jit(solution)/shard_map/pallas_call | solution.py:236
  76.0 2.4 %collective-permute-start.3 = (bf16[208,1024]{1,0:T(8,128)(2,1)S(1)}, bf16[208,1024]{1,0:T(8,128)(2,1)S(1)}, u32[]{:S(2)}, u32[]{:S(2)}) collective-permute-start(bf16[208,1024]{1,0:T(8,128)(2,1)S(1)} %get-tuple-element.22), channel_id=1, source_target_pairs={{0,48},{16,32},{32,16},{48,0},{1,49},{17,33},{33,17},{49,1},{2,50}... | collective-permute-start | bytes 1277960 | tf_op jit(solution)/shard_map/ppermute | solution.py:219
  78.4 2.2 %shard_map.114 = bf16[3072,256]{1,0:T(8,128)(2,1)} custom-call(bf16[192,2048]{1,0:T(8,128)(2,1)S(1)} %collective-permute-done.guest_ref, bf16[192,2048]{1,0:T(8,128)(2,1)S(1)} %reshape.30.own_ref, bf16[384,512]{1,0:T(8,128)(2,1)S(1)} %get-tuple-element.23.hidden_ref, bf16[384,512]{1,0:T(8,128)(2,1)S(1)} %get-tuple-element.24.gate_pre_ref, ...), custom_call_target="tpu_custom_call" | custom-call | flops 603979776 | bytes 6291456 | tf_op jit(solution)/shard_map/pallas_call | solution.py:236
  80.6 1.9 %collective-permute-start.4 = (bf16[3072,256]{1,0:T(8,128)(2,1)}, bf16[3072,256]{1,0:T(8,128)(2,1)}, u32[]{:S(2)}, u32[]{:S(2)}) collective-permute-start(bf16[3072,256]{1,0:T(8,128)(2,1)} %shard_map.114), channel_id=1, source_target_pairs={{0,16},{16,0},{32,48},{48,32},{1,17},{17,1},{33,49},{49,33},{2,18}... | collective-permute-start | bytes 4718600 | tf_op jit(solution)/shard_map/ppermute | solution.py:219
  82.6 8.4 %collective-permute-done.3 = bf16[208,1024]{1,0:T(8,128)(2,1)S(1)} collective-permute-done((bf16[208,1024]{1,0:T(8,128)(2,1)S(1)}, bf16[208,1024]{1,0:T(8,128)(2,1)S(1)}, u32[]{:S(2)}, u32[]{:S(2)}) %collective-permute-start.3) | collective-permute-done | bytes 426016 | tf_op jit(solution)/shard_map/ppermute | solution.py:219
  91.7 1.2 copy.20
  92.9 10.0 %all-to-all-start.1 = ((bf16[64,13,2,128]{3,2,1,0:T(2,128)(2,1)}), bf16[64,13,2,128]{3,2,1,0:T(2,128)(2,1)}, u32[]{:S(2)}, u32[]{:S(2)}) async-start(bf16[64,13,2,128]{3,2,1,0:T(2,128)(2,1)} %copy.20), calls=%async_computation.1 | async-start | bytes 851968 | tf_op jit(solution)/shard_map/all_to_all | solution.py:22
  102.9 1.1 copy-done.1
  104.1 1.1 copy-done.3
  107.2 1.0 shard_map.113.mine_ref
  108.2 11.6 %all-to-all-done.1 = bf16[64,13,2,128]{3,2,1,0:T(2,128)(2,1)} async-done(((bf16[64,13,2,128]{3,2,1,0:T(2,128)(2,1)}), bf16[64,13,2,128]{3,2,1,0:T(2,128)(2,1)}, u32[]{:S(2)}, u32[]{:S(2)}) %all-to-all-start.1) | async-done | bytes 426016 | tf_op jit(solution)/shard_map/all_to_all | solution.py:22
  119.8 1.1 copy.21
  122.9 2.7 %shard_map.115 = (bf16[1,1024,256]{2,1,0:T(8,128)(2,1)}, bf16[1,1024,256]{2,1,0:T(8,128)(2,1)}, bf16[1,256,1024]{2,1,0:T(8,128)(2,1)}) custom-call(f32[3072,256]{1,0:T(8,128)S(1)} %shard_map.113.mine_ref, bf16[3072,256]{1,0:T(8,128)(2,1)} %collective-permute-done.4.theirs_ref), custom_call_target="tpu_custom_call" | custom-call | bytes 6291456 | tf_op jit(solution)/shard_map/pallas_call | solution.py:236
  (54 shorter events, 9.0 us)
Async XLA Ops:
  0.6 19.2 %copy-start.4 = (bf16[1,1024,256]{2,1,0:T(8,128)(2,1)S(1)}, bf16[1,1024,256]{2,1,0:T(8,128)(2,1)}, u32[]{:S(2)}) copy-start(bf16[1,1024,256]{2,1,0:T(8,128)(2,1)} %param.11) | copy-start | bytes 1572868
  0.6 20.0 %copy-start.5 = (bf16[1,1024,256]{2,1,0:T(8,128)(2,1)S(1)}, bf16[1,1024,256]{2,1,0:T(8,128)(2,1)}, u32[]{:S(2)}) copy-start(bf16[1,1024,256]{2,1,0:T(8,128)(2,1)} %param.12) | copy-start | bytes 1572868
  2.8 18.7 %copy-start.6 = (bf16[1,256,1024]{2,1,0:T(8,128)(2,1)S(1)}, bf16[1,256,1024]{2,1,0:T(8,128)(2,1)}, u32[]{:S(2)}) copy-start(bf16[1,256,1024]{2,1,0:T(8,128)(2,1)} %param.13) | copy-start | bytes 1572868
  2.8 40.5 %all-to-all-start = ((bf16[64,48,128]{2,1,0:T(8,128)(2,1)}), bf16[64,48,128]{2,1,0:T(8,128)(2,1)}, u32[]{:S(2)}, u32[]{:S(2)}) async-start(bf16[64,48,128]{2,1,0:T(8,128)(2,1)} %bitcast.31), calls=%async_computation | async-start | bytes 1572864 | tf_op jit(solution)/shard_map/all_to_all | solution.py:22
  24.2 40.2 %collective-permute-start.1 = (bf16[3072,256]{1,0:T(8,128)(2,1)}, bf16[3072,256]{1,0:T(8,128)(2,1)S(1)}, u32[]{:S(2)}, u32[]{:S(2)}) collective-permute-start(bf16[3072,256]{1,0:T(8,128)(2,1)} %slice_dynamic-update-slice_fusion), channel_id=1, source_target_pairs={{0,16},{16,0},{32,48},{48,32},{1,17},{17,1},{33,49},{49,33},{2,18}... | collective-permute-start | bytes 4718600 | tf_op jit(solution)/shard_map/ppermute | solution.py:219
  44.7 33.6 %copy-start = (bf16[192,2048]{1,0:T(8,128)(2,1)}, bf16[192,2048]{1,0:T(8,128)(2,1)S(1)}, u32[]{:S(2)}) copy-start(bf16[192,2048]{1,0:T(8,128)(2,1)S(1)} %reshape.30.own_ref) | copy-start | bytes 2359300
  44.7 19.6 %collective-permute-start = (bf16[192,2048]{1,0:T(8,128)(2,1)S(1)}, bf16[192,2048]{1,0:T(8,128)(2,1)S(1)}, u32[]{:S(2)}, u32[]{:S(2)}) collective-permute-start(bf16[192,2048]{1,0:T(8,128)(2,1)S(1)} %reshape.30.own_ref), channel_id=1, source_target_pairs={{0,48},{16,32},{32,16},{48,0},{1,49},{17,33},{33,17},{49,1},{2,50}... | collective-permute-start | bytes 2359304 | tf_op jit(solution)/shard_map/ppermute | solution.py:219
  64.4 14.0 %copy-start.2 = (bf16[192,2048]{1,0:T(8,128)(2,1)}, bf16[192,2048]{1,0:T(8,128)(2,1)S(1)}, u32[]{:S(2)}) copy-start(bf16[192,2048]{1,0:T(8,128)(2,1)S(1)} %collective-permute-done.guest_ref) | copy-start | bytes 2359300
  64.4 1.3 %copy-start.7 = (bf16[1,256,1024]{2,1,0:T(8,128)(2,1)S(1)}, bf16[1,256,1024]{2,1,0:T(8,128)(2,1)}, u32[]{:S(2)}) copy-start(bf16[1,256,1024]{2,1,0:T(8,128)(2,1)} %param.13) | copy-start | bytes 1572868
  67.4 4.7 %collective-permute-start.2 = (bf16[384,1536]{1,0:T(8,128)(2,1)S(1)}, bf16[384,1536]{1,0:T(8,128)(2,1)S(1)}, u32[]{:S(2)}, u32[]{:S(2)}) collective-permute-start(bf16[384,1536]{1,0:T(8,128)(2,1)S(1)} %shard_map.111.partial_ref), channel_id=1, source_target_pairs={{0,1},{1,0},{2,3},{3,2},{4,5},{5,4},{6,7},{7,6},{8,9},{9,8},{10,11... | collective-permute-start | bytes 3538952 | tf_op jit(solution)/shard_map/ppermute | solution.py:222
  76.0 4.7 %copy-start.8 = (bf16[384,512]{1,0:T(8,128)(2,1)}, bf16[384,512]{1,0:T(8,128)(2,1)S(1)}, u32[]{:S(2)}) copy-start(bf16[384,512]{1,0:T(8,128)(2,1)S(1)} %get-tuple-element.23.hidden_ref) | copy-start | bytes 1179652
  76.0 4.7 %copy-start.10 = (bf16[384,512]{1,0:T(8,128)(2,1)}, bf16[384,512]{1,0:T(8,128)(2,1)S(1)}, u32[]{:S(2)}) copy-start(bf16[384,512]{1,0:T(8,128)(2,1)S(1)} %get-tuple-element.24.gate_pre_ref) | copy-start | bytes 1179652
  76.0 4.7 %copy-start.12 = (bf16[384,512]{1,0:T(8,128)(2,1)}, bf16[384,512]{1,0:T(8,128)(2,1)S(1)}, u32[]{:S(2)}) copy-start(bf16[384,512]{1,0:T(8,128)(2,1)S(1)} %get-tuple-element.25.up_pre_ref) | copy-start | bytes 1179652
  76.0 15.0 %collective-permute-start.3 = (bf16[208,1024]{1,0:T(8,128)(2,1)S(1)}, bf16[208,1024]{1,0:T(8,128)(2,1)S(1)}, u32[]{:S(2)}, u32[]{:S(2)}) collective-permute-start(bf16[208,1024]{1,0:T(8,128)(2,1)S(1)} %get-tuple-element.22), channel_id=1, source_target_pairs={{0,48},{16,32},{32,16},{48,0},{1,49},{17,33},{33,17},{49,1},{2,50}... | collective-permute-start | bytes 1277960 | tf_op jit(solution)/shard_map/ppermute | solution.py:219
  80.6 42.3 %collective-permute-start.4 = (bf16[3072,256]{1,0:T(8,128)(2,1)}, bf16[3072,256]{1,0:T(8,128)(2,1)}, u32[]{:S(2)}, u32[]{:S(2)}) collective-permute-start(bf16[3072,256]{1,0:T(8,128)(2,1)} %shard_map.114), channel_id=1, source_target_pairs={{0,16},{16,0},{32,48},{48,32},{1,17},{17,1},{33,49},{49,33},{2,18}... | collective-permute-start | bytes 4718600 | tf_op jit(solution)/shard_map/ppermute | solution.py:219
  91.4 11.5 %copy-start.15 = (s32[2,8]{1,0:T(2,128)S(1)}, s32[2,8]{1,0:T(2,128)}, u32[]{:S(2)}) copy-start(s32[2,8]{1,0:T(2,128)} %get-tuple-element.17) | copy-start | bytes 196
  91.4 11.5 %copy-start.9 = (bf16[384,512]{1,0:T(8,128)(2,1)S(1)}, bf16[384,512]{1,0:T(8,128)(2,1)}, u32[]{:S(2)}) copy-start(bf16[384,512]{1,0:T(8,128)(2,1)} %copy-done.8) | copy-start | bytes 1179652
  92.9 27.0 %all-to-all-start.1 = ((bf16[64,13,2,128]{3,2,1,0:T(2,128)(2,1)}), bf16[64,13,2,128]{3,2,1,0:T(2,128)(2,1)}, u32[]{:S(2)}, u32[]{:S(2)}) async-start(bf16[64,13,2,128]{3,2,1,0:T(2,128)(2,1)} %copy.20), calls=%async_computation.1 | async-start | bytes 851968 | tf_op jit(solution)/shard_map/all_to_all | solution.py:22
  102.9 1.1 copy-start.1
  104.1 1.1 copy-start.3
  105.2 1.0 copy-start.11
  106.2 1.0 copy-start.13
  108.2 13.4 %copy-start.14 = (f32[8,2]{0,1:T(2,128)S(1)}, f32[8,2]{0,1:T(2,128)}, u32[]{:S(2)}) copy-start(f32[8,2]{0,1:T(2,128)} %param.10) | copy-start | bytes 196

commit v6 on v5

--- a/solution.py
+++ b/solution.py
@@ -99,16 +99,17 @@
 
 def pullback_kernel(
     partial_ref, other_ref, gate_ref, up_ref, stack_ref,
-    pack_guest_ref, pack_own_ref, hidden_ref, gate_pre_ref, up_pre_ref, score_ref,
+    pack_ref, hidden_ref, gate_pre_ref, up_pre_ref, score_ref, *, first
 ):
     width, hid = gate_ref.shape
     both = 2 * hid
-    half = partial_ref.shape[0] // 2
+    half = hidden_ref.shape[0]
     step = 16
 
     def one(i, carry):
         rows = pl.ds(pl.multiple_of(i * step, step), step)
-        total = partial_ref[rows, :].astype(jnp.float32) + other_ref[rows, :].astype(jnp.float32)
+        source = pl.ds(pl.multiple_of(first + i * step, step), step)
+        total = partial_ref[source, :].astype(jnp.float32) + other_ref[source, :].astype(jnp.float32)
         gate_pre, up_pre, d_hidden = total[:, :both], total[:, both : 2 * both], total[:, 2 * both :]
         sigmoid_gate = jax.nn.sigmoid(gate_pre)
         silu_gate = gate_pre * sigmoid_gate
@@ -122,49 +123,43 @@
         score_ref[rows, :] = jnp.broadcast_to(score, (step, LANES))
         return carry
 
-    lax.fori_loop(0, partial_ref.shape[0] // step, one, 0)
+    lax.fori_loop(0, half // step, one, 0)
+    pack_ref[:half, :] = (
+        contract(gate_pre_ref[:, :hid], gate_ref[...], 1, 1)
+        + contract(gate_pre_ref[:, hid:], stack_ref[:width, :], 1, 1)
+        + contract(up_pre_ref[:, :hid], up_ref[...], 1, 1)
+        + contract(up_pre_ref[:, hid:], stack_ref[width : 2 * width, :], 1, 1)
+    ).astype(jnp.bfloat16)
+    extra = pack_ref.shape[0] - half
+    pack_ref[half:, :] = jnp.zeros((extra, width), jnp.bfloat16)
+    score = score_ref[...]
     a = lax.broadcasted_iota(jnp.int32, (half, LANES), 0)
     b = lax.broadcasted_iota(jnp.int32, (half, LANES), 1)
-    for h, pack_ref in enumerate((pack_guest_ref, pack_own_ref)):
-        rows = slice(h * half, (h + 1) * half)
-        pack_ref[:half, :] = (
-            contract(gate_pre_ref[rows, :hid], gate_ref[...], 1, 1)
-            + contract(gate_pre_ref[rows, hid:], stack_ref[:width, :], 1, 1)
-            + contract(up_pre_ref[rows, :hid], up_ref[...], 1, 1)
-            + contract(up_pre_ref[rows, hid:], stack_ref[width : 2 * width, :], 1, 1)
+    for k in range(-(-half // LANES)):
+        row = jnp.sum(jnp.where(a == b + k * LANES, score, 0.0), axis=0, keepdims=True)
+        pack_ref[half:, k * LANES : (k + 1) * LANES] = jnp.broadcast_to(
+            row, (extra, LANES)
         ).astype(jnp.bfloat16)
-        pack_ref[half:, :] = jnp.zeros((pack_ref.shape[0] - half, width), jnp.bfloat16)
-        score = score_ref[rows, :]
-        for k in range(-(-half // LANES)):
-            row = jnp.sum(jnp.where(a == b + k * LANES, score, 0.0), axis=0, keepdims=True)
-            pack_ref[half:, k * LANES : (k + 1) * LANES] = jnp.broadcast_to(
-                row, (pack_ref.shape[0] - half, LANES)
-            ).astype(jnp.bfloat16)
-
-
-def products_kernel(guest_ref, own_ref, hidden_ref, gate_pre_ref, up_pre_ref, out_ref, *, first):
+
+
+def products_kernel(*refs, first):
+    out_ref = refs[-1]
+    groups = (refs[:4], refs[4:8])
     hid = out_ref.shape[1]
-    width = guest_ref.shape[1] // 2
-    half = guest_ref.shape[0]
+    width = refs[0].shape[1] // 2
     part = slice(first, first + hid)
-    step = 256
 
     def product(left, right):
-        return sum(
-            contract(left(ref, rows), right(ref, rows), 0, 0)
-            for ref, rows in ((guest_ref, slice(0, half)), (own_ref, slice(half, 2 * half)))
-        ).astype(out_ref.dtype)
-
-    for k in range(width // step):
-        cols = slice(k * step, (k + 1) * step)
-        out_ref[cols, :] = product(lambda ref, _: ref[:, cols], lambda _, rows: gate_pre_ref[rows, part])
-        out_ref[width + k * step : width + (k + 1) * step, :] = product(
-            lambda ref, _: ref[:, cols], lambda _, rows: up_pre_ref[rows, part]
+        return sum(contract(left(group), right(group), 0, 0) for group in groups).astype(out_ref.dtype)
+
+    for k in range(width // hid):
+        low, high = k * hid, (k + 1) * hid
+        out_ref[low:high, :] = product(lambda g: g[0][:, low:high], lambda g: g[2][:, part])
+        out_ref[width + low : width + high, :] = product(
+            lambda g: g[0][:, low:high], lambda g: g[3][:, part]
         )
-    for k in range(width // hid):
-        cols = slice(width + k * hid, width + (k + 1) * hid)
-        out_ref[2 * width + k * hid : 2 * width + (k + 1) * hid, :] = product(
-            lambda _, rows: hidden_ref[rows, part], lambda ref, _: ref[:, cols]
+        out_ref[2 * width + low : 2 * width + high, :] = product(
+            lambda g: g[1][:, part], lambda g: g[0][:, width + low : width + high]
         )
 
 
@@ -203,6 +198,7 @@
             pl.BlockSpec(memory_space=pltpu.VMEM),
         ),
         scratch_shapes=[pltpu.VMEM((experts, rows_out, LANES), jnp.float32)],
+        compiler_params=pltpu.CompilerParams(vmem_limit_bytes=40 << 20),
     )(expert_ids.T, gate_probs.T, tokens, out_grad)
     send = send.reshape(experts * nz, rows_out, LANES)
     slot_names = jnp.arange(slots, dtype=jnp.int32)
@@ -230,7 +226,7 @@
     own, guest = lax.optimization_barrier((own, guest))
 
     vmem = pl.BlockSpec(memory_space=pltpu.VMEM)
-    params = pltpu.CompilerParams(vmem_limit_bytes=40 * 1024 * 1024)
+    params = pltpu.CompilerParams(vmem_limit_bytes=16 << 20)
 
     def call(kernel, outs, args, scratch=(), flops=0):
         return pl.pallas_call(
@@ -253,15 +249,21 @@
         flops=3 * dot_flops,
     )
     pack_rows = part_rows + 16
-    pack_guest, pack_own, hidden, grad_gate_pre, grad_up_pre = call(
-        pullback_kernel,
-        [((pack_rows, width), bf16)] * 2 + [((all_rows, both), bf16)] * 3,
-        (partial, swap(partial), gate_w, up_w, weights),
-        [pltpu.VMEM((all_rows, LANES), jnp.float32)],
-        flops=2 * dot_flops,
-    )
+    other = swap(partial)
+
+    def pulled(first):
+        return call(
+            functools.partial(pullback_kernel, first=first),
+            [((pack_rows, width), bf16)] + [((part_rows, both), bf16)] * 3,
+            (partial, other, gate_w, up_w, weights),
+            [pltpu.VMEM((part_rows, LANES), jnp.float32)],
+            flops=dot_flops,
+        )
+
+    pack_guest, *terms_guest = pulled(0)
     back = meet(pack_guest, 3)
-    terms = (guest, own, hidden, grad_gate_pre, grad_up_pre)
+    pack_own, *terms_own = pulled(part_rows)
+    terms = (guest, *terms_guest, own, *terms_own)
     (theirs,) = call(
         functools.partial(products_kernel, first=hid),
         [((3 * width, hid), bf16)],

time: 126 us -> 128 us (1.016); the launches traced: 126 us -> 126 us
  local copies, waits for them, and re-layouts: 14.3 us -> 18.9 us
  waiting for transfers between devices: 56.5 us -> 52.6 us
    unnamed x37 -> x55, local copies, waits for them, and re-layouts: 9.32 us -> 13.9 us
    ppermute x4, waiting for transfers between devices: 25.6 us -> 23.6 us  [meet(): return lax.ppermute(block, 'x', [(i, i ^ mask) for i in range(nx)])]
    all_to_all x2, waiting for transfers between devices: 28 us -> 26.3 us  [exchange(): return lax.all_to_all(block, axes, split_axis=0, concat_axis=0, tiled=True)]
    pallas_call x5 -> x6, Pallas kernels: 11.5 us -> 11.6 us  [call(): pl.pallas_call(kernel, out_shape=tuple((jax.ShapeDtypeStruct(s, d) for s,...]
  transfers between devices with their start and end apart: 7 -> 7, of which waited for: 5 -> 5; matrix products, arithmetic and copies ran while one was open for 8% -> 8% of each run, Pallas kernels for 3% -> 4%
where the time goes in v6:
time: 128 us; the launch traced here: 126 us
  waiting for transfers between devices  52.6 us (41%)
  starting transfers between devices  38.3 us (30%)
  local copies, waits for them, and re-layouts  18.9 us (15%)
  Pallas kernels  13 us (10%)
    all_to_all x2, starting transfers between devices, exchange(): return lax.all_to_all(block, axes, split_axis=0, concat_axis=0, tiled=True)  27 us
    all_to_all x2, waiting for transfers between devices, exchange(): return lax.all_to_all(block, axes, split_axis=0, concat_axis=0, tiled=True)  26.3 us
    ppermute x4, waiting for transfers between devices, meet(): return lax.ppermute(block, 'x', [(i, i ^ mask) for i in range(nx)])  23.6 us
    unnamed x55, local copies, waits for them, and re-layouts  13.9 us
    pallas_call x6, Pallas kernels, call(): pl.pallas_call(kernel, out_shape=tuple((jax.ShapeDtypeStruct(s, d) for s,...  11.6 us
    ppermute x4, starting transfers between devices, meet(): return lax.ppermute(block, 'x', [(i, i ^ mask) for i in range(nx)])  9.41 us
    ppermute x1, waiting for transfers between devices, swap(): return lax.ppermute(block, 'dp', [(0, 1), (1, 0)])  2.81 us
  transfers between devices with their start and end apart: 7, of which 5 were waited for; matrix products, arithmetic and copies ran while one was open for 8% of the time, Pallas kernels for 4%

profile of v6, /device:TPU:6, one launch (start us, length us, event | category | flops | bytes accessed | tf_op | source)
XLA Modules:
  0.0 125.8 jit_solution(9444885209220628292)
XLA Ops:
  3.5 1.3 %shard_map.110 = (bf16[8,8,48,128]{3,2,1,0:T(8,128)(2,1)}, s32[2,8]{1,0:T(2,128)S(1)}) custom-call(s32[2,8]{1,0:T(2,128)S(1)} %bitcast.32, f32[2,8]{1,0:T(2,128)S(1)} %bitcast.31, bf16[8,1024]{1,0:T(8,128)(2,1)S(1)} %copy-done.20, bf16[8,1024]{1,0:T(8,128)(2,1)S(1)} %copy-done.21), custom_call_target="tpu_custom_call" | custom-call | tf_op jit(solution)/shard_map/pallas_call | solution.py:189
  4.9 16.9 %all-to-all-start = ((bf16[64,48,128]{2,1,0:T(8,128)(2,1)}), bf16[64,48,128]{2,1,0:T(8,128)(2,1)}, u32[]{:S(2)}, u32[]{:S(2)}) async-start(bf16[64,48,128]{2,1,0:T(8,128)(2,1)} %bitcast.4), calls=%async_computation | async-start | bytes 1572864 | tf_op jit(solution)/shard_map/all_to_all | solution.py:22
  26.2 2.7 %collective-permute-start.1 = (bf16[3072,256]{1,0:T(8,128)(2,1)}, bf16[3072,256]{1,0:T(8,128)(2,1)S(1)}, u32[]{:S(2)}, u32[]{:S(2)}) collective-permute-start(bf16[3072,256]{1,0:T(8,128)(2,1)} %slice_dynamic-update-slice_fusion), channel_id=1, source_target_pairs={{0,16},{16,0},{32,48},{48,32},{1,17},{17,1},{33,49},{49,33},{2,18}... | collective-permute-start | bytes 4718600 | tf_op jit(solution)/shard_map/ppermute | solution.py:215
  29.0 16.4 %all-to-all-done = bf16[64,48,128]{2,1,0:T(8,128)(2,1)} async-done(((bf16[64,48,128]{2,1,0:T(8,128)(2,1)}), bf16[64,48,128]{2,1,0:T(8,128)(2,1)}, u32[]{:S(2)}, u32[]{:S(2)}) %all-to-all-start) | async-done | bytes 786464 | tf_op jit(solution)/shard_map/all_to_all | solution.py:22
  45.4 1.4 %reshape.30.own_ref.refs_4_ = bf16[192,2048]{1,0:T(8,128)(2,1)S(1)} reshape(bf16[64,48,128]{2,1,0:T(8,128)(2,1)} %all-to-all-done) | data formatting | bytes 1572864 | tf_op jit(solution)/shard_map/reshape | solution.py:224
  46.8 2.4 %collective-permute-start = (bf16[192,2048]{1,0:T(8,128)(2,1)S(1)}, bf16[192,2048]{1,0:T(8,128)(2,1)S(1)}, u32[]{:S(2)}, u32[]{:S(2)}) collective-permute-start(bf16[192,2048]{1,0:T(8,128)(2,1)S(1)} %reshape.30.own_ref.refs_4_), channel_id=1, source_target_pairs={{0,48},{16,32},{32,16},{48,0},{1,49},{17,33},{33,17},{49,1},{2,50}... | collective-permute-start | bytes 2359304 | tf_op jit(solution)/shard_map/ppermute | solution.py:215
  49.2 17.2 %collective-permute-done.guest_ref.refs_0_ = bf16[192,2048]{1,0:T(8,128)(2,1)S(1)} collective-permute-done((bf16[192,2048]{1,0:T(8,128)(2,1)S(1)}, bf16[192,2048]{1,0:T(8,128)(2,1)S(1)}, u32[]{:S(2)}, u32[]{:S(2)}) %collective-permute-start) | collective-permute-done | bytes 786464 | tf_op jit(solution)/shard_map/ppermute | solution.py:215
  66.4 1.3 %copy-done.7 = bf16[1,256,1024]{2,1,0:T(8,128)(2,1)S(1)} copy-done((bf16[1,256,1024]{2,1,0:T(8,128)(2,1)S(1)}, bf16[1,256,1024]{2,1,0:T(8,128)(2,1)}, u32[]{:S(2)}) %copy-start.7) | copy-done | bytes 524312
  67.8 1.7 %shard_map.111.partial_ref = bf16[384,1536]{1,0:T(8,128)(2,1)S(1)} custom-call(bf16[192,2048]{1,0:T(8,128)(2,1)S(1)} %collective-permute-done.guest_ref.refs_0_, bf16[192,2048]{1,0:T(8,128)(2,1)S(1)} %reshape.30.own_ref.refs_4_, bf16[1024,256]{1,0:T(8,128)(2,1)S(1)} %bitcast.20, bf16[1024,256]{1,0:T(8,128)(2,1)S(1)} %bitcast.23, ...), custom_call_target="tpu_custom_call" | custom-call | flops 1207959552 | bytes 6291456 | tf_op jit(solution)/shard_map/pallas_call | solution.py:232
  69.4 1.9 %collective-permute-start.2 = (bf16[384,1536]{1,0:T(8,128)(2,1)S(1)}, bf16[384,1536]{1,0:T(8,128)(2,1)S(1)}, u32[]{:S(2)}, u32[]{:S(2)}) collective-permute-start(bf16[384,1536]{1,0:T(8,128)(2,1)S(1)} %shard_map.111.partial_ref), channel_id=1, source_target_pairs={{0,1},{1,0},{2,3},{3,2},{4,5},{5,4},{6,7},{7,6},{8,9},{9,8},{10,11... | collective-permute-start | bytes 3538952 | tf_op jit(solution)/shard_map/ppermute | solution.py:218
  71.4 2.8 %collective-permute-done.2.other_ref = bf16[384,1536]{1,0:T(8,128)(2,1)S(1)} collective-permute-done((bf16[384,1536]{1,0:T(8,128)(2,1)S(1)}, bf16[384,1536]{1,0:T(8,128)(2,1)S(1)}, u32[]{:S(2)}, u32[]{:S(2)}) %collective-permute-start.2) | collective-permute-done | bytes 1179680 | tf_op jit(solution)/shard_map/ppermute | solution.py:218
  74.2 2.0 %shard_map.113 = (bf16[208,1024]{1,0:T(8,128)(2,1)S(1)}, bf16[192,512]{1,0:T(8,128)(2,1)S(1)}, bf16[192,512]{1,0:T(8,128)(2,1)S(1)}, bf16[192,512]{1,0:T(8,128)(2,1)S(1)}) custom-call(bf16[384,1536]{1,0:T(8,128)(2,1)S(1)} %shard_map.111.partial_ref, bf16[384,1536]{1,0:T(8,128)(2,1)S(1)} %collective-permute-done.2.other_ref, bf16[1024,256]{1,0:T(8,128)(2,1)S(1)} %bitcast.21, ...), custom_call_target="tpu_custom_call" | custom-call | flops 402653184 | bytes 6291456 | tf_op jit(solution)/shard_map/pallas_call | solution.py:232
  76.2 2.4 %collective-permute-start.3 = (bf16[208,1024]{1,0:T(8,128)(2,1)S(1)}, bf16[208,1024]{1,0:T(8,128)(2,1)S(1)}, u32[]{:S(2)}, u32[]{:S(2)}) collective-permute-start(bf16[208,1024]{1,0:T(8,128)(2,1)S(1)} %get-tuple-element.25), channel_id=1, source_target_pairs={{0,48},{16,32},{32,16},{48,0},{1,49},{17,33},{33,17},{49,1},{2,50}... | collective-permute-start | bytes 1277960 | tf_op jit(solution)/shard_map/ppermute | solution.py:215
  78.6 2.0 %shard_map.112 = (bf16[208,1024]{1,0:T(8,128)(2,1)S(1)}, bf16[192,512]{1,0:T(8,128)(2,1)S(1)}, bf16[192,512]{1,0:T(8,128)(2,1)S(1)}, bf16[192,512]{1,0:T(8,128)(2,1)S(1)}) custom-call(bf16[384,1536]{1,0:T(8,128)(2,1)S(1)} %shard_map.111.partial_ref, bf16[384,1536]{1,0:T(8,128)(2,1)S(1)} %collective-permute-done.2.other_ref, bf16[1024,256]{1,0:T(8,128)(2,1)S(1)} %bitcast.22, ...), custom_call_target="tpu_custom_call" | custom-call | flops 402653184 | bytes 6291456 | tf_op jit(solution)/shard_map/pallas_call | solution.py:232
  80.7 2.2 %shard_map.115 = bf16[3072,256]{1,0:T(8,128)(2,1)} custom-call(bf16[192,2048]{1,0:T(8,128)(2,1)S(1)} %collective-permute-done.guest_ref.refs_0_, bf16[192,512]{1,0:T(8,128)(2,1)S(1)} %get-tuple-element.26.refs_1_, bf16[192,512]{1,0:T(8,128)(2,1)S(1)} %get-tuple-element.27.refs_2_, bf16[192,512]{1,0:T(8,128)(2,1)S(1)} %get-tuple-element.28.refs_3_, ...), custom_call_target="tpu_custom_call" | custom-call | flops 603979776 | bytes 6291456 | tf_op jit(solution)/shard_map/pallas_call | solution.py:232
  82.9 1.9 %collective-permute-start.4 = (bf16[3072,256]{1,0:T(8,128)(2,1)}, bf16[3072,256]{1,0:T(8,128)(2,1)}, u32[]{:S(2)}, u32[]{:S(2)}) collective-permute-start(bf16[3072,256]{1,0:T(8,128)(2,1)} %shard_map.115), channel_id=1, source_target_pairs={{0,16},{16,0},{32,48},{48,32},{1,17},{17,1},{33,49},{49,33},{2,18}... | collective-permute-start | bytes 4718600 | tf_op jit(solution)/shard_map/ppermute | solution.py:215
  84.8 6.3 %collective-permute-done.3 = bf16[208,1024]{1,0:T(8,128)(2,1)S(1)} collective-permute-done((bf16[208,1024]{1,0:T(8,128)(2,1)S(1)}, bf16[208,1024]{1,0:T(8,128)(2,1)S(1)}, u32[]{:S(2)}, u32[]{:S(2)}) %collective-permute-start.3) | collective-permute-done | bytes 426016 | tf_op jit(solution)/shard_map/ppermute | solution.py:215
  91.8 1.2 copy.20
  93.0 10.0 %all-to-all-start.1 = ((bf16[64,13,2,128]{3,2,1,0:T(2,128)(2,1)}), bf16[64,13,2,128]{3,2,1,0:T(2,128)(2,1)}, u32[]{:S(2)}, u32[]{:S(2)}) async-start(bf16[64,13,2,128]{3,2,1,0:T(2,128)(2,1)} %copy.20), calls=%async_computation.1 | async-start | bytes 851968 | tf_op jit(solution)/shard_map/all_to_all | solution.py:22
  103.1 1.1 copy-done.1
  104.2 1.1 copy-done.5
  110.1 9.9 %all-to-all-done.1 = bf16[64,13,2,128]{3,2,1,0:T(2,128)(2,1)} async-done(((bf16[64,13,2,128]{3,2,1,0:T(2,128)(2,1)}), bf16[64,13,2,128]{3,2,1,0:T(2,128)(2,1)}, u32[]{:S(2)}, u32[]{:S(2)}) %all-to-all-start.1) | async-done | bytes 426016 | tf_op jit(solution)/shard_map/all_to_all | solution.py:22
  120.0 1.1 copy.21
  123.1 2.7 %shard_map.116 = (bf16[1,1024,256]{2,1,0:T(8,128)(2,1)}, bf16[1,1024,256]{2,1,0:T(8,128)(2,1)}, bf16[1,256,1024]{2,1,0:T(8,128)(2,1)}) custom-call(f32[3072,256]{1,0:T(8,128)S(1)} %shard_map.114.mine_ref, bf16[3072,256]{1,0:T(8,128)(2,1)} %collective-permute-done.4.theirs_ref), custom_call_target="tpu_custom_call" | custom-call | bytes 6291456 | tf_op jit(solution)/shard_map/pallas_call | solution.py:232
  (73 shorter events, 14.6 us)
Async XLA Ops:
  0.6 21.2 %copy-start.2 = (bf16[1,1024,256]{2,1,0:T(8,128)(2,1)S(1)}, bf16[1,1024,256]{2,1,0:T(8,128)(2,1)}, u32[]{:S(2)}) copy-start(bf16[1,1024,256]{2,1,0:T(8,128)(2,1)} %param.11) | copy-start | bytes 1572868
  0.6 22.1 %copy-start.3 = (bf16[1,1024,256]{2,1,0:T(8,128)(2,1)S(1)}, bf16[1,1024,256]{2,1,0:T(8,128)(2,1)}, u32[]{:S(2)}) copy-start(bf16[1,1024,256]{2,1,0:T(8,128)(2,1)} %param.12) | copy-start | bytes 1572868
  4.9 18.7 %copy-start.6 = (bf16[1,256,1024]{2,1,0:T(8,128)(2,1)S(1)}, bf16[1,256,1024]{2,1,0:T(8,128)(2,1)}, u32[]{:S(2)}) copy-start(bf16[1,256,1024]{2,1,0:T(8,128)(2,1)} %param.13) | copy-start | bytes 1572868
  4.9 40.5 %all-to-all-start = ((bf16[64,48,128]{2,1,0:T(8,128)(2,1)}), bf16[64,48,128]{2,1,0:T(8,128)(2,1)}, u32[]{:S(2)}, u32[]{:S(2)}) async-start(bf16[64,48,128]{2,1,0:T(8,128)(2,1)} %bitcast.4), calls=%async_computation | async-start | bytes 1572864 | tf_op jit(solution)/shard_map/all_to_all | solution.py:22
  26.2 40.2 %collective-permute-start.1 = (bf16[3072,256]{1,0:T(8,128)(2,1)}, bf16[3072,256]{1,0:T(8,128)(2,1)S(1)}, u32[]{:S(2)}, u32[]{:S(2)}) collective-permute-start(bf16[3072,256]{1,0:T(8,128)(2,1)} %slice_dynamic-update-slice_fusion), channel_id=1, source_target_pairs={{0,16},{16,0},{32,48},{48,32},{1,17},{17,1},{33,49},{49,33},{2,18}... | collective-permute-start | bytes 4718600 | tf_op jit(solution)/shard_map/ppermute | solution.py:215
  46.8 33.8 %copy-start = (bf16[192,2048]{1,0:T(8,128)(2,1)}, bf16[192,2048]{1,0:T(8,128)(2,1)S(1)}, u32[]{:S(2)}) copy-start(bf16[192,2048]{1,0:T(8,128)(2,1)S(1)} %reshape.30.own_ref.refs_4_) | copy-start | bytes 2359300
  46.8 19.6 %collective-permute-start = (bf16[192,2048]{1,0:T(8,128)(2,1)S(1)}, bf16[192,2048]{1,0:T(8,128)(2,1)S(1)}, u32[]{:S(2)}, u32[]{:S(2)}) collective-permute-start(bf16[192,2048]{1,0:T(8,128)(2,1)S(1)} %reshape.30.own_ref.refs_4_), channel_id=1, source_target_pairs={{0,48},{16,32},{32,16},{48,0},{1,49},{17,33},{33,17},{49,1},{2,50}... | collective-permute-start | bytes 2359304 | tf_op jit(solution)/shard_map/ppermute | solution.py:215
  66.4 14.2 %copy-start.4 = (bf16[192,2048]{1,0:T(8,128)(2,1)}, bf16[192,2048]{1,0:T(8,128)(2,1)S(1)}, u32[]{:S(2)}) copy-start(bf16[192,2048]{1,0:T(8,128)(2,1)S(1)} %collective-permute-done.guest_ref.refs_0_) | copy-start | bytes 2359300
  66.4 1.3 %copy-start.7 = (bf16[1,256,1024]{2,1,0:T(8,128)(2,1)S(1)}, bf16[1,256,1024]{2,1,0:T(8,128)(2,1)}, u32[]{:S(2)}) copy-start(bf16[1,256,1024]{2,1,0:T(8,128)(2,1)} %param.13) | copy-start | bytes 1572868
  69.4 4.7 %collective-permute-start.2 = (bf16[384,1536]{1,0:T(8,128)(2,1)S(1)}, bf16[384,1536]{1,0:T(8,128)(2,1)S(1)}, u32[]{:S(2)}, u32[]{:S(2)}) collective-permute-start(bf16[384,1536]{1,0:T(8,128)(2,1)S(1)} %shard_map.111.partial_ref), channel_id=1, source_target_pairs={{0,1},{1,0},{2,3},{3,2},{4,5},{5,4},{6,7},{7,6},{8,9},{9,8},{10,11... | collective-permute-start | bytes 3538952 | tf_op jit(solution)/shard_map/ppermute | solution.py:218
  76.2 4.5 %copy-start.8 = (bf16[192,512]{1,0:T(8,128)(2,1)}, bf16[192,512]{1,0:T(8,128)(2,1)S(1)}, u32[]{:S(2)}) copy-start(bf16[192,512]{1,0:T(8,128)(2,1)S(1)} %get-tuple-element.26.refs_1_) | copy-start | bytes 589828
  76.2 4.5 %copy-start.10 = (bf16[192,512]{1,0:T(8,128)(2,1)}, bf16[192,512]{1,0:T(8,128)(2,1)S(1)}, u32[]{:S(2)}) copy-start(bf16[192,512]{1,0:T(8,128)(2,1)S(1)} %get-tuple-element.27.refs_2_) | copy-start | bytes 589828
  76.2 4.5 %copy-start.12 = (bf16[192,512]{1,0:T(8,128)(2,1)}, bf16[192,512]{1,0:T(8,128)(2,1)S(1)}, u32[]{:S(2)}) copy-start(bf16[192,512]{1,0:T(8,128)(2,1)S(1)} %get-tuple-element.28.refs_3_) | copy-start | bytes 589828
  76.2 14.9 %collective-permute-start.3 = (bf16[208,1024]{1,0:T(8,128)(2,1)S(1)}, bf16[208,1024]{1,0:T(8,128)(2,1)S(1)}, u32[]{:S(2)}, u32[]{:S(2)}) collective-permute-start(bf16[208,1024]{1,0:T(8,128)(2,1)S(1)} %get-tuple-element.25), channel_id=1, source_target_pairs={{0,48},{16,32},{32,16},{48,0},{1,49},{17,33},{33,17},{49,1},{2,50}... | collective-permute-start | bytes 1277960 | tf_op jit(solution)/shard_map/ppermute | solution.py:215
  80.6 2.3 %copy-start.14 = (bf16[192,512]{1,0:T(8,128)(2,1)}, bf16[192,512]{1,0:T(8,128)(2,1)S(1)}, u32[]{:S(2)}) copy-start(bf16[192,512]{1,0:T(8,128)(2,1)S(1)} %get-tuple-element.29.refs_5_) | copy-start | bytes 589828
  80.6 2.3 %copy-start.16 = (bf16[192,512]{1,0:T(8,128)(2,1)}, bf16[192,512]{1,0:T(8,128)(2,1)S(1)}, u32[]{:S(2)}) copy-start(bf16[192,512]{1,0:T(8,128)(2,1)S(1)} %get-tuple-element.30.refs_6_) | copy-start | bytes 589828
  80.6 2.3 %copy-start.18 = (bf16[192,512]{1,0:T(8,128)(2,1)}, bf16[192,512]{1,0:T(8,128)(2,1)S(1)}, u32[]{:S(2)}) copy-start(bf16[192,512]{1,0:T(8,128)(2,1)S(1)} %get-tuple-element.31.refs_7_) | copy-start | bytes 589828
  82.9 40.2 %collective-permute-start.4 = (bf16[3072,256]{1,0:T(8,128)(2,1)}, bf16[3072,256]{1,0:T(8,128)(2,1)}, u32[]{:S(2)}, u32[]{:S(2)}) collective-permute-start(bf16[3072,256]{1,0:T(8,128)(2,1)} %shard_map.115), channel_id=1, source_target_pairs={{0,16},{16,0},{32,48},{48,32},{1,17},{17,1},{33,49},{49,33},{2,18}... | collective-permute-start | bytes 4718600 | tf_op jit(solution)/shard_map/ppermute | solution.py:215
  91.5 11.6 %copy-start.9 = (bf16[192,512]{1,0:T(8,128)(2,1)S(1)}, bf16[192,512]{1,0:T(8,128)(2,1)}, u32[]{:S(2)}) copy-start(bf16[192,512]{1,0:T(8,128)(2,1)} %copy-done.8) | copy-start | bytes 589828
  91.5 11.6 %copy-start.11 = (bf16[192,512]{1,0:T(8,128)(2,1)S(1)}, bf16[192,512]{1,0:T(8,128)(2,1)}, u32[]{:S(2)}) copy-start(bf16[192,512]{1,0:T(8,128)(2,1)} %copy-done.10) | copy-start | bytes 589828
  93.0 27.0 %all-to-all-start.1 = ((bf16[64,13,2,128]{3,2,1,0:T(2,128)(2,1)}), bf16[64,13,2,128]{3,2,1,0:T(2,128)(2,1)}, u32[]{:S(2)}, u32[]{:S(2)}) async-start(bf16[64,13,2,128]{3,2,1,0:T(2,128)(2,1)} %copy.20), calls=%async_computation.1 | async-start | bytes 851968 | tf_op jit(solution)/shard_map/all_to_all | solution.py:22
  103.1 1.1 copy-start.1
  104.2 1.1 copy-start.5
  110.1 11.6 %copy-start.23 = (f32[8,2]{0,1:T(2,128)S(1)}, f32[8,2]{0,1:T(2,128)}, u32[]{:S(2)}) copy-start(f32[8,2]{0,1:T(2,128)} %param.10) | copy-start | bytes 196
  (8 other events, 6.6 us)

commit v7 on v6

--- a/solution.py
+++ b/solution.py
@@ -163,17 +163,35 @@
         )
 
 
-def settle_kernel(mine_ref, theirs_ref, gate_ref, up_ref, down_ref):
-    width, hid = gate_ref.shape[1:]
+def settle_kernel(
+    mine_ref, theirs_hbm, gate_hbm, up_hbm, down_hbm, theirs_ref, wide_ref, tall_ref, in_sem, out_sem
+):
+    width, hid = gate_hbm.shape[1:]
+    loads = []
+    for k in range(3):
+        rows = pl.ds(k * width, width)
+        loads.append(
+            pltpu.make_async_copy(theirs_hbm.at[rows, :], theirs_ref.at[rows, :], in_sem.at[k])
+        )
+        loads[-1].start()
 
     def total(start, size):
         rows = slice(start, start + size)
         return (mine_ref[rows, :] + theirs_ref[rows, :].astype(jnp.float32)).astype(jnp.bfloat16)
 
-    gate_ref[0] = total(0, width)
-    up_ref[0] = total(width, width)
+    stores = []
+    for k, out in enumerate((gate_hbm, up_hbm)):
+        loads[k].wait()
+        wide_ref[k] = total(k * width, width)
+        stores.append(pltpu.make_async_copy(wide_ref.at[k], out.at[0], out_sem.at[k]))
+        stores[-1].start()
+    loads[2].wait()
     for k in range(width // hid):
-        down_ref[0, :, k * hid : (k + 1) * hid] = total(2 * width + k * hid, hid)
+        tall_ref[:, k * hid : (k + 1) * hid] = total(2 * width + k * hid, hid)
+    stores.append(pltpu.make_async_copy(tall_ref, down_hbm.at[0], out_sem.at[2]))
+    stores[-1].start()
+    for store in stores:
+        store.wait()
 
 
 def per_device(tokens, out_grad, expert_ids, gate_probs, w_gate, w_up, w_down):
@@ -198,7 +216,6 @@
             pl.BlockSpec(memory_space=pltpu.VMEM),
         ),
         scratch_shapes=[pltpu.VMEM((experts, rows_out, LANES), jnp.float32)],
-        compiler_params=pltpu.CompilerParams(vmem_limit_bytes=40 << 20),
     )(expert_ids.T, gate_probs.T, tokens, out_grad)
     send = send.reshape(experts * nz, rows_out, LANES)
     slot_names = jnp.arange(slots, dtype=jnp.int32)
@@ -228,12 +245,14 @@
     vmem = pl.BlockSpec(memory_space=pltpu.VMEM)
     params = pltpu.CompilerParams(vmem_limit_bytes=16 << 20)
 
-    def call(kernel, outs, args, scratch=(), flops=0):
+    hbm = pl.BlockSpec(memory_space=pl.ANY)
+
+    def call(kernel, outs, args, scratch=(), flops=0, far=(), far_out=False):
         return pl.pallas_call(
             kernel,
             out_shape=tuple(jax.ShapeDtypeStruct(s, d) for s, d in outs),
-            in_specs=[vmem] * len(args),
-            out_specs=tuple(vmem for _ in outs),
+            in_specs=[hbm if k in far else vmem for k in range(len(args))],
+            out_specs=tuple(hbm if far_out else vmem for _ in outs),
             scratch_shapes=list(scratch),
             compiler_params=params,
             cost_estimate=pl.CostEstimate(flops=flops, bytes_accessed=6 << 20, transcendentals=0),
@@ -282,6 +301,15 @@
         settle_kernel,
         [((1, width, hid), bf16), ((1, width, hid), bf16), ((1, hid, width), bf16)],
         (mine, theirs),
+        [
+            pltpu.VMEM((3 * width, hid), bf16),
+            pltpu.VMEM((2, width, hid), bf16),
+            pltpu.VMEM((hid, width), bf16),
+            pltpu.SemaphoreType.DMA((3,)),
+            pltpu.SemaphoreType.DMA((3,)),
+        ],
+        far=(1,),
+        far_out=True,
     )
 
     data = back[:part_rows].reshape(experts * nz, CAP * chunks, LANES)

time: 128 us -> 126 us (0.984)
  local copies, waits for them, and re-layouts: 18.9 us -> 16 us
    unnamed x55 -> x49, local copies, waits for them, and re-layouts: 13.9 us -> 11 us
  transfers between devices with their start and end apart: 7 -> 7, of which waited for: 5 -> 5; matrix products, arithmetic and copies ran while one was open for 8% -> 9% of each run, Pallas kernels for 4% -> 4%
where the time goes in v7:
time: 126 us; the launch traced here: 123 us
  waiting for transfers between devices  52.7 us (42%)
  starting transfers between devices  38.3 us (30%)
  local copies, waits for them, and re-layouts  16 us (13%)
  Pallas kernels  13.4 us (11%)
    all_to_all x2, starting transfers between devices, exchange(): return lax.all_to_all(block, axes, split_axis=0, concat_axis=0, tiled=True)  27 us
    all_to_all x2, waiting for transfers between devices, exchange(): return lax.all_to_all(block, axes, split_axis=0, concat_axis=0, tiled=True)  26.3 us
    ppermute x4, waiting for transfers between devices, meet(): return lax.ppermute(block, 'x', [(i, i ^ mask) for i in range(nx)])  23.6 us
    pallas_call x6, Pallas kernels, call(): pl.pallas_call(kernel, out_shape=tuple((jax.ShapeDtypeStruct(s, d) for s,...  11.2 us
    unnamed x49, local copies, waits for them, and re-layouts  11 us
    ppermute x4, starting transfers between devices, meet(): return lax.ppermute(block, 'x', [(i, i ^ mask) for i in range(nx)])  9.41 us
    ppermute x1, waiting for transfers between devices, swap(): return lax.ppermute(block, 'dp', [(0, 1), (1, 0)])  2.81 us
  transfers between devices with their start and end apart: 7, of which 5 were waited for; matrix products, arithmetic and copies ran while one was open for 9% of the time, Pallas kernels for 4%

profile of v7, /device:TPU:6, one launch (start us, length us, event | category | flops | bytes accessed | tf_op | source)
XLA Modules:
  0.0 123.4 jit_solution(6383136986935862768)
XLA Ops:
  0.7 2.2 %shard_map.110 = (bf16[8,8,48,128]{3,2,1,0:T(8,128)(2,1)}, s32[2,8]{1,0:T(2,128)}) custom-call(s32[2,8]{1,0:T(2,128)} %bitcast.37, f32[2,8]{1,0:T(2,128)} %bitcast.34, bf16[8,1024]{1,0:T(8,128)(2,1)} %tokens_ref.1, bf16[8,1024]{1,0:T(8,128)(2,1)} %out_grad_ref.1), custom_call_target="tpu_custom_call" | custom-call | tf_op jit(solution)/shard_map/pallas_call | solution.py:207
  2.8 16.9 %all-to-all-start = ((bf16[64,48,128]{2,1,0:T(8,128)(2,1)}), bf16[64,48,128]{2,1,0:T(8,128)(2,1)}, u32[]{:S(2)}, u32[]{:S(2)}) async-start(bf16[64,48,128]{2,1,0:T(8,128)(2,1)} %bitcast.33), calls=%async_computation | async-start | bytes 1572864 | tf_op jit(solution)/shard_map/all_to_all | solution.py:22
  24.2 2.7 %collective-permute-start.1 = (bf16[3072,256]{1,0:T(8,128)(2,1)}, bf16[3072,256]{1,0:T(8,128)(2,1)S(1)}, u32[]{:S(2)}, u32[]{:S(2)}) collective-permute-start(bf16[3072,256]{1,0:T(8,128)(2,1)} %slice_dynamic-update-slice_fusion), channel_id=1, source_target_pairs={{0,16},{16,0},{32,48},{48,32},{1,17},{17,1},{33,49},{49,33},{2,18}... | collective-permute-start | bytes 4718600 | tf_op jit(solution)/shard_map/ppermute | solution.py:232
  26.9 16.4 %all-to-all-done = bf16[64,48,128]{2,1,0:T(8,128)(2,1)} async-done(((bf16[64,48,128]{2,1,0:T(8,128)(2,1)}), bf16[64,48,128]{2,1,0:T(8,128)(2,1)}, u32[]{:S(2)}, u32[]{:S(2)}) %all-to-all-start) | async-done | bytes 786464 | tf_op jit(solution)/shard_map/all_to_all | solution.py:22
  43.3 1.4 %reshape.30.own_ref.refs_4_ = bf16[192,2048]{1,0:T(8,128)(2,1)S(1)} reshape(bf16[64,48,128]{2,1,0:T(8,128)(2,1)} %all-to-all-done) | data formatting | bytes 1572864 | tf_op jit(solution)/shard_map/reshape | solution.py:241
  44.8 2.4 %collective-permute-start = (bf16[192,2048]{1,0:T(8,128)(2,1)S(1)}, bf16[192,2048]{1,0:T(8,128)(2,1)S(1)}, u32[]{:S(2)}, u32[]{:S(2)}) collective-permute-start(bf16[192,2048]{1,0:T(8,128)(2,1)S(1)} %reshape.30.own_ref.refs_4_), channel_id=1, source_target_pairs={{0,48},{16,32},{32,16},{48,0},{1,49},{17,33},{33,17},{49,1},{2,50}... | collective-permute-start | bytes 2359304 | tf_op jit(solution)/shard_map/ppermute | solution.py:232
  47.2 17.2 %collective-permute-done.guest_ref.refs_0_ = bf16[192,2048]{1,0:T(8,128)(2,1)S(1)} collective-permute-done((bf16[192,2048]{1,0:T(8,128)(2,1)S(1)}, bf16[192,2048]{1,0:T(8,128)(2,1)S(1)}, u32[]{:S(2)}, u32[]{:S(2)}) %collective-permute-start) | collective-permute-done | bytes 786464 | tf_op jit(solution)/shard_map/ppermute | solution.py:232
  64.4 1.3 %copy-done.7 = bf16[1,256,1024]{2,1,0:T(8,128)(2,1)S(1)} copy-done((bf16[1,256,1024]{2,1,0:T(8,128)(2,1)S(1)}, bf16[1,256,1024]{2,1,0:T(8,128)(2,1)}, u32[]{:S(2)}) %copy-start.7) | copy-done | bytes 524312
  65.7 1.7 %shard_map.111.partial_ref = bf16[384,1536]{1,0:T(8,128)(2,1)S(1)} custom-call(bf16[192,2048]{1,0:T(8,128)(2,1)S(1)} %collective-permute-done.guest_ref.refs_0_, bf16[192,2048]{1,0:T(8,128)(2,1)S(1)} %reshape.30.own_ref.refs_4_, bf16[1024,256]{1,0:T(8,128)(2,1)S(1)} %bitcast.20, bf16[1024,256]{1,0:T(8,128)(2,1)S(1)} %bitcast.23, ...), custom_call_target="tpu_custom_call" | custom-call | flops 1207959552 | bytes 6291456 | tf_op jit(solution)/shard_map/pallas_call | solution.py:251
  67.4 1.9 %collective-permute-start.2 = (bf16[384,1536]{1,0:T(8,128)(2,1)S(1)}, bf16[384,1536]{1,0:T(8,128)(2,1)S(1)}, u32[]{:S(2)}, u32[]{:S(2)}) collective-permute-start(bf16[384,1536]{1,0:T(8,128)(2,1)S(1)} %shard_map.111.partial_ref), channel_id=1, source_target_pairs={{0,1},{1,0},{2,3},{3,2},{4,5},{5,4},{6,7},{7,6},{8,9},{9,8},{10,11... | collective-permute-start | bytes 3538952 | tf_op jit(solution)/shard_map/ppermute | solution.py:235
  69.3 2.8 %collective-permute-done.2.other_ref = bf16[384,1536]{1,0:T(8,128)(2,1)S(1)} collective-permute-done((bf16[384,1536]{1,0:T(8,128)(2,1)S(1)}, bf16[384,1536]{1,0:T(8,128)(2,1)S(1)}, u32[]{:S(2)}, u32[]{:S(2)}) %collective-permute-start.2) | collective-permute-done | bytes 1179680 | tf_op jit(solution)/shard_map/ppermute | solution.py:235
  72.1 2.0 %shard_map.113 = (bf16[208,1024]{1,0:T(8,128)(2,1)S(1)}, bf16[192,512]{1,0:T(8,128)(2,1)S(1)}, bf16[192,512]{1,0:T(8,128)(2,1)S(1)}, bf16[192,512]{1,0:T(8,128)(2,1)S(1)}) custom-call(bf16[384,1536]{1,0:T(8,128)(2,1)S(1)} %shard_map.111.partial_ref, bf16[384,1536]{1,0:T(8,128)(2,1)S(1)} %collective-permute-done.2.other_ref, bf16[1024,256]{1,0:T(8,128)(2,1)S(1)} %bitcast.21, ...), custom_call_target="tpu_custom_call" | custom-call | flops 402653184 | bytes 6291456 | tf_op jit(solution)/shard_map/pallas_call | solution.py:251
  74.2 2.4 %collective-permute-start.3 = (bf16[208,1024]{1,0:T(8,128)(2,1)S(1)}, bf16[208,1024]{1,0:T(8,128)(2,1)S(1)}, u32[]{:S(2)}, u32[]{:S(2)}) collective-permute-start(bf16[208,1024]{1,0:T(8,128)(2,1)S(1)} %get-tuple-element.25), channel_id=1, source_target_pairs={{0,48},{16,32},{32,16},{48,0},{1,49},{17,33},{33,17},{49,1},{2,50}... | collective-permute-start | bytes 1277960 | tf_op jit(solution)/shard_map/ppermute | solution.py:232
  76.6 2.0 %shard_map.112 = (bf16[208,1024]{1,0:T(8,128)(2,1)S(1)}, bf16[192,512]{1,0:T(8,128)(2,1)S(1)}, bf16[192,512]{1,0:T(8,128)(2,1)S(1)}, bf16[192,512]{1,0:T(8,128)(2,1)S(1)}) custom-call(bf16[384,1536]{1,0:T(8,128)(2,1)S(1)} %shard_map.111.partial_ref, bf16[384,1536]{1,0:T(8,128)(2,1)S(1)} %collective-permute-done.2.other_ref, bf16[1024,256]{1,0:T(8,128)(2,1)S(1)} %bitcast.22, ...), custom_call_target="tpu_custom_call" | custom-call | flops 402653184 | bytes 6291456 | tf_op jit(solution)/shard_map/pallas_call | solution.py:251
  78.6 2.2 %shard_map.115 = bf16[3072,256]{1,0:T(8,128)(2,1)} custom-call(bf16[192,2048]{1,0:T(8,128)(2,1)S(1)} %collective-permute-done.guest_ref.refs_0_, bf16[192,512]{1,0:T(8,128)(2,1)S(1)} %get-tuple-element.26.refs_1_, bf16[192,512]{1,0:T(8,128)(2,1)S(1)} %get-tuple-element.27.refs_2_, bf16[192,512]{1,0:T(8,128)(2,1)S(1)} %get-tuple-element.28.refs_3_, ...), custom_call_target="tpu_custom_call" | custom-call | flops 603979776 | bytes 6291456 | tf_op jit(solution)/shard_map/pallas_call | solution.py:251
  80.9 1.9 %collective-permute-start.4 = (bf16[3072,256]{1,0:T(8,128)(2,1)}, bf16[3072,256]{1,0:T(8,128)(2,1)}, u32[]{:S(2)}, u32[]{:S(2)}) collective-permute-start(bf16[3072,256]{1,0:T(8,128)(2,1)} %shard_map.115), channel_id=1, source_target_pairs={{0,16},{16,0},{32,48},{48,32},{1,17},{17,1},{33,49},{49,33},{2,18}... | collective-permute-start | bytes 4718600 | tf_op jit(solution)/shard_map/ppermute | solution.py:232
  82.8 6.3 %collective-permute-done.3 = bf16[208,1024]{1,0:T(8,128)(2,1)S(1)} collective-permute-done((bf16[208,1024]{1,0:T(8,128)(2,1)S(1)}, bf16[208,1024]{1,0:T(8,128)(2,1)S(1)}, u32[]{:S(2)}, u32[]{:S(2)}) %collective-permute-start.3) | collective-permute-done | bytes 426016 | tf_op jit(solution)/shard_map/ppermute | solution.py:232
  89.8 1.2 copy.20
  91.0 10.0 %all-to-all-start.1 = ((bf16[64,13,2,128]{3,2,1,0:T(2,128)(2,1)}), bf16[64,13,2,128]{3,2,1,0:T(2,128)(2,1)}, u32[]{:S(2)}, u32[]{:S(2)}) async-start(bf16[64,13,2,128]{3,2,1,0:T(2,128)(2,1)} %copy.20), calls=%async_computation.1 | async-start | bytes 851968 | tf_op jit(solution)/shard_map/all_to_all | solution.py:22
  101.1 1.1 copy-done.1
  102.2 1.1 copy-done.5
  108.1 9.8 %all-to-all-done.1 = bf16[64,13,2,128]{3,2,1,0:T(2,128)(2,1)} async-done(((bf16[64,13,2,128]{3,2,1,0:T(2,128)(2,1)}), bf16[64,13,2,128]{3,2,1,0:T(2,128)(2,1)}, u32[]{:S(2)}, u32[]{:S(2)}) %all-to-all-start.1) | async-done | bytes 426016 | tf_op jit(solution)/shard_map/all_to_all | solution.py:22
  117.9 1.1 copy.21
  121.0 2.3 %shard_map.116 = (bf16[1,1024,256]{2,1,0:T(8,128)(2,1)}, bf16[1,1024,256]{2,1,0:T(8,128)(2,1)}, bf16[1,256,1024]{2,1,0:T(8,128)(2,1)}) custom-call(f32[3072,256]{1,0:T(8,128)S(1)} %shard_map.114.mine_ref, bf16[3072,256]{1,0:T(8,128)(2,1)} %collective-permute-done.4.theirs_hbm), custom_call_target="tpu_custom_call" | custom-call | bytes 6291456 | tf_op jit(solution)/shard_map/pallas_call | solution.py:251
  (67 shorter events, 11.7 us)
Async XLA Ops:
  0.6 19.2 %copy-start.2 = (bf16[1,1024,256]{2,1,0:T(8,128)(2,1)S(1)}, bf16[1,1024,256]{2,1,0:T(8,128)(2,1)}, u32[]{:S(2)}) copy-start(bf16[1,1024,256]{2,1,0:T(8,128)(2,1)} %param.11) | copy-start | bytes 1572868
  0.6 20.0 %copy-start.3 = (bf16[1,1024,256]{2,1,0:T(8,128)(2,1)S(1)}, bf16[1,1024,256]{2,1,0:T(8,128)(2,1)}, u32[]{:S(2)}) copy-start(bf16[1,1024,256]{2,1,0:T(8,128)(2,1)} %param.12) | copy-start | bytes 1572868
  2.8 18.6 %copy-start.6 = (bf16[1,256,1024]{2,1,0:T(8,128)(2,1)S(1)}, bf16[1,256,1024]{2,1,0:T(8,128)(2,1)}, u32[]{:S(2)}) copy-start(bf16[1,256,1024]{2,1,0:T(8,128)(2,1)} %param.13) | copy-start | bytes 1572868
  2.8 40.5 %all-to-all-start = ((bf16[64,48,128]{2,1,0:T(8,128)(2,1)}), bf16[64,48,128]{2,1,0:T(8,128)(2,1)}, u32[]{:S(2)}, u32[]{:S(2)}) async-start(bf16[64,48,128]{2,1,0:T(8,128)(2,1)} %bitcast.33), calls=%async_computation | async-start | bytes 1572864 | tf_op jit(solution)/shard_map/all_to_all | solution.py:22
  24.2 40.2 %collective-permute-start.1 = (bf16[3072,256]{1,0:T(8,128)(2,1)}, bf16[3072,256]{1,0:T(8,128)(2,1)S(1)}, u32[]{:S(2)}, u32[]{:S(2)}) collective-permute-start(bf16[3072,256]{1,0:T(8,128)(2,1)} %slice_dynamic-update-slice_fusion), channel_id=1, source_target_pairs={{0,16},{16,0},{32,48},{48,32},{1,17},{17,1},{33,49},{49,33},{2,18}... | collective-permute-start | bytes 4718600 | tf_op jit(solution)/shard_map/ppermute | solution.py:232
  44.8 33.8 %copy-start = (bf16[192,2048]{1,0:T(8,128)(2,1)}, bf16[192,2048]{1,0:T(8,128)(2,1)S(1)}, u32[]{:S(2)}) copy-start(bf16[192,2048]{1,0:T(8,128)(2,1)S(1)} %reshape.30.own_ref.refs_4_) | copy-start | bytes 2359300
  44.8 19.6 %collective-permute-start = (bf16[192,2048]{1,0:T(8,128)(2,1)S(1)}, bf16[192,2048]{1,0:T(8,128)(2,1)S(1)}, u32[]{:S(2)}, u32[]{:S(2)}) collective-permute-start(bf16[192,2048]{1,0:T(8,128)(2,1)S(1)} %reshape.30.own_ref.refs_4_), channel_id=1, source_target_pairs={{0,48},{16,32},{32,16},{48,0},{1,49},{17,33},{33,17},{49,1},{2,50}... | collective-permute-start | bytes 2359304 | tf_op jit(solution)/shard_map/ppermute | solution.py:232
  64.4 14.2 %copy-start.4 = (bf16[192,2048]{1,0:T(8,128)(2,1)}, bf16[192,2048]{1,0:T(8,128)(2,1)S(1)}, u32[]{:S(2)}) copy-start(bf16[192,2048]{1,0:T(8,128)(2,1)S(1)} %collective-permute-done.guest_ref.refs_0_) | copy-start | bytes 2359300
  64.4 1.3 %copy-start.7 = (bf16[1,256,1024]{2,1,0:T(8,128)(2,1)S(1)}, bf16[1,256,1024]{2,1,0:T(8,128)(2,1)}, u32[]{:S(2)}) copy-start(bf16[1,256,1024]{2,1,0:T(8,128)(2,1)} %param.13) | copy-start | bytes 1572868
  67.4 4.7 %collective-permute-start.2 = (bf16[384,1536]{1,0:T(8,128)(2,1)S(1)}, bf16[384,1536]{1,0:T(8,128)(2,1)S(1)}, u32[]{:S(2)}, u32[]{:S(2)}) collective-permute-start(bf16[384,1536]{1,0:T(8,128)(2,1)S(1)} %shard_map.111.partial_ref), channel_id=1, source_target_pairs={{0,1},{1,0},{2,3},{3,2},{4,5},{5,4},{6,7},{7,6},{8,9},{9,8},{10,11... | collective-permute-start | bytes 3538952 | tf_op jit(solution)/shard_map/ppermute | solution.py:235
  74.1 4.5 %copy-start.8 = (bf16[192,512]{1,0:T(8,128)(2,1)}, bf16[192,512]{1,0:T(8,128)(2,1)S(1)}, u32[]{:S(2)}) copy-start(bf16[192,512]{1,0:T(8,128)(2,1)S(1)} %get-tuple-element.26.refs_1_) | copy-start | bytes 589828
  74.1 4.5 %copy-start.10 = (bf16[192,512]{1,0:T(8,128)(2,1)}, bf16[192,512]{1,0:T(8,128)(2,1)S(1)}, u32[]{:S(2)}) copy-start(bf16[192,512]{1,0:T(8,128)(2,1)S(1)} %get-tuple-element.27.refs_2_) | copy-start | bytes 589828
  74.2 4.5 %copy-start.12 = (bf16[192,512]{1,0:T(8,128)(2,1)}, bf16[192,512]{1,0:T(8,128)(2,1)S(1)}, u32[]{:S(2)}) copy-start(bf16[192,512]{1,0:T(8,128)(2,1)S(1)} %get-tuple-element.28.refs_3_) | copy-start | bytes 589828
  74.2 14.9 %collective-permute-start.3 = (bf16[208,1024]{1,0:T(8,128)(2,1)S(1)}, bf16[208,1024]{1,0:T(8,128)(2,1)S(1)}, u32[]{:S(2)}, u32[]{:S(2)}) collective-permute-start(bf16[208,1024]{1,0:T(8,128)(2,1)S(1)} %get-tuple-element.25), channel_id=1, source_target_pairs={{0,48},{16,32},{32,16},{48,0},{1,49},{17,33},{33,17},{49,1},{2,50}... | collective-permute-start | bytes 1277960 | tf_op jit(solution)/shard_map/ppermute | solution.py:232
  78.5 2.3 %copy-start.14 = (bf16[192,512]{1,0:T(8,128)(2,1)}, bf16[192,512]{1,0:T(8,128)(2,1)S(1)}, u32[]{:S(2)}) copy-start(bf16[192,512]{1,0:T(8,128)(2,1)S(1)} %get-tuple-element.29.refs_5_) | copy-start | bytes 589828
  78.6 2.3 %copy-start.16 = (bf16[192,512]{1,0:T(8,128)(2,1)}, bf16[192,512]{1,0:T(8,128)(2,1)S(1)}, u32[]{:S(2)}) copy-start(bf16[192,512]{1,0:T(8,128)(2,1)S(1)} %get-tuple-element.30.refs_6_) | copy-start | bytes 589828
  78.6 2.3 %copy-start.18 = (bf16[192,512]{1,0:T(8,128)(2,1)}, bf16[192,512]{1,0:T(8,128)(2,1)S(1)}, u32[]{:S(2)}) copy-start(bf16[192,512]{1,0:T(8,128)(2,1)S(1)} %get-tuple-element.31.refs_7_) | copy-start | bytes 589828
  80.9 40.2 %collective-permute-start.4 = (bf16[3072,256]{1,0:T(8,128)(2,1)}, bf16[3072,256]{1,0:T(8,128)(2,1)}, u32[]{:S(2)}, u32[]{:S(2)}) collective-permute-start(bf16[3072,256]{1,0:T(8,128)(2,1)} %shard_map.115), channel_id=1, source_target_pairs={{0,16},{16,0},{32,48},{48,32},{1,17},{17,1},{33,49},{49,33},{2,18}... | collective-permute-start | bytes 4718600 | tf_op jit(solution)/shard_map/ppermute | solution.py:232
  89.5 11.5 %copy-start.21 = (s32[2,8]{1,0:T(2,128)S(1)}, s32[2,8]{1,0:T(2,128)}, u32[]{:S(2)}) copy-start(s32[2,8]{1,0:T(2,128)} %get-tuple-element.20) | copy-start | bytes 196
  89.5 11.5 %copy-start.9 = (bf16[192,512]{1,0:T(8,128)(2,1)S(1)}, bf16[192,512]{1,0:T(8,128)(2,1)}, u32[]{:S(2)}) copy-start(bf16[192,512]{1,0:T(8,128)(2,1)} %copy-done.8) | copy-start | bytes 589828
  89.5 11.5 %copy-start.11 = (bf16[192,512]{1,0:T(8,128)(2,1)S(1)}, bf16[192,512]{1,0:T(8,128)(2,1)}, u32[]{:S(2)}) copy-start(bf16[192,512]{1,0:T(8,128)(2,1)} %copy-done.10) | copy-start | bytes 589828
  91.0 26.9 %all-to-all-start.1 = ((bf16[64,13,2,128]{3,2,1,0:T(2,128)(2,1)}), bf16[64,13,2,128]{3,2,1,0:T(2,128)(2,1)}, u32[]{:S(2)}, u32[]{:S(2)}) async-start(bf16[64,13,2,128]{3,2,1,0:T(2,128)(2,1)} %copy.20), calls=%async_computation.1 | async-start | bytes 851968 | tf_op jit(solution)/shard_map/all_to_all | solution.py:22
  101.1 1.1 copy-start.1
  108.1 11.6 %copy-start.20 = (f32[8,2]{0,1:T(2,128)S(1)}, f32[8,2]{0,1:T(2,128)}, u32[]{:S(2)}) copy-start(f32[8,2]{0,1:T(2,128)} %param.10) | copy-start | bytes 196
  (5 other events, 4.8 us)

commit v8 on v7

--- a/solution.py
+++ b/solution.py
@@ -70,38 +70,45 @@
             send_ref[e, z] = block
 
 
-def project_kernel(guest_ref, own_ref, gate_ref, up_ref, down_ref, stack_ref, partial_ref):
-    width, hid = gate_ref.shape
+def project_kernel(guest_ref, own_ref, mine_hbm, stack_ref, partial_ref, mine_ref, mine_sem):
+    hid = stack_ref.shape[1]
+    width = stack_ref.shape[0] // 3
     half = own_ref.shape[0]
-    for h, rows_ref in enumerate((guest_ref, own_ref)):
-        rows = slice(h * half, (h + 1) * half)
-        x = rows_ref[:, :width]
-        parts = [
-            contract(x, gate_ref[...], 1, 0),
-            contract(x, stack_ref[:width, :], 1, 0),
-            contract(x, up_ref[...], 1, 0),
-            contract(x, stack_ref[width : 2 * width, :], 1, 0),
-            contract(rows_ref[:, width:], down_ref[...], 1, 1),
-        ]
-        total = None
-        for k in range(width // hid):
-            piece = contract(
-                rows_ref[:, width + k * hid : width + (k + 1) * hid],
-                stack_ref[2 * width + k * hid : 2 * width + (k + 1) * hid, :],
-                1,
-                1,
+    fetch = pltpu.make_async_copy(mine_hbm, mine_ref, mine_sem)
+    fetch.start()
+    for place, weights_ref in ((1, stack_ref), (0, mine_ref)):
+        if place == 0:
+            fetch.wait()
+        for h, rows_ref in enumerate((guest_ref, own_ref)):
+            rows = slice(h * half, (h + 1) * half)
+            x = rows_ref[:, :width]
+            total = None
+            for k in range(width // hid):
+                piece = contract(
+                    rows_ref[:, width + k * hid : width + (k + 1) * hid],
+                    weights_ref[2 * width + k * hid : 2 * width + (k + 1) * hid, :],
+                    1,
+                    1,
+                )
+                total = piece if total is None else total + piece
+            parts = (
+                contract(x, weights_ref[:width, :], 1, 0),
+                contract(x, weights_ref[width : 2 * width, :], 1, 0),
+                total,
             )
-            total = piece if total is None else total + piece
-        parts.append(total)
-        for k, part in enumerate(parts):
-            partial_ref[rows, k * hid : (k + 1) * hid] = part.astype(jnp.bfloat16)
+            for k, part in enumerate(parts):
+                low = (2 * k + place) * hid
+                partial_ref[rows, low : low + hid] = part.astype(jnp.bfloat16)
 
 
 def pullback_kernel(
-    partial_ref, other_ref, gate_ref, up_ref, stack_ref,
-    pack_ref, hidden_ref, gate_pre_ref, up_pre_ref, score_ref, *, first
+    partial_ref, other_ref, mine_hbm, stack_ref,
+    pack_ref, hidden_ref, gate_pre_ref, up_pre_ref, score_ref, mine_ref, mine_sem, *, first
 ):
-    width, hid = gate_ref.shape
+    hid = stack_ref.shape[1]
+    width = stack_ref.shape[0] // 3
+    fetch = pltpu.make_async_copy(mine_hbm.at[pl.ds(0, 2 * width), :], mine_ref, mine_sem)
+    fetch.start()
     both = 2 * hid
     half = hidden_ref.shape[0]
     step = 16
@@ -124,10 +131,11 @@
         return carry
 
     lax.fori_loop(0, half // step, one, 0)
+    fetch.wait()
     pack_ref[:half, :] = (
-        contract(gate_pre_ref[:, :hid], gate_ref[...], 1, 1)
+        contract(gate_pre_ref[:, :hid], mine_ref[:width, :], 1, 1)
         + contract(gate_pre_ref[:, hid:], stack_ref[:width, :], 1, 1)
-        + contract(up_pre_ref[:, :hid], up_ref[...], 1, 1)
+        + contract(up_pre_ref[:, :hid], mine_ref[width:, :], 1, 1)
         + contract(up_pre_ref[:, hid:], stack_ref[width : 2 * width, :], 1, 1)
     ).astype(jnp.bfloat16)
     extra = pack_ref.shape[0] - half
@@ -237,7 +245,8 @@
     def stacked(gate, up, down):
         return jnp.concatenate([gate, up] + jnp.split(down, width // hid, axis=1), axis=0)
 
-    weights = meet(stacked(gate_w, up_w, down_w), 1)
+    own_weights = stacked(gate_w, up_w, down_w)
+    weights = meet(own_weights, 1)
     own = exchange(send, ("expert", "z")).reshape(part_rows, 2 * width)
     guest = meet(own, 3)
     own, guest = lax.optimization_barrier((own, guest))
@@ -264,8 +273,10 @@
     (partial,) = call(
         project_kernel,
         [((all_rows, 3 * both), bf16)],
-        (guest, own, gate_w, up_w, down_w, weights),
+        (guest, own, own_weights, weights),
+        [pltpu.VMEM((3 * width, hid), bf16), pltpu.SemaphoreType.DMA],
         flops=3 * dot_flops,
+        far=(2,),
     )
     pack_rows = part_rows + 16
     other = swap(partial)
@@ -274,9 +285,14 @@
         return call(
             functools.partial(pullback_kernel, first=first),
             [((pack_rows, width), bf16)] + [((part_rows, both), bf16)] * 3,
-            (partial, other, gate_w, up_w, weights),
-            [pltpu.VMEM((part_rows, LANES), jnp.float32)],
+            (partial, other, own_weights, weights),
+            [
+                pltpu.VMEM((part_rows, LANES), jnp.float32),
+                pltpu.VMEM((2 * width, hid), bf16),
+                pltpu.SemaphoreType.DMA,
+            ],
             flops=dot_flops,
+            far=(2,),
         )
 
     pack_guest, *terms_guest = pulled(0)

time: 126 us -> 127 us (level)
  the two profiles are of different devices: /device:TPU:6 before, /device:TPU:16 now
where the time goes in v8:
time: 127 us
  waiting for transfers between devices  55.4 us (44%)
  starting transfers between devices  41.7 us (33%)
  Pallas kernels  13.9 us (11%)
  local copies, waits for them, and re-layouts  12.6 us (10%)
    all_to_all x2, waiting for transfers between devices, exchange(): return lax.all_to_all(block, axes, split_axis=0, concat_axis=0, tiled=True)  30.8 us
    all_to_all x2, starting transfers between devices, exchange(): return lax.all_to_all(block, axes, split_axis=0, concat_axis=0, tiled=True)  25 us
    ppermute x4, waiting for transfers between devices, meet(): return lax.ppermute(block, 'x', [(i, i ^ mask) for i in range(nx)])  21.8 us
    ppermute x4, starting transfers between devices, meet(): return lax.ppermute(block, 'x', [(i, i ^ mask) for i in range(nx)])  14.8 us
    pallas_call x6, Pallas kernels, call(): pl.pallas_call(kernel, out_shape=tuple((jax.ShapeDtypeStruct(s, d) for s,...  11.7 us
    unnamed x41, local copies, waits for them, and re-layouts  7.57 us
    ppermute x1, waiting for transfers between devices, swap(): return lax.ppermute(block, 'dp', [(0, 1), (1, 0)])  2.81 us
  transfers between devices with their start and end apart: 7, of which 6 were waited for; matrix products, arithmetic and copies ran while one was open for 6% of the time, Pallas kernels for 4%

profile of v8, /device:TPU:16, one launch (start us, length us, event | category | flops | bytes accessed | tf_op | source)
XLA Modules:
  0.0 126.7 jit_solution(4220337245413527381)
XLA Ops:
  0.7 2.2 %shard_map.110 = (bf16[8,8,48,128]{3,2,1,0:T(8,128)(2,1)}, s32[2,8]{1,0:T(2,128)}) custom-call(s32[2,8]{1,0:T(2,128)} %bitcast.30, f32[2,8]{1,0:T(2,128)} %bitcast.27, bf16[8,1024]{1,0:T(8,128)(2,1)} %tokens_ref.1, bf16[8,1024]{1,0:T(8,128)(2,1)} %out_grad_ref.1), custom_call_target="tpu_custom_call" | custom-call | tf_op jit(solution)/shard_map/pallas_call | solution.py:215
  2.9 16.8 %all-to-all-start = ((bf16[64,48,128]{2,1,0:T(8,128)(2,1)}), bf16[64,48,128]{2,1,0:T(8,128)(2,1)}, u32[]{:S(2)}, u32[]{:S(2)}) async-start(bf16[64,48,128]{2,1,0:T(8,128)(2,1)} %bitcast.22), calls=%async_computation | async-start | bytes 1572864 | tf_op jit(solution)/shard_map/all_to_all | solution.py:22
  19.9 3.4 %collective-permute-start.1 = (bf16[3072,256]{1,0:T(8,128)(2,1)S(1)}, bf16[3072,256]{1,0:T(8,128)(2,1)S(1)}, u32[]{:S(2)}, u32[]{:S(2)}) collective-permute-start(bf16[3072,256]{1,0:T(8,128)(2,1)S(1)} %slice_dynamic-update-slice_fusion.mine_hbm), channel_id=1, source_target_pairs={{0,16},{16,0},{32,48},{48,32},{1,17},{17,1},{33,49},{49,33},{2,18}... | collective-permute-start | bytes 4718600 | tf_op jit(solution)/shard_map/ppermute | solution.py:240
  23.3 21.2 %all-to-all-done = bf16[64,48,128]{2,1,0:T(8,128)(2,1)} async-done(((bf16[64,48,128]{2,1,0:T(8,128)(2,1)}), bf16[64,48,128]{2,1,0:T(8,128)(2,1)}, u32[]{:S(2)}, u32[]{:S(2)}) %all-to-all-start) | async-done | bytes 786464 | tf_op jit(solution)/shard_map/all_to_all | solution.py:22
  44.4 2.2 %reshape.30.own_ref.refs_4_ = bf16[192,2048]{1,0:T(8,128)(2,1)} reshape(bf16[64,48,128]{2,1,0:T(8,128)(2,1)} %all-to-all-done) | data formatting | bytes 1572864 | tf_op jit(solution)/shard_map/reshape | solution.py:250
  46.6 4.7 %collective-permute-start = (bf16[192,2048]{1,0:T(8,128)(2,1)}, bf16[192,2048]{1,0:T(8,128)(2,1)S(1)}, u32[]{:S(2)}, u32[]{:S(2)}) collective-permute-start(bf16[192,2048]{1,0:T(8,128)(2,1)} %reshape.30.own_ref.refs_4_), channel_id=1, source_target_pairs={{0,48},{16,32},{32,16},{48,0},{1,49},{17,33},{33,17},{49,1},{2,50}... | collective-permute-start | bytes 2359304 | tf_op jit(solution)/shard_map/ppermute | solution.py:240
  51.3 15.2 %collective-permute-done.guest_ref.refs_0_ = bf16[192,2048]{1,0:T(8,128)(2,1)S(1)} collective-permute-done((bf16[192,2048]{1,0:T(8,128)(2,1)}, bf16[192,2048]{1,0:T(8,128)(2,1)S(1)}, u32[]{:S(2)}, u32[]{:S(2)}) %collective-permute-start) | collective-permute-done | bytes 786464 | tf_op jit(solution)/shard_map/ppermute | solution.py:240
  66.5 1.4 %copy-done = bf16[192,2048]{1,0:T(8,128)(2,1)S(1)} copy-done((bf16[192,2048]{1,0:T(8,128)(2,1)S(1)}, bf16[192,2048]{1,0:T(8,128)(2,1)}, u32[]{:S(2)}) %copy-start) | copy-done | bytes 786456
  67.9 1.9 %shard_map.111.partial_ref = bf16[384,1536]{1,0:T(8,128)(2,1)S(1)} custom-call(bf16[192,2048]{1,0:T(8,128)(2,1)S(1)} %collective-permute-done.guest_ref.refs_0_, bf16[192,2048]{1,0:T(8,128)(2,1)S(1)} %copy-done, bf16[3072,256]{1,0:T(8,128)(2,1)S(1)} %slice_dynamic-update-slice_fusion.mine_hbm, bf16[3072,256]{1,0:T(8,128)(2,1)S(1)} %collective-permute-done.1.stack_ref), custom_call_target="tpu_custom_call" | custom-call | flops 1207959552 | bytes 6291456 | tf_op jit(solution)/shard_map/pallas_call | solution.py:260
  69.8 1.9 %collective-permute-start.2 = (bf16[384,1536]{1,0:T(8,128)(2,1)S(1)}, bf16[384,1536]{1,0:T(8,128)(2,1)S(1)}, u32[]{:S(2)}, u32[]{:S(2)}) collective-permute-start(bf16[384,1536]{1,0:T(8,128)(2,1)S(1)} %shard_map.111.partial_ref), channel_id=1, source_target_pairs={{0,1},{1,0},{2,3},{3,2},{4,5},{5,4},{6,7},{7,6},{8,9},{9,8},{10,11... | collective-permute-start | bytes 3538952 | tf_op jit(solution)/shard_map/ppermute | solution.py:243
  71.7 2.8 %collective-permute-done.2.other_ref = bf16[384,1536]{1,0:T(8,128)(2,1)S(1)} collective-permute-done((bf16[384,1536]{1,0:T(8,128)(2,1)S(1)}, bf16[384,1536]{1,0:T(8,128)(2,1)S(1)}, u32[]{:S(2)}, u32[]{:S(2)}) %collective-permute-start.2) | collective-permute-done | bytes 1179680 | tf_op jit(solution)/shard_map/ppermute | solution.py:243
  74.5 2.1 %shard_map.113 = (bf16[208,1024]{1,0:T(8,128)(2,1)S(1)}, bf16[192,512]{1,0:T(8,128)(2,1)S(1)}, bf16[192,512]{1,0:T(8,128)(2,1)S(1)}, bf16[192,512]{1,0:T(8,128)(2,1)S(1)}) custom-call(bf16[384,1536]{1,0:T(8,128)(2,1)S(1)} %shard_map.111.partial_ref, bf16[384,1536]{1,0:T(8,128)(2,1)S(1)} %collective-permute-done.2.other_ref, ...), custom_call_target="tpu_custom_call" | custom-call | flops 402653184 | bytes 6291456 | tf_op jit(solution)/shard_map/pallas_call | solution.py:260
  76.7 4.8 %collective-permute-start.3 = (bf16[208,1024]{1,0:T(8,128)(2,1)S(1)}, bf16[208,1024]{1,0:T(8,128)(2,1)S(1)}, u32[]{:S(2)}, u32[]{:S(2)}) collective-permute-start(bf16[208,1024]{1,0:T(8,128)(2,1)S(1)} %get-tuple-element.25), channel_id=1, source_target_pairs={{0,48},{16,32},{32,16},{48,0},{1,49},{17,33},{33,17},{49,1},{2,50}... | collective-permute-start | bytes 1277960 | tf_op jit(solution)/shard_map/ppermute | solution.py:240
  81.5 2.2 %shard_map.112 = (bf16[208,1024]{1,0:T(8,128)(2,1)S(1)}, bf16[192,512]{1,0:T(8,128)(2,1)S(1)}, bf16[192,512]{1,0:T(8,128)(2,1)S(1)}, bf16[192,512]{1,0:T(8,128)(2,1)S(1)}) custom-call(bf16[384,1536]{1,0:T(8,128)(2,1)S(1)} %shard_map.111.partial_ref, bf16[384,1536]{1,0:T(8,128)(2,1)S(1)} %collective-permute-done.2.other_ref, ...), custom_call_target="tpu_custom_call" | custom-call | flops 402653184 | bytes 6291456 | tf_op jit(solution)/shard_map/pallas_call | solution.py:260
  83.7 2.2 %shard_map.115 = bf16[3072,256]{1,0:T(8,128)(2,1)} custom-call(bf16[192,2048]{1,0:T(8,128)(2,1)S(1)} %collective-permute-done.guest_ref.refs_0_, bf16[192,512]{1,0:T(8,128)(2,1)S(1)} %get-tuple-element.26.refs_1_, bf16[192,512]{1,0:T(8,128)(2,1)S(1)} %get-tuple-element.27.refs_2_, bf16[192,512]{1,0:T(8,128)(2,1)S(1)} %get-tuple-element.28.refs_3_, ...), custom_call_target="tpu_custom_call" | custom-call | flops 603979776 | bytes 6291456 | tf_op jit(solution)/shard_map/pallas_call | solution.py:260
  86.0 1.9 %collective-permute-start.4 = (bf16[3072,256]{1,0:T(8,128)(2,1)}, bf16[3072,256]{1,0:T(8,128)(2,1)}, u32[]{:S(2)}, u32[]{:S(2)}) collective-permute-start(bf16[3072,256]{1,0:T(8,128)(2,1)} %shard_map.115), channel_id=1, source_target_pairs={{0,16},{16,0},{32,48},{48,32},{1,17},{17,1},{33,49},{49,33},{2,18}... | collective-permute-start | bytes 4718600 | tf_op jit(solution)/shard_map/ppermute | solution.py:240
  87.9 3.9 %collective-permute-done.3 = bf16[208,1024]{1,0:T(8,128)(2,1)S(1)} collective-permute-done((bf16[208,1024]{1,0:T(8,128)(2,1)S(1)}, bf16[208,1024]{1,0:T(8,128)(2,1)S(1)}, u32[]{:S(2)}, u32[]{:S(2)}) %collective-permute-start.3) | collective-permute-done | bytes 426016 | tf_op jit(solution)/shard_map/ppermute | solution.py:240
  92.5 1.2 copy.20
  93.7 8.2 %all-to-all-start.1 = ((bf16[64,13,2,128]{3,2,1,0:T(2,128)(2,1)}), bf16[64,13,2,128]{3,2,1,0:T(2,128)(2,1)}, u32[]{:S(2)}, u32[]{:S(2)}) async-start(bf16[64,13,2,128]{3,2,1,0:T(2,128)(2,1)} %copy.20), calls=%async_computation.1 | async-start | bytes 851968 | tf_op jit(solution)/shard_map/all_to_all | solution.py:22
  101.9 1.1 copy-done.2
  103.1 1.1 copy-done.4
  109.0 9.7 %all-to-all-done.1 = bf16[64,13,2,128]{3,2,1,0:T(2,128)(2,1)} async-done(((bf16[64,13,2,128]{3,2,1,0:T(2,128)(2,1)}), bf16[64,13,2,128]{3,2,1,0:T(2,128)(2,1)}, u32[]{:S(2)}, u32[]{:S(2)}) %all-to-all-start.1) | async-done | bytes 426016 | tf_op jit(solution)/shard_map/all_to_all | solution.py:22
  121.7 2.6 %collective-permute-done.4.theirs_hbm = bf16[3072,256]{1,0:T(8,128)(2,1)} collective-permute-done((bf16[3072,256]{1,0:T(8,128)(2,1)}, bf16[3072,256]{1,0:T(8,128)(2,1)}, u32[]{:S(2)}, u32[]{:S(2)}) %collective-permute-start.4) | collective-permute-done | bytes 1572896 | tf_op jit(solution)/shard_map/ppermute | solution.py:240
  124.3 2.3 %shard_map.116 = (bf16[1,1024,256]{2,1,0:T(8,128)(2,1)}, bf16[1,1024,256]{2,1,0:T(8,128)(2,1)}, bf16[1,256,1024]{2,1,0:T(8,128)(2,1)}) custom-call(f32[3072,256]{1,0:T(8,128)S(1)} %shard_map.114.mine_ref, bf16[3072,256]{1,0:T(8,128)(2,1)} %collective-permute-done.4.theirs_hbm), custom_call_target="tpu_custom_call" | custom-call | bytes 6291456 | tf_op jit(solution)/shard_map/pallas_call | solution.py:260
  (59 shorter events, 8.6 us)
Async XLA Ops:
  0.6 19.0 %copy-start.13 = (bf16[1,1024,256]{2,1,0:T(8,128)(2,1)S(1)}, bf16[1,1024,256]{2,1,0:T(8,128)(2,1)}, u32[]{:S(2)}) copy-start(bf16[1,1024,256]{2,1,0:T(8,128)(2,1)} %param.11) | copy-start | bytes 1572868
  0.6 19.1 %copy-start.14 = (bf16[1,1024,256]{2,1,0:T(8,128)(2,1)S(1)}, bf16[1,1024,256]{2,1,0:T(8,128)(2,1)}, u32[]{:S(2)}) copy-start(bf16[1,1024,256]{2,1,0:T(8,128)(2,1)} %param.12) | copy-start | bytes 1572868
  2.9 16.9 %copy-start.15 = (bf16[1,256,1024]{2,1,0:T(8,128)(2,1)S(1)}, bf16[1,256,1024]{2,1,0:T(8,128)(2,1)}, u32[]{:S(2)}) copy-start(bf16[1,256,1024]{2,1,0:T(8,128)(2,1)} %param.13) | copy-start | bytes 1572868
  2.9 41.6 %all-to-all-start = ((bf16[64,48,128]{2,1,0:T(8,128)(2,1)}), bf16[64,48,128]{2,1,0:T(8,128)(2,1)}, u32[]{:S(2)}, u32[]{:S(2)}) async-start(bf16[64,48,128]{2,1,0:T(8,128)(2,1)} %bitcast.22), calls=%async_computation | async-start | bytes 1572864 | tf_op jit(solution)/shard_map/all_to_all | solution.py:22
  19.9 46.6 %collective-permute-start.1 = (bf16[3072,256]{1,0:T(8,128)(2,1)S(1)}, bf16[3072,256]{1,0:T(8,128)(2,1)S(1)}, u32[]{:S(2)}, u32[]{:S(2)}) collective-permute-start(bf16[3072,256]{1,0:T(8,128)(2,1)S(1)} %slice_dynamic-update-slice_fusion.mine_hbm), channel_id=1, source_target_pairs={{0,16},{16,0},{32,48},{48,32},{1,17},{17,1},{33,49},{49,33},{2,18}... | collective-permute-start | bytes 4718600 | tf_op jit(solution)/shard_map/ppermute | solution.py:240
  46.6 19.9 %collective-permute-start = (bf16[192,2048]{1,0:T(8,128)(2,1)}, bf16[192,2048]{1,0:T(8,128)(2,1)S(1)}, u32[]{:S(2)}, u32[]{:S(2)}) collective-permute-start(bf16[192,2048]{1,0:T(8,128)(2,1)} %reshape.30.own_ref.refs_4_), channel_id=1, source_target_pairs={{0,48},{16,32},{32,16},{48,0},{1,49},{17,33},{33,17},{49,1},{2,50}... | collective-permute-start | bytes 2359304 | tf_op jit(solution)/shard_map/ppermute | solution.py:240
  66.5 17.2 %copy-start.3 = (bf16[192,2048]{1,0:T(8,128)(2,1)}, bf16[192,2048]{1,0:T(8,128)(2,1)S(1)}, u32[]{:S(2)}) copy-start(bf16[192,2048]{1,0:T(8,128)(2,1)S(1)} %collective-permute-done.guest_ref.refs_0_) | copy-start | bytes 2359300
  66.5 1.4 %copy-start = (bf16[192,2048]{1,0:T(8,128)(2,1)S(1)}, bf16[192,2048]{1,0:T(8,128)(2,1)}, u32[]{:S(2)}) copy-start(bf16[192,2048]{1,0:T(8,128)(2,1)} %reshape.30.own_ref.refs_4_) | copy-start | bytes 2359300
  69.8 4.7 %collective-permute-start.2 = (bf16[384,1536]{1,0:T(8,128)(2,1)S(1)}, bf16[384,1536]{1,0:T(8,128)(2,1)S(1)}, u32[]{:S(2)}, u32[]{:S(2)}) collective-permute-start(bf16[384,1536]{1,0:T(8,128)(2,1)S(1)} %shard_map.111.partial_ref), channel_id=1, source_target_pairs={{0,1},{1,0},{2,3},{3,2},{4,5},{5,4},{6,7},{7,6},{8,9},{9,8},{10,11... | collective-permute-start | bytes 3538952 | tf_op jit(solution)/shard_map/ppermute | solution.py:243
  76.7 7.0 %copy-start.5 = (bf16[192,512]{1,0:T(8,128)(2,1)}, bf16[192,512]{1,0:T(8,128)(2,1)S(1)}, u32[]{:S(2)}) copy-start(bf16[192,512]{1,0:T(8,128)(2,1)S(1)} %get-tuple-element.28.refs_3_) | copy-start | bytes 589828
  76.7 7.0 %copy-start.1 = (bf16[192,2048]{1,0:T(8,128)(2,1)S(1)}, bf16[192,2048]{1,0:T(8,128)(2,1)}, u32[]{:S(2)}) copy-start(bf16[192,2048]{1,0:T(8,128)(2,1)} %reshape.30.own_ref.refs_4_) | copy-start | bytes 2359300
  76.7 15.1 %collective-permute-start.3 = (bf16[208,1024]{1,0:T(8,128)(2,1)S(1)}, bf16[208,1024]{1,0:T(8,128)(2,1)S(1)}, u32[]{:S(2)}, u32[]{:S(2)}) collective-permute-start(bf16[208,1024]{1,0:T(8,128)(2,1)S(1)} %get-tuple-element.25), channel_id=1, source_target_pairs={{0,48},{16,32},{32,16},{48,0},{1,49},{17,33},{33,17},{49,1},{2,50}... | collective-permute-start | bytes 1277960 | tf_op jit(solution)/shard_map/ppermute | solution.py:240
  83.7 2.3 %copy-start.7 = (bf16[192,512]{1,0:T(8,128)(2,1)}, bf16[192,512]{1,0:T(8,128)(2,1)S(1)}, u32[]{:S(2)}) copy-start(bf16[192,512]{1,0:T(8,128)(2,1)S(1)} %get-tuple-element.29.refs_5_) | copy-start | bytes 589828
  83.7 2.3 %copy-start.9 = (bf16[192,512]{1,0:T(8,128)(2,1)}, bf16[192,512]{1,0:T(8,128)(2,1)S(1)}, u32[]{:S(2)}) copy-start(bf16[192,512]{1,0:T(8,128)(2,1)S(1)} %get-tuple-element.30.refs_6_) | copy-start | bytes 589828
  83.7 2.3 %copy-start.11 = (bf16[192,512]{1,0:T(8,128)(2,1)}, bf16[192,512]{1,0:T(8,128)(2,1)S(1)}, u32[]{:S(2)}) copy-start(bf16[192,512]{1,0:T(8,128)(2,1)S(1)} %get-tuple-element.31.refs_7_) | copy-start | bytes 589828
  86.0 38.4 %collective-permute-start.4 = (bf16[3072,256]{1,0:T(8,128)(2,1)}, bf16[3072,256]{1,0:T(8,128)(2,1)}, u32[]{:S(2)}, u32[]{:S(2)}) collective-permute-start(bf16[3072,256]{1,0:T(8,128)(2,1)} %shard_map.115), channel_id=1, source_target_pairs={{0,16},{16,0},{32,48},{48,32},{1,17},{17,1},{33,49},{49,33},{2,18}... | collective-permute-start | bytes 4718600 | tf_op jit(solution)/shard_map/ppermute | solution.py:240
  92.2 9.7 %copy-start.17 = (s32[2,8]{1,0:T(2,128)S(1)}, s32[2,8]{1,0:T(2,128)}, u32[]{:S(2)}) copy-start(s32[2,8]{1,0:T(2,128)} %get-tuple-element.20) | copy-start | bytes 196
  93.7 24.9 %all-to-all-start.1 = ((bf16[64,13,2,128]{3,2,1,0:T(2,128)(2,1)}), bf16[64,13,2,128]{3,2,1,0:T(2,128)(2,1)}, u32[]{:S(2)}, u32[]{:S(2)}) async-start(bf16[64,13,2,128]{3,2,1,0:T(2,128)(2,1)} %copy.20), calls=%async_computation.1 | async-start | bytes 851968 | tf_op jit(solution)/shard_map/all_to_all | solution.py:22
  101.9 1.1 copy-start.2
  103.1 1.1 copy-start.4
  104.2 0.9 copy-start.6
  105.1 0.9 copy-start.8
  106.0 0.9 copy-start.10
  108.9 11.4 %copy-start.16 = (f32[8,2]{0,1:T(2,128)S(1)}, f32[8,2]{0,1:T(2,128)}, u32[]{:S(2)}) copy-start(f32[8,2]{0,1:T(2,128)} %param.10) | copy-start | bytes 196
  (1 other events, 0.9 us)
